TPU v7x, 32 devices: a whole 2x2x4 slice. The times are simulated.
32 devices in a mesh: groups: 2 (over y), node: 4 (over z), tensor: 4 (over x, core).
Axes of the slice: x: 2, y: 2, z: 4, core: 2. Of those that a mesh axis runs over, the one named last changes fastest.
Arguments:
- queries: bfloat16 [6144, 5120], P(('groups', 'node'), 'tensor'), parts along dimension 0, may hold values from -90 to 90
- keys: bfloat16 [6144, 1024], P(('groups', 'node'), 'tensor'), parts along dimension 0, may hold values from -4.1 to 4.1
- values: bfloat16 [6144, 1024], P(('groups', 'node'), 'tensor'), parts along dimension 0, may hold values from -4 to 4
- out_weight: bfloat16 [5120, 5120], P('node', 'tensor'), may hold values from -0.59765625 to 0.59765625
- slot_nodes: int32 [48], P('groups'), parts along dimension 0, may hold values from 0 to 23, as said below
- ancestors: int32 [48, 7], P('groups'), parts along dimension 0, may hold values from -1 to 23, as said below
- depth: int32 [48], P('groups'), parts along dimension 0, may hold values from 0 to 7, as said below
Outputs:
- projected: bfloat16 [6144, 5120], P(('groups', 'node', 'tensor')), parts along dimension 0
There are 2 independent parts, one for each index of `groups`. A program takes and returns all parts, laid end to end along the dimension named above; an argument that names none is the same for every part. Nothing has to cross between parts.
Inputs may be any that keep to these rules, and one draw needn't show every extreme that they name: `slot_nodes`: every node is held in exactly one slot. `ancestors`: every device holds one subtree: a node whose parent, if any, lies on another device, and its 5 children. When a node's parent lies on another device, that parent is one of the children of its device's subtree, and all nodes of other devices below a device hang below the same one of its children. Above any device lie at most 3 other devices. depth counts the entries of a row of ancestors that are not -1.
All inputs are finite; a program needn't handle non-finite values.
Results may differ from a plain program's by a relative error of at most 0.009.
Values may be sent and summed in bfloat16 or wider, within the bound.
No kernel may reach another device: no remote copies, remote signals or barrier semaphores. Data moves between devices by JAX's collectives and lax.ppermute only.
A program may use at most 128 MiB of HBM per device.

v0:
```python
import functools
import math

import jax
import jax.numpy as jnp
from jax import lax
from jax.experimental import pallas as pl
from jax.experimental.pallas import tpu as pltpu
from jax.sharding import PartitionSpec as P

HEAD = 128
NODE_TOK = 128
A_MAX = 7
CHAIN = A_MAX - 1
EXPORTS = 2
SCALE = math.log2(math.e) / math.sqrt(HEAD)
DEAD = -1e30
LIGHT = pl.CostEstimate(flops=1, bytes_accessed=1, transcendentals=0)
VMEM_LIMIT = 20 * 1024 * 1024
ATTEND_LIMIT = 24 * 1024 * 1024


def prepare_body(nodes, *refs):
    slot_hbm, ancestors_hbm, depth_hbm, keys, values, exported, table_hbm = refs[:7]
    slot_nodes, ancestors, depth, table, holder, within, roots, sem = refs[7:]
    devices = slot_nodes.shape[0] // nodes
    me = lax.axis_index("node")
    fetches = [
        pltpu.make_async_copy(source, target, sem.at[2 * EXPORTS + 1 + order])
        for order, (source, target) in enumerate(
            ((slot_hbm, slot_nodes), (ancestors_hbm, ancestors), (depth_hbm, depth))
        )
    ]
    for fetch in fetches:
        fetch.start()
    for fetch in fetches:
        fetch.wait()

    def place(device, mine):
        root, root_index = jnp.int32(0), jnp.int32(0)
        for index in range(nodes):
            node = slot_nodes[device * nodes + index]
            holder[node] = device
            within[node] = index
            even = (depth[node] & 1) == 0
            root = jnp.where(even, node, root)
            root_index = jnp.where(even, index, root_index)
        roots[device] = root
        return jnp.where(device == me, root_index, mine)

    root = lax.fori_loop(0, devices, place, jnp.int32(0))

    def find_attach(device, attach):
        node = roots[device]
        level = depth[node]
        for step in range(0, CHAIN, 2):
            above = jnp.maximum(ancestors[step, node], 0)
            hit = (step < level) & (holder[above] == me)
            attach = jnp.where(hit, within[above], attach)
        return attach

    attach = lax.fori_loop(0, devices, find_attach, jnp.int32(0))
    copies = []
    for position, (source, index) in enumerate(
        ((keys, root), (keys, attach), (values, root), (values, attach))
    ):
        rows = pl.ds(pl.multiple_of(index * NODE_TOK, NODE_TOK), NODE_TOK)
        copies.append(
            pltpu.make_async_copy(source.at[rows, :], exported.at[position], sem.at[position])
        )
    for copy in copies:
        copy.start()
    root_node = roots[me]
    count = depth[root_node]
    table[0] = root
    table[1] = count
    for step in range(CHAIN):
        above = jnp.maximum(ancestors[step, root_node], 0)
        entry = holder[above] * (2 * EXPORTS) + (1 if step % 2 == 0 else 0)
        table[2 + step] = jnp.where(step < count, entry, 0)
    store = pltpu.make_async_copy(table, table_hbm, sem.at[2 * EXPORTS])
    store.start()
    for copy in (*copies, store):
        copy.wait()


def prepare(slot_nodes, ancestors, depth, keys, values):
    nodes = keys.shape[0] // NODE_TOK
    slots = slot_nodes.shape[0]
    hbm = pl.BlockSpec(memory_space=pltpu.HBM)
    vmem = pl.BlockSpec(memory_space=pltpu.VMEM)
    return pl.pallas_call(
        functools.partial(prepare_body, nodes),
        out_shape=(
            jax.ShapeDtypeStruct((2 * EXPORTS, NODE_TOK, keys.shape[1]), keys.dtype),
            jax.ShapeDtypeStruct((2 + CHAIN,), jnp.int32),
        ),
        in_specs=[hbm, hbm, hbm, vmem, vmem],
        out_specs=(hbm, hbm),
        scratch_shapes=[
            pltpu.SMEM((slots,), jnp.int32),
            pltpu.SMEM((A_MAX, slots), jnp.int32),
            pltpu.SMEM((slots,), jnp.int32),
            pltpu.SMEM((2 + CHAIN,), jnp.int32),
            pltpu.SMEM((slots,), jnp.int32),
            pltpu.SMEM((slots,), jnp.int32),
            pltpu.SMEM((slots // nodes,), jnp.int32),
            pltpu.SemaphoreType.DMA((2 * EXPORTS + 4,)),
        ],
        compiler_params=pltpu.CompilerParams(vmem_limit_bytes=VMEM_LIMIT),
        name="prepare",
    )(slot_nodes, ancestors.T, depth, keys, values)


def attend_body(kv, parts, table, query_hbm, keys_hbm, values_hbm, got, *refs):
    out, query, keys, values, above_keys, above_values, all_keys, all_values, sem = refs[-9:]
    nodes = query.shape[0] // NODE_TOK
    group = query.shape[1] // HEAD
    per_part = query.shape[0] // parts
    side = all_keys.shape[0]
    lanes = pl.ds(kv * HEAD, HEAD)
    pairs = [(keys_hbm.at[:, lanes], keys), (values_hbm.at[:, lanes], values)]
    for step in range(CHAIN):
        entry = table[2 + step]
        pairs.append((got.at[entry, :, lanes], above_keys.at[step]))
        pairs.append((got.at[entry + EXPORTS, :, lanes], above_values.at[step]))
    pairs.append((query_hbm.at[:, pl.ds(kv * group * HEAD, group * HEAD)], query))
    copies = [
        pltpu.make_async_copy(source, target, sem.at[order])
        for order, (source, target) in enumerate(pairs)
    ]
    for copy in copies:
        copy.start()
    ones = jnp.ones((NODE_TOK, HEAD), all_values.dtype)
    nothing = jnp.zeros((NODE_TOK, 2 * HEAD), all_values.dtype)
    query_index = lax.broadcasted_iota(jnp.int32, (NODE_TOK, NODE_TOK), 0)
    key_index = lax.broadcasted_iota(jnp.int32, (NODE_TOK, NODE_TOK), 1)
    own_bias = jnp.where(key_index <= query_index, 0.0, DEAD)
    piece = math.gcd(NODE_TOK, per_part)
    pieces_part = per_part // piece
    me = lax.axis_index("tensor")
    above = (CHAIN + 1) * NODE_TOK
    for copy in copies:
        copy.wait()

    def node_rows(node):
        return pl.ds(pl.multiple_of(node * NODE_TOK, NODE_TOK), NODE_TOK)

    def put(place, order, key_block, value_block):
        rows = pl.ds(order * NODE_TOK, NODE_TOK)
        all_keys[place, rows, :] = key_block
        all_values[place, rows, :HEAD] = value_block
        all_values[place, rows, HEAD:] = ones

    def put_nothing(place, order, first_key):
        rows = pl.ds(order * NODE_TOK, NODE_TOK)
        all_keys[place, rows, :] = jnp.broadcast_to(first_key, (NODE_TOK, HEAD))
        all_values[place, rows, :] = nothing

    for place in range(side):
        for step in range(CHAIN):
            put(place, step, above_keys[step], above_values[step])

    def lay_out(place, node):
        own_key = keys[node_rows(node), :]
        put(place, CHAIN + 1, own_key, values[node_rows(node), :])
        for step in range(CHAIN):
            pl.when(step >= table[1])(functools.partial(put_nothing, place, step, own_key[:1]))
        is_root = node == table[0]
        pl.when(is_root)(functools.partial(put_nothing, place, CHAIN, own_key[:1]))

        @pl.when(jnp.logical_not(is_root))
        def _():
            put(place, CHAIN, keys[node_rows(table[0]), :], values[node_rows(table[0]), :])

    def score(place, node):
        stacked = jnp.concatenate(
            [query[node_rows(node), h * HEAD : (h + 1) * HEAD] for h in range(group)], 0
        )
        return times(stacked, all_keys[place])

    def weigh(scores):
        own = scores[:, above:] + jnp.concatenate([own_bias] * group, 0)
        masked = jnp.concatenate([scores[:, :above], own], 1)
        largest = jnp.max(masked, axis=1, keepdims=True)
        return jnp.exp2((masked - largest) * SCALE).astype(jnp.bfloat16)

    def finish(place, node, expo):
        mixed = jnp.dot(expo, all_values[place], preferred_element_type=jnp.float32)
        result = (mixed[:, :HEAD] / mixed[:, HEAD:]).astype(jnp.bfloat16)
        for part in range(NODE_TOK // piece):
            block = node * (NODE_TOK // piece) + part
            owner = block // pieces_part
            target = slot_position(parts, owner ^ me)
            inner = (block - owner * pieces_part) * piece
            to = pl.ds(pl.multiple_of(inner, piece), piece)
            for h in range(group):
                first = h * NODE_TOK + part * piece
                out[target, to, h * HEAD : (h + 1) * HEAD] = result[first : first + piece]

    def some_nodes(turn, carry):
        mine = [(place, turn * side + place) for place in range(side)]
        for place, node in mine:
            lay_out(place, node)
        scores = [score(place, node) for place, node in mine]
        for (place, node), each in zip(mine, scores):
            finish(place, node, weigh(each))
        return carry

    lax.fori_loop(0, nodes // side, some_nodes, 0)


def slot_position(parts, distance):
    half = parts // 2
    return jnp.where(distance % 2 == 1, distance // 2, half + distance // 2)


def in_hbm(array):
    return pltpu.with_memory_space_constraint(array, pltpu.HBM)


def attend(kv, table, queries, keys, values, got, parts, after):
    rows = queries.shape[0]
    width = queries.shape[1] // (keys.shape[1] // HEAD)
    total = (CHAIN + 2) * NODE_TOK
    side = 2 if rows % (2 * NODE_TOK) == 0 else 1
    hbm = pl.BlockSpec(memory_space=pltpu.HBM)
    return pl.pallas_call(
        functools.partial(attend_body, kv, parts),
        out_shape=jax.ShapeDtypeStruct((parts, rows // parts, width), queries.dtype),
        in_specs=[pl.BlockSpec(memory_space=pltpu.SMEM)]
        + [hbm] * 4
        + [pl.BlockSpec(memory_space=pl.ANY)] * len(after),
        scratch_shapes=[
            pltpu.VMEM((rows, width), queries.dtype),
            pltpu.VMEM((rows, HEAD), keys.dtype),
            pltpu.VMEM((rows, HEAD), keys.dtype),
            pltpu.VMEM((CHAIN, NODE_TOK, HEAD), keys.dtype),
            pltpu.VMEM((CHAIN, NODE_TOK, HEAD), keys.dtype),
            pltpu.VMEM((side, total, HEAD), keys.dtype),
            pltpu.VMEM((side, total, 2 * HEAD), keys.dtype),
            pltpu.SemaphoreType.DMA((3 + 2 * CHAIN,)),
        ],
        compiler_params=pltpu.CompilerParams(vmem_limit_bytes=ATTEND_LIMIT),
        cost_estimate=LIGHT,
        name="attend",
    )(table, *[in_hbm(x) for x in (queries, keys, values, got)], *after)


def swap(array, axis, distance):
    size = lax.axis_size(axis)
    return lax.ppermute(array, axis, [(i, i ^ distance) for i in range(size)])


def times(rows, weight):
    return lax.dot_general(
        rows, weight, (((1,), (1,)), ((), ())), preferred_element_type=jnp.float32
    )


def is_middle(index):
    return (index == 1) | (index == 2)


def product(parts, pieces, sent, kept):
    half = parts[0].shape[0] // 2
    for out, start in ((sent, 0), (kept, half)):
        whole = jnp.concatenate([part[start : start + half, :] for part in parts], 1)
        column = 0
        for weight, first, count in pieces:
            out[:, column : column + count] = times(
                whole, weight[first : first + count, :]
            ).astype(out.dtype)
            column += count


def core_sum(pair, upper):
    kept, from_core = pair
    half = kept.shape[0] // 2
    rows = slice(half, 2 * half) if upper else slice(0, half)
    return kept[rows, :].astype(jnp.float32) + from_core[rows, :].astype(jnp.float32)


def step_body(plan, *refs):
    refs = list(refs)

    def take(count):
        return [refs.pop(0) for _ in range(count)]

    rows = [take(count) for count in plan["rows"]]
    arrays = take(plan["arrays"])
    weights = [
        [[(arrays[index], first, count) for index, first, count in pieces] for pieces in weight]
        for weight in plan["weights"]
    ]
    cores = [[take(2) for _ in range(count)] for count in plan["cores"]]
    chips = [([take(2) for _ in range(count)], take(1)[0]) for count in plan["chips"]]
    take(plan["after"])
    outs = take(plan["outs"])
    middle = is_middle(lax.axis_index("node"))
    picks = (middle, jnp.logical_not(middle))
    fetched = None
    for order, weight in enumerate(weights):
        if len(weight) == 2 and not plan["direct"]:
            chosen, sem = refs
            fetched = order
            for pick, pieces in zip(picks, weight):
                column = 0
                for array, first, count in pieces:
                    source = array.at[pl.ds(first, count), :]
                    target = chosen.at[pl.ds(column, count), :]
                    pl.when(pick)(pltpu.make_async_copy(source, target, sem).start)
                    column += count
    made = [[(outs.pop(0), outs.pop(0)) for _ in rows] for _ in weights]
    for bundle in cores:
        out, column = outs.pop(0), 0
        for pair in bundle:
            width = pair[0].shape[1]
            out[:, column : column + width] = core_sum(pair, True).astype(out.dtype)
            column += width
    for bundle, from_chip in chips:
        column = 0
        for pair in bundle:
            out = outs.pop(0)
            width = out.shape[1]
            away = from_chip[:, column : column + width].astype(jnp.float32)
            out[...] = (core_sum(pair, False) + away).astype(out.dtype)
            column += width
    for order, (weight, pairs) in enumerate(zip(weights, made)):
        if order == fetched:
            pltpu.make_async_copy(chosen, chosen, sem).wait()
            weight = [[(chosen, 0, chosen.shape[0])]]
        for parts, (sent, kept) in zip(rows, pairs):
            if len(weight) == 2:
                for pick, pieces in zip(picks, weight):
                    pl.when(pick)(functools.partial(product, parts, pieces, sent, kept))
            else:
                product(parts, weight[0], sent, kept)


def step(rows=(), weights=(), cores=(), chips=(), after=(), direct=False):
    weights = [weight if isinstance(weight, tuple) else (weight,) for weight in weights]
    arrays, fetch, plans = [], [], []
    for weight in weights:
        plans.append([])
        for pieces in weight:
            plans[-1].append([])
            for array, first, count in pieces:
                known = [index for index, x in enumerate(arrays) if x is array]
                if not known:
                    known = [len(arrays)]
                    arrays.append(array)
                    fetch.append(len(weight) == 2 and not direct)
                plans[-1][-1].append((known[0], first, count))
    widths = [sum(count for _, _, count in weight[0]) for weight in weights]
    shapes = []
    for width in widths:
        shapes += [(parts[0].shape[0] // 2, width) for parts in rows for _ in range(2)]
    for bundle in cores:
        shapes.append((bundle[0][0].shape[0] // 2, sum(kept.shape[1] for kept, _ in bundle)))
    for bundle in chips:
        shapes += [(kept.shape[0] // 2, kept.shape[1]) for kept, _ in bundle[:-1]]
    plan = {
        "rows": [len(parts) for parts in rows],
        "arrays": len(arrays),
        "weights": plans,
        "cores": [len(bundle) for bundle in cores],
        "chips": [len(bundle) - 1 for bundle in chips],
        "after": len(after),
        "outs": len(shapes),
        "direct": direct,
    }
    vmem, hbm = pl.BlockSpec(memory_space=pltpu.VMEM), pl.BlockSpec(memory_space=pl.ANY)
    read = [(part, vmem) for parts in rows for part in parts]
    read += [(array, hbm if far else vmem) for array, far in zip(arrays, fetch)]
    read += [(x, vmem) for bundle in cores for pair in bundle for x in pair]
    for bundle in chips:
        read += [(x, vmem) for pair in bundle[:-1] for x in pair] + [(bundle[-1], vmem)]
    read += [(x, hbm) for x in after]
    dtype = read[0][0].dtype
    scratch = []
    if any(fetch):
        width = [w for w, weight in zip(widths, weights) if len(weight) == 2][0]
        scratch = [
            pltpu.VMEM((width, rows[0][0].shape[1] * len(rows[0])), dtype),
            pltpu.SemaphoreType.DMA,
        ]
    return pl.pallas_call(
        functools.partial(step_body, plan),
        out_shape=[jax.ShapeDtypeStruct(shape, dtype) for shape in shapes],
        in_specs=[spec for _, spec in read],
        scratch_shapes=scratch,
        compiler_params=pltpu.CompilerParams(vmem_limit_bytes=VMEM_LIMIT),
        cost_estimate=LIGHT,
        name="step",
    )(*[x for x, _ in read])


PAIRS = [(0, 1), (1, 0), (2, 3), (3, 2)]
MIDDLE = [(1, 2), (2, 1)]
OUTWARD = [(1, 0), (2, 3)]


def relay(piece, exported):
    near = lax.ppermute(piece, "node", PAIRS)
    across = lax.ppermute(piece, "node", MIDDLE)
    near, _ = lax.optimization_barrier((near, exported))
    across, _ = lax.optimization_barrier((across, exported))
    across_out = lax.ppermute(across, "node", OUTWARD)
    near_across = lax.ppermute(near, "node", MIDDLE)
    return near, across, near_across, across_out


def place_body(spots, features, *refs):
    sources, out, sem = refs[: len(spots)], refs[-2], refs[-1]
    half = features // 2
    device = lax.axis_index("node")
    mine = lax.axis_index("groups")
    copies = []
    for order, (source, (distance, side, offset)) in enumerate(zip(sources, spots)):
        group = {"own": mine, "other": 1 - mine, "first": 0}[side]
        column = pl.multiple_of((device ^ distance) * features + group * half + offset, HEAD)
        target = out.at[:, pl.ds(column, source.shape[1])]
        copies.append(pltpu.make_async_copy(source, target, sem.at[order]))
    for copy in copies:
        copy.start()
    for copy in copies:
        copy.wait()


def place(sources, spots, devices, features, begun=None):
    hbm = pl.BlockSpec(memory_space=pltpu.HBM)
    more = [] if begun is None else [begun]
    return pl.pallas_call(
        functools.partial(place_body, spots, features),
        out_shape=jax.ShapeDtypeStruct(
            (sources[0].shape[0], devices * features), sources[0].dtype
        ),
        in_specs=[pl.BlockSpec(memory_space=pltpu.VMEM)] * len(sources) + [hbm] * len(more),
        out_specs=hbm,
        input_output_aliases={len(sources): 0} if more else {},
        scratch_shapes=[pltpu.SemaphoreType.DMA((len(sources),))],
        compiler_params=pltpu.CompilerParams(vmem_limit_bytes=VMEM_LIMIT),
        cost_estimate=LIGHT,
        name="place",
    )(*sources, *more)


def cut_body(weight, out, sem):
    half = out.shape[0]
    rows = half // sem.shape[0]
    start = lax.axis_index("groups") * half
    copies = []
    for part in range(sem.shape[0]):
        source = weight.at[pl.ds(pl.multiple_of(start + part * rows, rows), rows), :]
        target = out.at[pl.ds(part * rows, rows), :]
        copies.append(pltpu.make_async_copy(source, target, sem.at[part]))
    for copy in copies:
        copy.start()
    for copy in copies:
        copy.wait()


def cut(weight):
    return pl.pallas_call(
        cut_body,
        out_shape=jax.ShapeDtypeStruct((weight.shape[0] // 2, weight.shape[1]), weight.dtype),
        in_specs=[pl.BlockSpec(memory_space=pltpu.HBM)],
        out_specs=pl.BlockSpec(memory_space=pltpu.VMEM),
        scratch_shapes=[pltpu.SemaphoreType.DMA((4,))],
        compiler_params=pltpu.CompilerParams(vmem_limit_bytes=VMEM_LIMIT),
        cost_estimate=LIGHT,
        name="cut",
    )(in_hbm(weight))


def project_split(halves, relayed, out_weight):
    features = out_weight.shape[0]
    half = features // 2
    rows = [part.reshape(-1, part.shape[-1]) for part in halves]
    other = [swap(part, "groups", 1) for part in rows]
    near, across, near_across, across_out = relayed
    far_out = lax.ppermute(near_across, "node", OUTWARD)

    def core(sent):
        return swap(sent, "tensor", 1)

    def chip(away):
        return swap(away, "tensor", 2)

    def back(done):
        return swap(done, "groups", 1)

    def whole(weight):
        return [(weight, 0, weight.shape[0])]

    second = (whole(near_across), whole(across_out))
    far = (whole(across), whole(far_out))

    last = features - HEAD
    sent_a, kept_a, sent_b, kept_b, sent_c, kept_c = step(
        [rows],
        [[(out_weight, 0, half)], [(out_weight, half, last - half)], [(out_weight, last, HEAD)]],
    )
    one = [(kept_a, core(sent_a)), (kept_b, core(sent_b))]
    (away,) = step(cores=[one])
    one.append(chip(away))
    sent_1, kept_1 = step([rows], [whole(near)], after=[away, other[0]])
    sent_2, kept_2, done_a, done_b = step([rows], [second], chips=[one], after=[sent_1])
    two = [(kept_c, core(sent_c)), (kept_1, core(sent_1)), (kept_2, core(sent_2))]
    (away,) = step(cores=[two])
    two.append(chip(away))
    sent_3, kept_3, sent_4, kept_4 = step([other], [whole(near), second], after=[away])
    three = [(kept_3, core(sent_3))]
    four = [(kept_4, core(sent_4))]
    away, done_c, done_1, done_2 = step(cores=[three], chips=[two])
    three.append(chip(away))
    away, done_3 = step(cores=[four], chips=[three])
    four.append(chip(away))
    back_3 = back(done_3)
    sent_5, kept_5 = step([other], [far], after=[away], direct=True)
    five = [(kept_5, core(sent_5))]
    (done_4,) = step(chips=[four], after=[sent_5, back_3])
    back_4 = back(done_4)
    sent_6, kept_6 = step([rows], [far], after=[done_4], direct=True)
    six = [(kept_6, core(sent_6))]
    (away,) = step(cores=[five], after=[sent_6])
    five.append(chip(away))
    (away,) = step(cores=[six], after=[away])
    six.append(chip(away))
    (done_5,) = step(chips=[five], after=[away, back_4])
    back_5 = back(done_5)
    devices = lax.axis_size("node")
    begun = place(
        (done_a, done_b, done_c, done_1, done_2, back_3, back_4),
        (
            (0, "first", 0),
            (0, "first", half),
            (0, "first", last),
            (1, "own", 0),
            (2, "own", 0),
            (1, "other", 0),
            (2, "other", 0),
        ),
        devices,
        features,
    )
    (done_6,) = step(chips=[six], after=[done_5, in_hbm(begun)])
    return place(
        (back_5, done_6), ((3, "other", 0), (3, "own", 0)), devices, features, begun
    )


def project_plain(halves, out_weight):
    attended = jnp.concatenate(halves, 2)
    parts, per_part, width = attended.shape
    me = lax.axis_index("tensor")
    order = slot_position(parts, jnp.arange(parts, dtype=jnp.int32) ^ me)
    rows = attended[order].reshape(parts * per_part, width)
    weight = lax.all_gather(out_weight, "node", axis=0, tiled=True)
    terms = times(rows, weight).astype(jnp.bfloat16)
    return lax.psum_scatter(terms, "tensor", scatter_dimension=0, tiled=True)


def local(queries, keys, values, out_weight, slot_nodes, ancestors, depth):
    parts = lax.axis_size("tensor")
    devices = lax.axis_size("node")
    features = out_weight.shape[0]
    kv_count = keys.shape[1] // HEAD
    relayed, after = None, []
    exported, table = prepare(slot_nodes, ancestors, depth, keys, values)
    got = lax.all_gather(exported, "node", axis=0, tiled=True)
    if (
        devices == 4
        and parts == 4
        and lax.axis_size("groups") == 2
        and features % (2 * HEAD) == 0
    ):
        relayed = relay(cut(out_weight), exported)
        after = relayed[:2]
    halves = []
    for kv in range(kv_count):
        halves.append(attend(kv, table, queries, keys, values, got, parts, after))
        after = halves[-1:]
    if relayed is None:
        return project_plain(halves, out_weight)
    return project_split(halves, relayed, out_weight)


def solution(mesh):
    placed = (
        P(("groups", "node"), "tensor"),
        P(("groups", "node"), "tensor"),
        P(("groups", "node"), "tensor"),
        P("node", "tensor"),
        P("groups"),
        P("groups", None),
        P("groups"),
    )
    return jax.shard_map(
        local,
        mesh=mesh,
        in_specs=placed,
        out_specs=P(("groups", "node", "tensor"), None),
        check_vma=False,
    )
```

profile of v0, /device:TPU:0, one launch (start us, length us, event | category | flops | bytes accessed | tf_op | source)
XLA Modules:
  0.0 170.8 jit_solution(15258696760241943672)
XLA Ops:
  6.6 2.7 %cut.1 = bf16[640,1280]{1,0:T(8,128)(2,1)} custom-call(bf16[1280,1280]{1,0:T(8,128)(2,1)} %refs_2_.3), custom_call_target="tpu_custom_call" | custom-call | flops 1 | bytes 1 | tf_op jit(solution)/shard_map/cut/pallas_call | solution.py:465
  9.2 3.1 %collective-permute-start = (bf16[640,1280]{1,0:T(8,128)(2,1)}, bf16[640,1280]{1,0:T(8,128)(2,1)S(1)}, u32[]{:S(2)}, u32[]{:S(2)}) collective-permute-start(bf16[640,1280]{1,0:T(8,128)(2,1)} %cut.1), channel_id=1, source_target_pairs={{0,4},{4,0},{8,12},{12,8},{1,5},{5,1},{9,13},{13,9},{2,6},{6,2},{1... | collective-permute-start | bytes 4915208 | tf_op jit(solution)/shard_map/ppermute | solution.py:405
  13.1 1.6 prepare.1
  14.7 50.5 %collective-permute-done.refs_0_.refs_2_ = bf16[640,1280]{1,0:T(8,128)(2,1)S(1)} collective-permute-done((bf16[640,1280]{1,0:T(8,128)(2,1)}, bf16[640,1280]{1,0:T(8,128)(2,1)S(1)}, u32[]{:S(2)}, u32[]{:S(2)}) %collective-permute-start) | collective-permute-done | bytes 1638432 | tf_op jit(solution)/shard_map/ppermute | solution.py:405
  65.2 1.9 %collective-permute-start.4 = (bf16[640,1280]{1,0:T(8,128)(2,1)S(1)}, bf16[640,1280]{1,0:T(8,128)(2,1)}, u32[]{:S(2)}, u32[]{:S(2)}) collective-permute-start(bf16[640,1280]{1,0:T(8,128)(2,1)S(1)} %collective-permute-done.refs_0_.refs_2_), channel_id=1, source_target_pairs={{4,8},{8,4},{5,9},{9,5},{6,10},{10,6},{7,11},{11,7},{20,24},{24,20... | collective-permute-start | bytes 4915208 | tf_op jit(solution)/shard_map/ppermute | solution.py:410
  68.4 8.5 %attend.2.refs_0_ = bf16[4,192,640]{2,1,0:T(8,128)(2,1)S(1)} custom-call(s32[8]{0:T(128)S(1)} %get-tuple-element.35.table, bf16[768,1280]{1,0:T(8,128)(2,1)} %query_hbm.3, bf16[768,256]{1,0:T(8,128)(2,1)} %keys_hbm.3, bf16[768,256]{1,0:T(8,128)(2,1)} %values_hbm.3, bf16[16,128,256]{2,1,0:T(8,128)(2,1)} %all-gather.2.cloned.1.call-done.got, ...), custom_call_target="tpu_custom_call" | custom-call | flops 1 | bytes 1 | tf_op jit(solution)/shard_map/attend/pallas_call | solution.py:228
  76.8 1.7 collective-permute-start.2
  78.5 8.5 %attend.3 = bf16[4,192,640]{2,1,0:T(8,128)(2,1)S(1)} custom-call(s32[8]{0:T(128)S(1)} %get-tuple-element.35.table, bf16[768,1280]{1,0:T(8,128)(2,1)} %query_hbm.3, bf16[768,256]{1,0:T(8,128)(2,1)} %keys_hbm.3, bf16[768,256]{1,0:T(8,128)(2,1)} %values_hbm.3, bf16[16,128,256]{2,1,0:T(8,128)(2,1)} %all-gather.2.cloned.1.call-done.got, ...), custom_call_target="tpu_custom_call" | custom-call | flops 1 | bytes 1 | tf_op jit(solution)/shard_map/attend/pallas_call | solution.py:228
  87.0 3.2 %step.15 = (bf16[384,640]{1,0:T(8,128)(2,1)S(1)}, bf16[384,640]{1,0:T(8,128)(2,1)S(1)}, bf16[384,512]{1,0:T(8,128)(2,1)S(1)}, bf16[384,512]{1,0:T(8,128)(2,1)S(1...) custom-call(bf16[768,640]{1,0:T(8,128)(2,1)S(1)} %bitcast.4, bf16[768,640]{1,0:T(8,128)(2,1)S(1)} %bitcast.8, ...), custom_call_target="tpu_custom_call" | custom-call | flops 1 | bytes 1 | tf_op jit(solution)/shard_map/step/pallas_call | solution.py:388
  90.8 1.9 %collective-permute-done.9.refs_3_.refs_7_ = bf16[384,512]{1,0:T(8,128)(2,1)S(1)} collective-permute-done((bf16[384,512]{1,0:T(8,128)(2,1)S(1)}, bf16[384,512]{1,0:T(8,128)(2,1)S(1)}, u32[]{:S(2)}, u32[]{:S(2)}) %collective-permute-start.9) | collective-permute-done | bytes 393248 | tf_op jit(solution)/shard_map/ppermute | solution.py:252
  92.9 1.6 collective-permute-start.11
  94.9 1.5 collective-permute-start.5
  96.4 5.2 %collective-permute-done.2.refs_4_.refs_0_ = bf16[768,640]{1,0:T(8,128)(2,1)S(1)} collective-permute-done((bf16[768,640]{1,0:T(8,128)(2,1)S(1)}, bf16[768,640]{1,0:T(8,128)(2,1)S(1)}, u32[]{:S(2)}, u32[]{:S(2)}) %collective-permute-start.2) | collective-permute-done | bytes 983072 | tf_op jit(solution)/shard_map/ppermute | solution.py:252
  101.6 1.7 %step.17 = (bf16[384,640]{1,0:T(8,128)(2,1)S(1)}, bf16[384,640]{1,0:T(8,128)(2,1)S(1)}) custom-call(bf16[768,640]{1,0:T(8,128)(2,1)S(1)} %bitcast.5, bf16[768,640]{1,0:T(8,128)(2,1)S(1)} %bitcast.10, bf16[640,1280]{1,0:T(8,128)(2,1)S(1)} %collective-permute-done.refs_0_.refs_2_, bf16[192,1152]{1,0:T(8,128)(2,1)S(1)} %step.16.refs_3_, ...), custom_call_target="tpu_custom_call" | custom-call | flops 1 | bytes 1 | tf_op jit(solution)/shard_map/step/pallas_call | solution.py:388
  103.4 1.8 %collective-permute-done.11.refs_8_ = bf16[192,1152]{1,0:T(8,128)(2,1)S(1)} collective-permute-done((bf16[192,1152]{1,0:T(8,128)(2,1)S(1)}, bf16[192,1152]{1,0:T(8,128)(2,1)S(1)}, u32[]{:S(2)}, u32[]{:S(2)}) %collective-permute-start.11) | collective-permute-done | bytes 442400 | tf_op jit(solution)/shard_map/ppermute | solution.py:252
  105.1 1.6 collective-permute-done.6.refs_3_.refs_4_
  106.8 3.2 %step.18 = (bf16[384,640]{1,0:T(8,128)(2,1)S(1)}, bf16[384,640]{1,0:T(8,128)(2,1)S(1)}, bf16[192,640]{1,0:T(8,128)(2,1)S(1)}, bf16[192,512]{1,0:T(8,128)(2,1)S(1)}) custom-call(bf16[768,640]{1,0:T(8,128)(2,1)S(1)} %bitcast.6, bf16[768,640]{1,0:T(8,128)(2,1)S(1)} %bitcast.11, bf16[640,1280]{1,0:T(8,128)(2,1)} %collective-permute-done.4.refs_2_.refs_3_, ...), custom_call_target="tpu_custom_call" | custom-call | flops 1 | bytes 1 | tf_op jit(solution)/shard_map/step/pallas_call | solution.py:388
  110.5 1.5 collective-permute-done.7.refs_1_.refs_3_
  112.2 1.6 collective-permute-start.15
  113.7 7.2 %collective-permute-done.3.refs_1_ = bf16[768,640]{1,0:T(8,128)(2,1)S(1)} collective-permute-done((bf16[768,640]{1,0:T(8,128)(2,1)S(1)}, bf16[768,640]{1,0:T(8,128)(2,1)S(1)}, u32[]{:S(2)}, u32[]{:S(2)}) %collective-permute-start.3) | collective-permute-done | bytes 983072 | tf_op jit(solution)/shard_map/ppermute | solution.py:252
  120.9 4.6 %step.20 = (bf16[384,640]{1,0:T(8,128)(2,1)S(1)}, bf16[384,640]{1,0:T(8,128)(2,1)S(1)}, bf16[384,640]{1,0:T(8,128)(2,1)S(1)}, bf16[384,640]{1,0:T(8,128)(2,1)S(1)}) custom-call(bf16[768,640]{1,0:T(8,128)(2,1)S(1)} %collective-permute-done.2.refs_4_.refs_0_, bf16[768,640]{1,0:T(8,128)(2,1)S(1)} %collective-permute-done.3.refs_1_, ...), custom_call_target="tpu_custom_call" | custom-call | flops 1 | bytes 1 | tf_op jit(solution)/shard_map/step/pallas_call | solution.py:388
  127.7 1.4 collective-permute-start.16
  129.1 6.7 %collective-permute-done.16.refs_4_ = bf16[192,640]{1,0:T(8,128)(2,1)S(1)} collective-permute-done((bf16[192,640]{1,0:T(8,128)(2,1)S(1)}, bf16[192,640]{1,0:T(8,128)(2,1)S(1)}, u32[]{:S(2)}, u32[]{:S(2)}) %collective-permute-start.16) | collective-permute-done | bytes 245792 | tf_op jit(solution)/shard_map/ppermute | solution.py:252
  137.3 1.5 collective-permute-start.19
  138.8 2.7 %collective-permute-done.5.refs_3_ = bf16[640,1280]{1,0:T(8,128)(2,1)S(1)} collective-permute-done((bf16[640,1280]{1,0:T(8,128)(2,1)}, bf16[640,1280]{1,0:T(8,128)(2,1)S(1)}, u32[]{:S(2)}, u32[]{:S(2)}) %collective-permute-start.5) | collective-permute-done | bytes 1638432 | tf_op jit(solution)/shard_map/ppermute | solution.py:483
  141.4 1.7 %step.23 = (bf16[384,640]{1,0:T(8,128)(2,1)S(1)}, bf16[384,640]{1,0:T(8,128)(2,1)S(1)}) custom-call(bf16[768,640]{1,0:T(8,128)(2,1)S(1)} %collective-permute-done.2.refs_4_.refs_0_, bf16[768,640]{1,0:T(8,128)(2,1)S(1)} %collective-permute-done.3.refs_1_, bf16[640,1280]{1,0:T(8,128)(2,1)S(1)} %collective-permute-done.1.refs_1_.refs_2_, ...), custom_call_target="tpu_custom_call" | custom-call | flops 1 | bytes 1 | tf_op jit(solution)/shard_map/step/pallas_call | solution.py:388
  144.3 1.7 %step.25 = (bf16[384,640]{1,0:T(8,128)(2,1)S(1)}, bf16[384,640]{1,0:T(8,128)(2,1)S(1)}) custom-call(bf16[768,640]{1,0:T(8,128)(2,1)S(1)} %bitcast.7, bf16[768,640]{1,0:T(8,128)(2,1)S(1)} %bitcast.12, bf16[640,1280]{1,0:T(8,128)(2,1)S(1)} %collective-permute-done.1.refs_1_.refs_2_, bf16[640,1280]{1,0:T(8,128)(2,1)S(1)} %collective-permute-done.5.refs_3_, ...), custom_call_target="tpu_custom_call" | custom-call | flops 1 | bytes 1 | tf_op jit(solution)/shard_map/step/pallas_call | solution.py:388
  146.1 1.5 collective-permute-start.22
  149.9 4.6 %collective-permute-done.22.refs_4_.refs_6_ = bf16[192,640]{1,0:T(8,128)(2,1)S(1)} collective-permute-done((bf16[192,640]{1,0:T(8,128)(2,1)S(1)}, bf16[192,640]{1,0:T(8,128)(2,1)S(1)}, u32[]{:S(2)}, u32[]{:S(2)}) %collective-permute-start.22) | collective-permute-done | bytes 245792 | tf_op jit(solution)/shard_map/ppermute | solution.py:252
  154.5 2.1 %collective-permute-done.20.refs_2_ = bf16[192,640]{1,0:T(8,128)(2,1)S(1)} collective-permute-done((bf16[192,640]{1,0:T(8,128)(2,1)S(1)}, bf16[192,640]{1,0:T(8,128)(2,1)S(1)}, u32[]{:S(2)}, u32[]{:S(2)}) %collective-permute-start.20) | collective-permute-done | bytes 245792 | tf_op jit(solution)/shard_map/ppermute | solution.py:252
  158.4 2.6 %collective-permute-done.24.refs_2_ = bf16[192,640]{1,0:T(8,128)(2,1)S(1)} collective-permute-done((bf16[192,640]{1,0:T(8,128)(2,1)S(1)}, bf16[192,640]{1,0:T(8,128)(2,1)S(1)}, u32[]{:S(2)}, u32[]{:S(2)}) %collective-permute-start.24) | collective-permute-done | bytes 245792 | tf_op jit(solution)/shard_map/ppermute | solution.py:252
  161.1 2.0 %collective-permute-done.23.refs_0_ = bf16[192,640]{1,0:T(8,128)(2,1)S(1)} collective-permute-done((bf16[192,640]{1,0:T(8,128)(2,1)S(1)}, bf16[192,640]{1,0:T(8,128)(2,1)S(1)}, u32[]{:S(2)}, u32[]{:S(2)}) %collective-permute-start.23) | collective-permute-done | bytes 245792 | tf_op jit(solution)/shard_map/ppermute | solution.py:252
  (54 shorter events, 14.0 us)
Async XLA Ops:
  6.5 6.5 %copy-start.3 = (s32[24,7]{0,1:T(8,128)S(1)}, s32[24,7]{0,1:T(8,128)}, u32[]{:S(2)}) copy-start(s32[24,7]{0,1:T(8,128)} %param.12) | copy-start | bytes 2020
  6.5 6.6 %copy-start.4 = (s32[24]{0:T(128)S(1)}, s32[24]{0:T(128)}, u32[]{:S(2)}) copy-start(s32[24]{0:T(128)} %refs_0_.1) | copy-start | bytes 292
  6.5 6.6 %copy-start.5 = (s32[24]{0:T(128)S(1)}, s32[24]{0:T(128)}, u32[]{:S(2)}) copy-start(s32[24]{0:T(128)} %refs_2_.2) | copy-start | bytes 292
  6.5 61.8 %all-gather.2.cloned.1.call-start = ((), (), s32[]{:S(2)}) async-start(), calls=%async_computation | async-start | bytes 1310720 | tf_op jit(solution)/shard_map/all_gather | solution.py:572
  6.5 6.6 %copy-start.1 = (bf16[768,256]{1,0:T(8,128)(2,1)S(1)}, bf16[768,256]{1,0:T(8,128)(2,1)}, u32[]{:S(2)}) copy-start(bf16[768,256]{1,0:T(8,128)(2,1)} %keys_hbm.3) | copy-start | bytes 1179652
  6.6 6.6 %copy-start.2 = (bf16[768,256]{1,0:T(8,128)(2,1)S(1)}, bf16[768,256]{1,0:T(8,128)(2,1)}, u32[]{:S(2)}) copy-start(bf16[768,256]{1,0:T(8,128)(2,1)} %values_hbm.3) | copy-start | bytes 1179652
  9.2 56.0 %collective-permute-start = (bf16[640,1280]{1,0:T(8,128)(2,1)}, bf16[640,1280]{1,0:T(8,128)(2,1)S(1)}, u32[]{:S(2)}, u32[]{:S(2)}) collective-permute-start(bf16[640,1280]{1,0:T(8,128)(2,1)} %cut.1), channel_id=1, source_target_pairs={{0,4},{4,0},{8,12},{12,8},{1,5},{5,1},{9,13},{13,9},{2,6},{6,2},{1... | collective-permute-start | bytes 4915208 | tf_op jit(solution)/shard_map/ppermute | solution.py:405
  12.3 54.7 %collective-permute-start.1 = (bf16[640,1280]{1,0:T(8,128)(2,1)}, bf16[640,1280]{1,0:T(8,128)(2,1)S(1)}, u32[]{:S(2)}, u32[]{:S(2)}) collective-permute-start(bf16[640,1280]{1,0:T(8,128)(2,1)} %cut.1), channel_id=1, source_target_pairs={{4,8},{8,4},{5,9},{9,5},{6,10},{10,6},{7,11},{11,7},{20,24},{24,20... | collective-permute-start | bytes 4915208 | tf_op jit(solution)/shard_map/ppermute | solution.py:406
  65.2 29.7 %collective-permute-start.4 = (bf16[640,1280]{1,0:T(8,128)(2,1)S(1)}, bf16[640,1280]{1,0:T(8,128)(2,1)}, u32[]{:S(2)}, u32[]{:S(2)}) collective-permute-start(bf16[640,1280]{1,0:T(8,128)(2,1)S(1)} %collective-permute-done.refs_0_.refs_2_), channel_id=1, source_target_pairs={{4,8},{8,4},{5,9},{9,5},{6,10},{10,6},{7,11},{11,7},{20,24},{24,20... | collective-permute-start | bytes 4915208 | tf_op jit(solution)/shard_map/ppermute | solution.py:410
  67.0 39.7 %collective-permute-start.6 = (bf16[640,1280]{1,0:T(8,128)(2,1)S(1)}, bf16[640,1280]{1,0:T(8,128)(2,1)}, u32[]{:S(2)}, u32[]{:S(2)}) collective-permute-start(bf16[640,1280]{1,0:T(8,128)(2,1)S(1)} %collective-permute-done.1.refs_1_.refs_2_), channel_id=1, source_target_pairs={{4,0},{8,12},{5,1},{9,13},{6,2},{10,14},{7,3},{11,15},{20,16},{24,... | collective-permute-start | bytes 4915208 | tf_op jit(solution)/shard_map/ppermute | solution.py:409
  76.8 10.2 %copy-start = (bf16[1280,1280]{1,0:T(8,128)(2,1)S(1)}, bf16[1280,1280]{1,0:T(8,128)(2,1)}, u32[]{:S(2)}) copy-start(bf16[1280,1280]{1,0:T(8,128)(2,1)} %refs_2_.3) | copy-start | bytes 9830404
  76.8 24.8 %collective-permute-start.2 = (bf16[768,640]{1,0:T(8,128)(2,1)S(1)}, bf16[768,640]{1,0:T(8,128)(2,1)S(1)}, u32[]{:S(2)}, u32[]{:S(2)}) collective-permute-start(bf16[768,640]{1,0:T(8,128)(2,1)S(1)} %bitcast.3), channel_id=1, source_target_pairs={{0,16},{16,0},{1,17},{17,1},{2,18},{18,2},{3,19},{19,3},{4,20},{20... | collective-permute-start | bytes 2949128 | tf_op jit(solution)/shard_map/ppermute | solution.py:252
  90.3 2.5 %collective-permute-start.8 = (bf16[384,640]{1,0:T(8,128)(2,1)S(1)}, bf16[384,640]{1,0:T(8,128)(2,1)S(1)}, u32[]{:S(2)}, u32[]{:S(2)}) collective-permute-start(bf16[384,640]{1,0:T(8,128)(2,1)S(1)} %get-tuple-element.42), channel_id=1, source_target_pairs={{0,1},{1,0},{2,3},{3,2},{4,5},{5,4},{6,7},{7,6},{8,9},{9,8},{10,11... | collective-permute-start | bytes 1474568 | tf_op jit(solution)/shard_map/ppermute | solution.py:252
  90.3 2.4 %collective-permute-start.9 = (bf16[384,512]{1,0:T(8,128)(2,1)S(1)}, bf16[384,512]{1,0:T(8,128)(2,1)S(1)}, u32[]{:S(2)}, u32[]{:S(2)}) collective-permute-start(bf16[384,512]{1,0:T(8,128)(2,1)S(1)} %get-tuple-element.44), channel_id=1, source_target_pairs={{0,1},{1,0},{2,3},{3,2},{4,5},{5,4},{6,7},{7,6},{8,9},{9,8},{10,11... | collective-permute-start | bytes 1179656 | tf_op jit(solution)/shard_map/ppermute | solution.py:252
  92.9 12.3 %collective-permute-start.11 = (bf16[192,1152]{1,0:T(8,128)(2,1)S(1)}, bf16[192,1152]{1,0:T(8,128)(2,1)S(1)}, u32[]{:S(2)}, u32[]{:S(2)}) collective-permute-start(bf16[192,1152]{1,0:T(8,128)(2,1)S(1)} %step.16.refs_3_), channel_id=1, source_target_pairs={{0,2},{1,3},{2,0},{3,1},{4,6},{5,7},{6,4},{7,5},{8,10},{9,11},{10,... | collective-permute-start | bytes 1327112 | tf_op jit(solution)/shard_map/ppermute | solution.py:252
  94.4 26.5 %collective-permute-start.3 = (bf16[768,640]{1,0:T(8,128)(2,1)S(1)}, bf16[768,640]{1,0:T(8,128)(2,1)S(1)}, u32[]{:S(2)}, u32[]{:S(2)}) collective-permute-start(bf16[768,640]{1,0:T(8,128)(2,1)S(1)} %bitcast.9), channel_id=1, source_target_pairs={{0,16},{16,0},{1,17},{17,1},{2,18},{18,2},{3,19},{19,3},{4,20},{20... | collective-permute-start | bytes 2949128 | tf_op jit(solution)/shard_map/ppermute | solution.py:252
  94.9 46.5 %collective-permute-start.5 = (bf16[640,1280]{1,0:T(8,128)(2,1)}, bf16[640,1280]{1,0:T(8,128)(2,1)S(1)}, u32[]{:S(2)}, u32[]{:S(2)}) collective-permute-start(bf16[640,1280]{1,0:T(8,128)(2,1)} %collective-permute-done.4.refs_2_.refs_3_), channel_id=1, source_target_pairs={{4,0},{8,12},{5,1},{9,13},{6,2},{10,14},{7,3},{11,15},{20,16},{24,... | collective-permute-start | bytes 4915208 | tf_op jit(solution)/shard_map/ppermute | solution.py:483
  103.3 8.7 %collective-permute-start.10 = (bf16[384,640]{1,0:T(8,128)(2,1)S(1)}, bf16[384,640]{1,0:T(8,128)(2,1)S(1)}, u32[]{:S(2)}, u32[]{:S(2)}) collective-permute-start(bf16[384,640]{1,0:T(8,128)(2,1)S(1)} %get-tuple-element.46.refs_9_), channel_id=1, source_target_pairs={{0,1},{1,0},{2,3},{3,2},{4,5},{5,4},{6,7},{7,6},{8,9},{9,8},{10,11... | collective-permute-start | bytes 1474568 | tf_op jit(solution)/shard_map/ppermute | solution.py:252
  109.9 2.1 %collective-permute-start.12 = (bf16[384,640]{1,0:T(8,128)(2,1)S(1)}, bf16[384,640]{1,0:T(8,128)(2,1)S(1)}, u32[]{:S(2)}, u32[]{:S(2)}) collective-permute-start(bf16[384,640]{1,0:T(8,128)(2,1)S(1)} %get-tuple-element.48), channel_id=1, source_target_pairs={{0,1},{1,0},{2,3},{3,2},{4,5},{5,4},{6,7},{7,6},{8,9},{9,8},{10,11... | collective-permute-start | bytes 1474568 | tf_op jit(solution)/shard_map/ppermute | solution.py:252
  110.0 2.0 %collective-permute-start.7 = (bf16[384,128]{1,0:T(8,128)(2,1)S(1)}, bf16[384,128]{1,0:T(8,128)(2,1)S(1)}, u32[]{:S(2)}, u32[]{:S(2)}) collective-permute-start(bf16[384,128]{1,0:T(8,128)(2,1)S(1)} %get-tuple-element.40), channel_id=1, source_target_pairs={{0,1},{1,0},{2,3},{3,2},{4,5},{5,4},{6,7},{7,6},{8,9},{9,8},{10,11... | collective-permute-start | bytes 294920 | tf_op jit(solution)/shard_map/ppermute | solution.py:252
  112.2 15.3 %collective-permute-start.15 = (bf16[192,1408]{1,0:T(8,128)(2,1)S(1)}, bf16[192,1408]{1,0:T(8,128)(2,1)S(1)}, u32[]{:S(2)}, u32[]{:S(2)}) collective-permute-start(bf16[192,1408]{1,0:T(8,128)(2,1)S(1)} %step.19.refs_5_), channel_id=1, source_target_pairs={{0,2},{1,3},{2,0},{3,1},{4,6},{5,7},{6,4},{7,5},{8,10},{9,11},{10,... | collective-permute-start | bytes 1622024 | tf_op jit(solution)/shard_map/ppermute | solution.py:252
  125.5 1.9 %collective-permute-start.14 = (bf16[384,640]{1,0:T(8,128)(2,1)S(1)}, bf16[384,640]{1,0:T(8,128)(2,1)S(1)}, u32[]{:S(2)}, u32[]{:S(2)}) collective-permute-start(bf16[384,640]{1,0:T(8,128)(2,1)S(1)} %get-tuple-element.52), channel_id=1, source_target_pairs={{0,1},{1,0},{2,3},{3,2},{4,5},{5,4},{6,7},{7,6},{8,9},{9,8},{10,11... | collective-permute-start | bytes 1474568 | tf_op jit(solution)/shard_map/ppermute | solution.py:252
  125.6 3.5 %collective-permute-start.13 = (bf16[384,640]{1,0:T(8,128)(2,1)S(1)}, bf16[384,640]{1,0:T(8,128)(2,1)S(1)}, u32[]{:S(2)}, u32[]{:S(2)}) collective-permute-start(bf16[384,640]{1,0:T(8,128)(2,1)S(1)} %get-tuple-element.50), channel_id=1, source_target_pairs={{0,1},{1,0},{2,3},{3,2},{4,5},{5,4},{6,7},{7,6},{8,9},{9,8},{10,11... | collective-permute-start | bytes 1474568 | tf_op jit(solution)/shard_map/ppermute | solution.py:252
  127.7 8.1 %collective-permute-start.16 = (bf16[192,640]{1,0:T(8,128)(2,1)S(1)}, bf16[192,640]{1,0:T(8,128)(2,1)S(1)}, u32[]{:S(2)}, u32[]{:S(2)}) collective-permute-start(bf16[192,640]{1,0:T(8,128)(2,1)S(1)} %get-tuple-element.53), channel_id=1, source_target_pairs={{0,2},{1,3},{2,0},{3,1},{4,6},{5,7},{6,4},{7,5},{8,10},{9,11},{10,... | collective-permute-start | bytes 737288 | tf_op jit(solution)/shard_map/ppermute | solution.py:252
  135.9 7.4 %collective-permute-start.18 = (bf16[192,640]{1,0:T(8,128)(2,1)S(1)}, bf16[192,640]{1,0:T(8,128)(2,1)S(1)}, u32[]{:S(2)}, u32[]{:S(2)}) collective-permute-start(bf16[192,640]{1,0:T(8,128)(2,1)S(1)} %get-tuple-element.54.refs_4_), channel_id=1, source_target_pairs={{0,2},{1,3},{2,0},{3,1},{4,6},{5,7},{6,4},{7,5},{8,10},{9,11},{10,... | collective-permute-start | bytes 737288 | tf_op jit(solution)/shard_map/ppermute | solution.py:252
  137.3 6.9 %collective-permute-start.19 = (bf16[192,640]{1,0:T(8,128)(2,1)S(1)}, bf16[192,640]{1,0:T(8,128)(2,1)S(1)}, u32[]{:S(2)}, u32[]{:S(2)}) collective-permute-start(bf16[192,640]{1,0:T(8,128)(2,1)S(1)} %get-tuple-element.57), channel_id=1, source_target_pairs={{0,16},{16,0},{1,17},{17,1},{2,18},{18,2},{3,19},{19,3},{4,20},{20... | collective-permute-start | bytes 737288 | tf_op jit(solution)/shard_map/ppermute | solution.py:252
  143.2 4.5 %collective-permute-start.17 = (bf16[384,640]{1,0:T(8,128)(2,1)S(1)}, bf16[384,640]{1,0:T(8,128)(2,1)S(1)}, u32[]{:S(2)}, u32[]{:S(2)}) collective-permute-start(bf16[384,640]{1,0:T(8,128)(2,1)S(1)} %get-tuple-element.56.refs_3_), channel_id=1, source_target_pairs={{0,1},{1,0},{2,3},{3,2},{4,5},{5,4},{6,7},{7,6},{8,9},{9,8},{10,11... | collective-permute-start | bytes 1474568 | tf_op jit(solution)/shard_map/ppermute | solution.py:252
  146.0 2.8 %collective-permute-start.21 = (bf16[384,640]{1,0:T(8,128)(2,1)S(1)}, bf16[384,640]{1,0:T(8,128)(2,1)S(1)}, u32[]{:S(2)}, u32[]{:S(2)}) collective-permute-start(bf16[384,640]{1,0:T(8,128)(2,1)S(1)} %get-tuple-element.58.refs_2_), channel_id=1, source_target_pairs={{0,1},{1,0},{2,3},{3,2},{4,5},{5,4},{6,7},{7,6},{8,9},{9,8},{10,11... | collective-permute-start | bytes 1474568 | tf_op jit(solution)/shard_map/ppermute | solution.py:252
  146.1 8.4 %collective-permute-start.22 = (bf16[192,640]{1,0:T(8,128)(2,1)S(1)}, bf16[192,640]{1,0:T(8,128)(2,1)S(1)}, u32[]{:S(2)}, u32[]{:S(2)}) collective-permute-start(bf16[192,640]{1,0:T(8,128)(2,1)S(1)} %step.24.refs_4_), channel_id=1, source_target_pairs={{0,16},{16,0},{1,17},{17,1},{2,18},{18,2},{3,19},{19,3},{4,20},{20... | collective-permute-start | bytes 737288 | tf_op jit(solution)/shard_map/ppermute | solution.py:252
  147.7 8.9 %collective-permute-start.20 = (bf16[192,640]{1,0:T(8,128)(2,1)S(1)}, bf16[192,640]{1,0:T(8,128)(2,1)S(1)}, u32[]{:S(2)}, u32[]{:S(2)}) collective-permute-start(bf16[192,640]{1,0:T(8,128)(2,1)S(1)} %step.26.refs_2_), channel_id=1, source_target_pairs={{0,2},{1,3},{2,0},{3,1},{4,6},{5,7},{6,4},{7,5},{8,10},{9,11},{10,... | collective-permute-start | bytes 737288 | tf_op jit(solution)/shard_map/ppermute | solution.py:252
  148.9 12.2 %collective-permute-start.24 = (bf16[192,640]{1,0:T(8,128)(2,1)S(1)}, bf16[192,640]{1,0:T(8,128)(2,1)S(1)}, u32[]{:S(2)}, u32[]{:S(2)}) collective-permute-start(bf16[192,640]{1,0:T(8,128)(2,1)S(1)} %step.27.refs_3_), channel_id=1, source_target_pairs={{0,2},{1,3},{2,0},{3,1},{4,6},{5,7},{6,4},{7,5},{8,10},{9,11},{10,... | collective-permute-start | bytes 737288 | tf_op jit(solution)/shard_map/ppermute | solution.py:252
  156.7 6.5 %collective-permute-start.23 = (bf16[192,640]{1,0:T(8,128)(2,1)S(1)}, bf16[192,640]{1,0:T(8,128)(2,1)S(1)}, u32[]{:S(2)}, u32[]{:S(2)}) collective-permute-start(bf16[192,640]{1,0:T(8,128)(2,1)S(1)} %step.28.refs_3_), channel_id=1, source_target_pairs={{0,16},{16,0},{1,17},{17,1},{2,18},{18,2},{3,19},{19,3},{4,20},{20... | collective-permute-start | bytes 737288 | tf_op jit(solution)/shard_map/ppermute | solution.py:252
Sparse Core Ops, SparseCore 0:
  14.8 43.9 all-gather.1
where the time goes:
time: 173 us; the launch traced here: 171 us
  waiting for transfers between devices  92.6 us (54%)
  Pallas kernels  40.3 us (23%)
  starting transfers between devices  24.2 us (14%)
  between operations  13.7 us (8%)
    ppermute x1, waiting for transfers between devices, relay(): near = lax.ppermute(piece, 'node', PAIRS)  50.5 us
    ppermute x20, waiting for transfers between devices, swap(): return lax.ppermute(array, axis, [(i, i ^ distance) for i in range(size)])  37.8 us
    pallas_call x15, Pallas kernels, step(): pl.pallas_call(functools.partial(step_body, plan), out_shape=[jax.ShapeDt...  17.2 us
    pallas_call x2, Pallas kernels, attend(): pl.pallas_call(functools.partial(attend_body, kv, parts), out_shape=jax.S...  16.9 us
    ppermute x20, starting transfers between devices, swap(): return lax.ppermute(array, axis, [(i, i ^ distance) for i in range(size)])  15.8 us
  transfers between devices with their start and end apart: 26, of which 15 were waited for; matrix products, arithmetic and copies ran while one was open for 0% of the time, Pallas kernels for 22%

commit v1 on v0

--- a/solution.py
+++ b/solution.py
@@ -20,7 +20,7 @@
 ATTEND_LIMIT = 24 * 1024 * 1024
 
 
-def prepare_body(nodes, *refs):
+def prepare_body(nodes, relative, *refs):
     slot_hbm, ancestors_hbm, depth_hbm, keys, values, exported, table_hbm = refs[:7]
     slot_nodes, ancestors, depth, table, holder, within, roots, sem = refs[7:]
     devices = slot_nodes.shape[0] // nodes
@@ -76,7 +76,8 @@
     table[1] = count
     for step in range(CHAIN):
         above = jnp.maximum(ancestors[step, root_node], 0)
-        entry = holder[above] * (2 * EXPORTS) + (1 if step % 2 == 0 else 0)
+        where = (holder[above] ^ me) - 1 if relative else holder[above]
+        entry = where * (2 * EXPORTS) + (1 if step % 2 == 0 else 0)
         table[2 + step] = jnp.where(step < count, entry, 0)
     store = pltpu.make_async_copy(table, table_hbm, sem.at[2 * EXPORTS])
     store.start()
@@ -84,13 +85,13 @@
         copy.wait()
 
 
-def prepare(slot_nodes, ancestors, depth, keys, values):
+def prepare(slot_nodes, ancestors, depth, keys, values, relative):
     nodes = keys.shape[0] // NODE_TOK
     slots = slot_nodes.shape[0]
     hbm = pl.BlockSpec(memory_space=pltpu.HBM)
     vmem = pl.BlockSpec(memory_space=pltpu.VMEM)
     return pl.pallas_call(
-        functools.partial(prepare_body, nodes),
+        functools.partial(prepare_body, nodes, relative),
         out_shape=(
             jax.ShapeDtypeStruct((2 * EXPORTS, NODE_TOK, keys.shape[1]), keys.dtype),
             jax.ShapeDtypeStruct((2 + CHAIN,), jnp.int32),
@@ -112,7 +113,8 @@
     )(slot_nodes, ancestors.T, depth, keys, values)
 
 
-def attend_body(kv, parts, table, query_hbm, keys_hbm, values_hbm, got, *refs):
+def attend_body(kv, parts, count, table, query_hbm, keys_hbm, values_hbm, *refs):
+    got = refs[:count]
     out, query, keys, values, above_keys, above_values, all_keys, all_values, sem = refs[-9:]
     nodes = query.shape[0] // NODE_TOK
     group = query.shape[1] // HEAD
@@ -120,10 +122,6 @@
     side = all_keys.shape[0]
     lanes = pl.ds(kv * HEAD, HEAD)
     pairs = [(keys_hbm.at[:, lanes], keys), (values_hbm.at[:, lanes], values)]
-    for step in range(CHAIN):
-        entry = table[2 + step]
-        pairs.append((got.at[entry, :, lanes], above_keys.at[step]))
-        pairs.append((got.at[entry + EXPORTS, :, lanes], above_values.at[step]))
     pairs.append((query_hbm.at[:, pl.ds(kv * group * HEAD, group * HEAD)], query))
     copies = [
         pltpu.make_async_copy(source, target, sem.at[order])
@@ -131,6 +129,20 @@
     ]
     for copy in copies:
         copy.start()
+    for step in range(CHAIN):
+        each = got[0].shape[0]
+        for order, array in enumerate(got):
+            entry = table[2 + step] - order * each
+            inside = jnp.clip(entry, 0, each - 1 - EXPORTS)
+            blocks = (
+                (array.at[inside, :, lanes], above_keys.at[step]),
+                (array.at[inside + EXPORTS, :, lanes], above_values.at[step]),
+            )
+            for part, (source, target) in enumerate(blocks):
+                copy = pltpu.make_async_copy(source, target, sem.at[3 + 2 * step + part])
+                pl.when((entry >= 0) & (entry < each))(copy.start)
+                if order == 0:
+                    copies.append(copy)
     ones = jnp.ones((NODE_TOK, HEAD), all_values.dtype)
     nothing = jnp.zeros((NODE_TOK, 2 * HEAD), all_values.dtype)
     query_index = lax.broadcasted_iota(jnp.int32, (NODE_TOK, NODE_TOK), 0)
@@ -226,11 +238,11 @@
     side = 2 if rows % (2 * NODE_TOK) == 0 else 1
     hbm = pl.BlockSpec(memory_space=pltpu.HBM)
     return pl.pallas_call(
-        functools.partial(attend_body, kv, parts),
+        functools.partial(attend_body, kv, parts, len(got)),
         out_shape=jax.ShapeDtypeStruct((parts, rows // parts, width), queries.dtype),
         in_specs=[pl.BlockSpec(memory_space=pltpu.SMEM)]
-        + [hbm] * 4
-        + [pl.BlockSpec(memory_space=pl.ANY)] * len(after),
+        + [hbm] * 3
+        + [pl.BlockSpec(memory_space=pl.ANY)] * (len(got) + len(after)),
         scratch_shapes=[
             pltpu.VMEM((rows, width), queries.dtype),
             pltpu.VMEM((rows, HEAD), keys.dtype),
@@ -244,7 +256,7 @@
         compiler_params=pltpu.CompilerParams(vmem_limit_bytes=ATTEND_LIMIT),
         cost_estimate=LIGHT,
         name="attend",
-    )(table, *[in_hbm(x) for x in (queries, keys, values, got)], *after)
+    )(table, *[in_hbm(x) for x in (queries, keys, values)], *got, *after)
 
 
 def swap(array, axis, distance):
@@ -401,11 +413,11 @@
 OUTWARD = [(1, 0), (2, 3)]
 
 
-def relay(piece, exported):
+def relay(piece, got):
     near = lax.ppermute(piece, "node", PAIRS)
     across = lax.ppermute(piece, "node", MIDDLE)
-    near, _ = lax.optimization_barrier((near, exported))
-    across, _ = lax.optimization_barrier((across, exported))
+    near, _ = lax.optimization_barrier((near, got))
+    across, _ = lax.optimization_barrier((across, got))
     across_out = lax.ppermute(across, "node", OUTWARD)
     near_across = lax.ppermute(near, "node", MIDDLE)
     return near, across, near_across, across_out
@@ -568,15 +580,19 @@
     features = out_weight.shape[0]
     kv_count = keys.shape[1] // HEAD
     relayed, after = None, []
-    exported, table = prepare(slot_nodes, ancestors, depth, keys, values)
-    got = lax.all_gather(exported, "node", axis=0, tiled=True)
+    relative = devices == 4
+    exported, table = prepare(slot_nodes, ancestors, depth, keys, values, relative)
+    if relative:
+        got = [swap(exported, "node", distance) for distance in (1, 2, 3)]
+    else:
+        got = [lax.all_gather(exported, "node", axis=0, tiled=True)]
     if (
         devices == 4
         and parts == 4
         and lax.axis_size("groups") == 2
         and features % (2 * HEAD) == 0
     ):
-        relayed = relay(cut(out_weight), exported)
+        relayed = relay(cut(out_weight), got)
         after = relayed[:2]
     halves = []
     for kv in range(kv_count):

time: 173 us -> 164 us (0.948); the launches traced: 171 us -> 164 us
  between operations: 13.7 us -> 0.47 us
  starting transfers between devices: 24.2 us -> 30.4 us
  waiting for transfers between devices: 92.6 us -> 96 us
  Pallas kernels: 40.3 us -> 37.2 us
    ppermute x1, waiting for transfers between devices: 50.5 us -> 0.01 us  [relay(): near = lax.ppermute(piece, 'node', PAIRS)]
    ppermute x20 -> x23, waiting for transfers between devices: 37.8 us -> 84.6 us  [swap(): return lax.ppermute(array, axis, [(i, i ^ distance) for i in range(size)])]
    ppermute x20 -> x23, starting transfers between devices: 15.8 us -> 23.2 us  [swap(): return lax.ppermute(array, axis, [(i, i ^ distance) for i in range(size)])]
    ppermute x1, waiting for transfers between devices: 1.62 us -> 6.28 us  [relay(): across_out = lax.ppermute(across, 'node', OUTWARD)]
    ppermute x1, waiting for transfers between devices: 2.69 us -> 5.1 us  [project_split(): far_out = lax.ppermute(near_across, 'node', OUTWARD)]
    pallas_call x15, Pallas kernels: 17.2 us -> 15.3 us  [step(): pl.pallas_call(functools.partial(step_body, plan), out_shape=[jax.ShapeDt...]
  transfers between devices with their start and end apart: 26 -> 28, of which waited for: 15 -> 16; matrix products, arithmetic and copies ran while one was open for 0% -> 0% of each run, Pallas kernels for 22% -> 21%
where the time goes in v1:
time: 164 us
  waiting for transfers between devices  96 us (59%)
  Pallas kernels  37.2 us (23%)
  starting transfers between devices  30.4 us (19%)
    ppermute x23, waiting for transfers between devices, swap(): return lax.ppermute(array, axis, [(i, i ^ distance) for i in range(size)])  84.6 us
    ppermute x23, starting transfers between devices, swap(): return lax.ppermute(array, axis, [(i, i ^ distance) for i in range(size)])  23.2 us
    pallas_call x2, Pallas kernels, attend(): pl.pallas_call(functools.partial(attend_body, kv, parts, len(got)), out_s...  16.6 us
    pallas_call x15, Pallas kernels, step(): pl.pallas_call(functools.partial(step_body, plan), out_shape=[jax.ShapeDt...  15.3 us
    ppermute x1, waiting for transfers between devices, relay(): across_out = lax.ppermute(across, 'node', OUTWARD)  6.28 us
    ppermute x1, waiting for transfers between devices, project_split(): far_out = lax.ppermute(near_across, 'node', OUTWARD)  5.1 us
  transfers between devices with their start and end apart: 28, of which 16 were waited for; matrix products, arithmetic and copies ran while one was open for 0% of the time, Pallas kernels for 21%

profile of v1, /device:TPU:0, one launch (start us, length us, event | category | flops | bytes accessed | tf_op | source)
XLA Modules:
  0.0 164.0 jit_solution(5390162758299859885)
XLA Ops:
  1.5 3.1 %collective-permute-start.3 = (bf16[640,1280]{1,0:T(8,128)(2,1)S(1)}, bf16[640,1280]{1,0:T(8,128)(2,1)S(1)}, u32[]{:S(2)}, u32[]{:S(2)}) collective-permute-start(bf16[640,1280]{1,0:T(8,128)(2,1)S(1)} %cut.1), channel_id=1, source_target_pairs={{0,4},{4,0},{8,12},{12,8},{1,5},{5,1},{9,13},{13,9},{2,6},{6,2},{1... | collective-permute-start | bytes 4915208 | tf_op jit(solution)/shard_map/ppermute | solution.py:417
  5.4 1.8 %prepare.1 = (bf16[4,128,256]{2,1,0:T(8,128)(2,1)S(1)}, s32[8]{0:T(128)S(1)}) custom-call(s32[24]{0:T(128)S(1)} %copy-done.4, s32[7,24]{1,0:T(8,128)S(1)} %bitcast.13, s32[24]{0:T(128)S(1)} %copy-done.5, bf16[768,256]{1,0:T(8,128)(2,1)S(1)} %copy-done.1, bf16[768,256]{1,0:T(8,128)(2,1)S(1)} %copy-done.2), custom_call_target="tpu_custom_call" | custom-call | tf_op jit(solution)/shard_map/prepare/pallas_call | solution.py:93
  7.3 4.4 %collective-permute-start = (bf16[4,128,256]{2,1,0:T(8,128)(2,1)S(1)}, bf16[4,128,256]{2,1,0:T(8,128)(2,1)S(1)}, u32[]{:S(2)}, u32[]{:S(2)}) collective-permute-start(bf16[4,128,256]{2,1,0:T(8,128)(2,1)S(1)} %get-tuple-element.36), channel_id=1, source_target_pairs={{0,4},{4,0},{8,12},{12,8},{1,5},{5,1},{9,13},{13,9},{2,6},{6,2},{1... | collective-permute-start | bytes 786440 | tf_op jit(solution)/shard_map/ppermute | solution.py:264
  11.6 2.4 %collective-permute-start.2 = (bf16[4,128,256]{2,1,0:T(8,128)(2,1)S(1)}, bf16[4,128,256]{2,1,0:T(8,128)(2,1)S(1)}, u32[]{:S(2)}, u32[]{:S(2)}) collective-permute-start(bf16[4,128,256]{2,1,0:T(8,128)(2,1)S(1)} %get-tuple-element.36), channel_id=1, source_target_pairs={{0,12},{4,8},{8,4},{12,0},{1,13},{5,9},{9,5},{13,1},{2,14},{6,10},... | collective-permute-start | bytes 786440 | tf_op jit(solution)/shard_map/ppermute | solution.py:264
  14.1 35.7 %collective-permute-done.refs_0_ = bf16[4,128,256]{2,1,0:T(8,128)(2,1)S(1)} collective-permute-done((bf16[4,128,256]{2,1,0:T(8,128)(2,1)S(1)}, bf16[4,128,256]{2,1,0:T(8,128)(2,1)S(1)}, u32[]{:S(2)}, u32[]{:S(2)}) %collective-permute-start) | collective-permute-done | bytes 262176 | tf_op jit(solution)/shard_map/ppermute | solution.py:264
  49.7 13.0 %collective-permute-done.1.refs_1_ = bf16[4,128,256]{2,1,0:T(8,128)(2,1)S(1)} collective-permute-done((bf16[4,128,256]{2,1,0:T(8,128)(2,1)S(1)}, bf16[4,128,256]{2,1,0:T(8,128)(2,1)S(1)}, u32[]{:S(2)}, u32[]{:S(2)}) %collective-permute-start.1) | collective-permute-done | bytes 262176 | tf_op jit(solution)/shard_map/ppermute | solution.py:264
  64.7 8.3 %attend.2.refs_3_ = bf16[4,192,640]{2,1,0:T(8,128)(2,1)S(1)} custom-call(s32[8]{0:T(128)S(1)} %get-tuple-element.35.table, bf16[768,1280]{1,0:T(8,128)(2,1)} %query_hbm.3, bf16[768,256]{1,0:T(8,128)(2,1)} %keys_hbm.3, bf16[768,256]{1,0:T(8,128)(2,1)} %values_hbm.3, bf16[4,128,256]{2,1,0:T(8,128)(2,1)S(1)} %collective-permute-done.refs_0_, ...), custom_call_target="tpu_custom_call" | custom-call | flops 1 | bytes 1 | tf_op jit(solution)/shard_map/attend/pallas_call | solution.py:240
  73.1 1.5 collective-permute-start.5
  74.6 8.3 %attend.3 = bf16[4,192,640]{2,1,0:T(8,128)(2,1)S(1)} custom-call(s32[8]{0:T(128)S(1)} %get-tuple-element.35.table, bf16[768,1280]{1,0:T(8,128)(2,1)} %query_hbm.3, bf16[768,256]{1,0:T(8,128)(2,1)} %keys_hbm.3, bf16[768,256]{1,0:T(8,128)(2,1)} %values_hbm.3, bf16[4,128,256]{2,1,0:T(8,128)(2,1)S(1)} %collective-permute-done.refs_0_, ...), custom_call_target="tpu_custom_call" | custom-call | flops 1 | bytes 1 | tf_op jit(solution)/shard_map/attend/pallas_call | solution.py:240
  82.9 3.2 %step.15 = (bf16[384,640]{1,0:T(8,128)(2,1)S(1)}, bf16[384,640]{1,0:T(8,128)(2,1)S(1)}, bf16[384,512]{1,0:T(8,128)(2,1)S(1)}, bf16[384,512]{1,0:T(8,128)(2,1)S(1...) custom-call(bf16[768,640]{1,0:T(8,128)(2,1)S(1)} %bitcast.4, bf16[768,640]{1,0:T(8,128)(2,1)S(1)} %bitcast.8, ...), custom_call_target="tpu_custom_call" | custom-call | flops 1 | bytes 1 | tf_op jit(solution)/shard_map/step/pallas_call | solution.py:400
  86.8 1.9 %collective-permute-done.12.refs_3_.refs_7_ = bf16[384,512]{1,0:T(8,128)(2,1)S(1)} collective-permute-done((bf16[384,512]{1,0:T(8,128)(2,1)S(1)}, bf16[384,512]{1,0:T(8,128)(2,1)S(1)}, u32[]{:S(2)}, u32[]{:S(2)}) %collective-permute-start.12) | collective-permute-done | bytes 393248 | tf_op jit(solution)/shard_map/ppermute | solution.py:264
  88.8 1.6 collective-permute-start.14
  92.1 4.3 %collective-permute-done.5.refs_4_.refs_0_ = bf16[768,640]{1,0:T(8,128)(2,1)S(1)} collective-permute-done((bf16[768,640]{1,0:T(8,128)(2,1)S(1)}, bf16[768,640]{1,0:T(8,128)(2,1)S(1)}, u32[]{:S(2)}, u32[]{:S(2)}) %collective-permute-start.5) | collective-permute-done | bytes 983072 | tf_op jit(solution)/shard_map/ppermute | solution.py:264
  96.4 1.7 %step.17 = (bf16[384,640]{1,0:T(8,128)(2,1)S(1)}, bf16[384,640]{1,0:T(8,128)(2,1)S(1)}) custom-call(bf16[768,640]{1,0:T(8,128)(2,1)S(1)} %bitcast.5, bf16[768,640]{1,0:T(8,128)(2,1)S(1)} %bitcast.10, bf16[640,1280]{1,0:T(8,128)(2,1)S(1)} %collective-permute-done.3.refs_3_.refs_2_, bf16[192,1152]{1,0:T(8,128)(2,1)S(1)} %step.16.refs_3_, ...), custom_call_target="tpu_custom_call" | custom-call | flops 1 | bytes 1 | tf_op jit(solution)/shard_map/step/pallas_call | solution.py:400
  98.2 2.9 %collective-permute-done.14.refs_8_ = bf16[192,1152]{1,0:T(8,128)(2,1)S(1)} collective-permute-done((bf16[192,1152]{1,0:T(8,128)(2,1)S(1)}, bf16[192,1152]{1,0:T(8,128)(2,1)S(1)}, u32[]{:S(2)}, u32[]{:S(2)}) %collective-permute-start.14) | collective-permute-done | bytes 442400 | tf_op jit(solution)/shard_map/ppermute | solution.py:264
  101.1 6.3 %collective-permute-done.9.refs_3_.refs_4_ = bf16[640,1280]{1,0:T(8,128)(2,1)S(1)} collective-permute-done((bf16[640,1280]{1,0:T(8,128)(2,1)S(1)}, bf16[640,1280]{1,0:T(8,128)(2,1)S(1)}, u32[]{:S(2)}, u32[]{:S(2)}) %collective-permute-start.9) | collective-permute-done | bytes 1638432 | tf_op jit(solution)/shard_map/ppermute | solution.py:421
  107.3 2.3 %step.18 = (bf16[384,640]{1,0:T(8,128)(2,1)S(1)}, bf16[384,640]{1,0:T(8,128)(2,1)S(1)}, bf16[192,640]{1,0:T(8,128)(2,1)S(1)}, bf16[192,512]{1,0:T(8,128)(2,1)S(1)}) custom-call(bf16[768,640]{1,0:T(8,128)(2,1)S(1)} %bitcast.6, bf16[768,640]{1,0:T(8,128)(2,1)S(1)} %bitcast.11, bf16[640,1280]{1,0:T(8,128)(2,1)S(1)} %collective-permute-done.7.refs_2_.refs_3_, ...), custom_call_target="tpu_custom_call" | custom-call | flops 1 | bytes 1 | tf_op jit(solution)/shard_map/step/pallas_call | solution.py:400
  111.8 1.6 collective-permute-start.18
  113.4 2.3 %collective-permute-done.6.refs_1_ = bf16[768,640]{1,0:T(8,128)(2,1)S(1)} collective-permute-done((bf16[768,640]{1,0:T(8,128)(2,1)S(1)}, bf16[768,640]{1,0:T(8,128)(2,1)S(1)}, u32[]{:S(2)}, u32[]{:S(2)}) %collective-permute-start.6) | collective-permute-done | bytes 983072 | tf_op jit(solution)/shard_map/ppermute | solution.py:264
  115.7 3.6 %step.20 = (bf16[384,640]{1,0:T(8,128)(2,1)S(1)}, bf16[384,640]{1,0:T(8,128)(2,1)S(1)}, bf16[384,640]{1,0:T(8,128)(2,1)S(1)}, bf16[384,640]{1,0:T(8,128)(2,1)S(1)}) custom-call(bf16[768,640]{1,0:T(8,128)(2,1)S(1)} %collective-permute-done.5.refs_4_.refs_0_, bf16[768,640]{1,0:T(8,128)(2,1)S(1)} %collective-permute-done.6.refs_1_, ...), custom_call_target="tpu_custom_call" | custom-call | flops 1 | bytes 1 | tf_op jit(solution)/shard_map/step/pallas_call | solution.py:400
  121.3 4.9 %collective-permute-done.18.refs_8_ = bf16[192,1408]{1,0:T(8,128)(2,1)S(1)} collective-permute-done((bf16[192,1408]{1,0:T(8,128)(2,1)S(1)}, bf16[192,1408]{1,0:T(8,128)(2,1)S(1)}, u32[]{:S(2)}, u32[]{:S(2)}) %collective-permute-start.18) | collective-permute-done | bytes 540704 | tf_op jit(solution)/shard_map/ppermute | solution.py:264
  126.5 1.6 collective-permute-start.19
  128.0 5.7 %collective-permute-done.19.refs_4_ = bf16[192,640]{1,0:T(8,128)(2,1)S(1)} collective-permute-done((bf16[192,640]{1,0:T(8,128)(2,1)S(1)}, bf16[192,640]{1,0:T(8,128)(2,1)S(1)}, u32[]{:S(2)}, u32[]{:S(2)}) %collective-permute-start.19) | collective-permute-done | bytes 245792 | tf_op jit(solution)/shard_map/ppermute | solution.py:264
  133.8 1.6 collective-permute-start.21
  136.9 5.1 %collective-permute-done.8.refs_3_ = bf16[640,1280]{1,0:T(8,128)(2,1)S(1)} collective-permute-done((bf16[640,1280]{1,0:T(8,128)(2,1)S(1)}, bf16[640,1280]{1,0:T(8,128)(2,1)S(1)}, u32[]{:S(2)}, u32[]{:S(2)}) %collective-permute-start.8) | collective-permute-done | bytes 1638432 | tf_op jit(solution)/shard_map/ppermute | solution.py:495
  142.0 1.7 %step.23 = (bf16[384,640]{1,0:T(8,128)(2,1)S(1)}, bf16[384,640]{1,0:T(8,128)(2,1)S(1)}) custom-call(bf16[768,640]{1,0:T(8,128)(2,1)S(1)} %collective-permute-done.5.refs_4_.refs_0_, bf16[768,640]{1,0:T(8,128)(2,1)S(1)} %collective-permute-done.6.refs_1_, bf16[640,1280]{1,0:T(8,128)(2,1)S(1)} %collective-permute-done.4.refs_4_.refs_2_, ...), custom_call_target="tpu_custom_call" | custom-call | flops 1 | bytes 1 | tf_op jit(solution)/shard_map/step/pallas_call | solution.py:400
  143.9 1.7 %step.25 = (bf16[384,640]{1,0:T(8,128)(2,1)S(1)}, bf16[384,640]{1,0:T(8,128)(2,1)S(1)}) custom-call(bf16[768,640]{1,0:T(8,128)(2,1)S(1)} %bitcast.7, bf16[768,640]{1,0:T(8,128)(2,1)S(1)} %bitcast.12, bf16[640,1280]{1,0:T(8,128)(2,1)S(1)} %collective-permute-done.4.refs_4_.refs_2_, bf16[640,1280]{1,0:T(8,128)(2,1)S(1)} %collective-permute-done.8.refs_3_, ...), custom_call_target="tpu_custom_call" | custom-call | flops 1 | bytes 1 | tf_op jit(solution)/shard_map/step/pallas_call | solution.py:400
  147.8 1.6 collective-permute-start.23
  150.0 4.1 %collective-permute-done.25.refs_4_.refs_6_ = bf16[192,640]{1,0:T(8,128)(2,1)S(1)} collective-permute-done((bf16[192,640]{1,0:T(8,128)(2,1)S(1)}, bf16[192,640]{1,0:T(8,128)(2,1)S(1)}, u32[]{:S(2)}, u32[]{:S(2)}) %collective-permute-start.25) | collective-permute-done | bytes 245792 | tf_op jit(solution)/shard_map/ppermute | solution.py:264
  154.2 2.6 %collective-permute-done.23.refs_2_ = bf16[192,640]{1,0:T(8,128)(2,1)S(1)} collective-permute-done((bf16[192,640]{1,0:T(8,128)(2,1)S(1)}, bf16[192,640]{1,0:T(8,128)(2,1)S(1)}, u32[]{:S(2)}, u32[]{:S(2)}) %collective-permute-start.23) | collective-permute-done | bytes 245792 | tf_op jit(solution)/shard_map/ppermute | solution.py:264
  158.6 2.2 %collective-permute-done.27.refs_2_ = bf16[192,640]{1,0:T(8,128)(2,1)S(1)} collective-permute-done((bf16[192,640]{1,0:T(8,128)(2,1)S(1)}, bf16[192,640]{1,0:T(8,128)(2,1)S(1)}, u32[]{:S(2)}, u32[]{:S(2)}) %collective-permute-start.27) | collective-permute-done | bytes 245792 | tf_op jit(solution)/shard_map/ppermute | solution.py:264
  160.9 2.2 %collective-permute-done.26.refs_0_ = bf16[192,640]{1,0:T(8,128)(2,1)S(1)} collective-permute-done((bf16[192,640]{1,0:T(8,128)(2,1)S(1)}, bf16[192,640]{1,0:T(8,128)(2,1)S(1)}, u32[]{:S(2)}, u32[]{:S(2)}) %collective-permute-start.26) | collective-permute-done | bytes 245792 | tf_op jit(solution)/shard_map/ppermute | solution.py:264
  (57 shorter events, 18.6 us)
Async XLA Ops:
  0.0 5.4 %copy-start.5 = (s32[24]{0:T(128)S(1)}, s32[24]{0:T(128)}, u32[]{:S(2)}) copy-start(s32[24]{0:T(128)} %refs_2_.2) | copy-start | bytes 292
  0.0 5.4 %copy-start.1 = (bf16[768,256]{1,0:T(8,128)(2,1)S(1)}, bf16[768,256]{1,0:T(8,128)(2,1)}, u32[]{:S(2)}) copy-start(bf16[768,256]{1,0:T(8,128)(2,1)} %keys_hbm.3) | copy-start | bytes 1179652
  0.0 5.4 %copy-start.2 = (bf16[768,256]{1,0:T(8,128)(2,1)S(1)}, bf16[768,256]{1,0:T(8,128)(2,1)}, u32[]{:S(2)}) copy-start(bf16[768,256]{1,0:T(8,128)(2,1)} %values_hbm.3) | copy-start | bytes 1179652
  1.5 61.2 %collective-permute-start.3 = (bf16[640,1280]{1,0:T(8,128)(2,1)S(1)}, bf16[640,1280]{1,0:T(8,128)(2,1)S(1)}, u32[]{:S(2)}, u32[]{:S(2)}) collective-permute-start(bf16[640,1280]{1,0:T(8,128)(2,1)S(1)} %cut.1), channel_id=1, source_target_pairs={{0,4},{4,0},{8,12},{12,8},{1,5},{5,1},{9,13},{13,9},{2,6},{6,2},{1... | collective-permute-start | bytes 4915208 | tf_op jit(solution)/shard_map/ppermute | solution.py:417
  4.6 58.8 %collective-permute-start.4 = (bf16[640,1280]{1,0:T(8,128)(2,1)S(1)}, bf16[640,1280]{1,0:T(8,128)(2,1)S(1)}, u32[]{:S(2)}, u32[]{:S(2)}) collective-permute-start(bf16[640,1280]{1,0:T(8,128)(2,1)S(1)} %cut.1), channel_id=1, source_target_pairs={{4,8},{8,4},{5,9},{9,5},{6,10},{10,6},{7,11},{11,7},{20,24},{24,20... | collective-permute-start | bytes 4915208 | tf_op jit(solution)/shard_map/ppermute | solution.py:418
  7.3 42.5 %collective-permute-start = (bf16[4,128,256]{2,1,0:T(8,128)(2,1)S(1)}, bf16[4,128,256]{2,1,0:T(8,128)(2,1)S(1)}, u32[]{:S(2)}, u32[]{:S(2)}) collective-permute-start(bf16[4,128,256]{2,1,0:T(8,128)(2,1)S(1)} %get-tuple-element.36), channel_id=1, source_target_pairs={{0,4},{4,0},{8,12},{12,8},{1,5},{5,1},{9,13},{13,9},{2,6},{6,2},{1... | collective-permute-start | bytes 786440 | tf_op jit(solution)/shard_map/ppermute | solution.py:264
  11.6 51.1 %collective-permute-start.1 = (bf16[4,128,256]{2,1,0:T(8,128)(2,1)S(1)}, bf16[4,128,256]{2,1,0:T(8,128)(2,1)S(1)}, u32[]{:S(2)}, u32[]{:S(2)}) collective-permute-start(bf16[4,128,256]{2,1,0:T(8,128)(2,1)S(1)} %get-tuple-element.36), channel_id=1, source_target_pairs={{0,8},{4,12},{8,0},{12,4},{1,9},{5,13},{9,1},{13,5},{2,10},{6,14},... | collective-permute-start | bytes 786440 | tf_op jit(solution)/shard_map/ppermute | solution.py:264
  11.6 51.1 %collective-permute-start.2 = (bf16[4,128,256]{2,1,0:T(8,128)(2,1)S(1)}, bf16[4,128,256]{2,1,0:T(8,128)(2,1)S(1)}, u32[]{:S(2)}, u32[]{:S(2)}) collective-permute-start(bf16[4,128,256]{2,1,0:T(8,128)(2,1)S(1)} %get-tuple-element.36), channel_id=1, source_target_pairs={{0,12},{4,8},{8,4},{12,0},{1,13},{5,9},{9,5},{13,1},{2,14},{6,10},... | collective-permute-start | bytes 786440 | tf_op jit(solution)/shard_map/ppermute | solution.py:264
  62.7 28.2 %collective-permute-start.7 = (bf16[640,1280]{1,0:T(8,128)(2,1)S(1)}, bf16[640,1280]{1,0:T(8,128)(2,1)S(1)}, u32[]{:S(2)}, u32[]{:S(2)}) collective-permute-start(bf16[640,1280]{1,0:T(8,128)(2,1)S(1)} %collective-permute-done.3.refs_3_.refs_2_), channel_id=1, source_target_pairs={{4,8},{8,4},{5,9},{9,5},{6,10},{10,6},{7,11},{11,7},{20,24},{24,20... | collective-permute-start | bytes 4915208 | tf_op jit(solution)/shard_map/ppermute | solution.py:422
  63.4 43.9 %collective-permute-start.9 = (bf16[640,1280]{1,0:T(8,128)(2,1)S(1)}, bf16[640,1280]{1,0:T(8,128)(2,1)S(1)}, u32[]{:S(2)}, u32[]{:S(2)}) collective-permute-start(bf16[640,1280]{1,0:T(8,128)(2,1)S(1)} %collective-permute-done.4.refs_4_.refs_2_), channel_id=1, source_target_pairs={{4,0},{8,12},{5,1},{9,13},{6,2},{10,14},{7,3},{11,15},{20,16},{24,... | collective-permute-start | bytes 4915208 | tf_op jit(solution)/shard_map/ppermute | solution.py:421
  73.1 9.9 %copy-start = (bf16[1280,1280]{1,0:T(8,128)(2,1)S(1)}, bf16[1280,1280]{1,0:T(8,128)(2,1)}, u32[]{:S(2)}) copy-start(bf16[1280,1280]{1,0:T(8,128)(2,1)} %refs_2_.3) | copy-start | bytes 9830404
  73.1 23.3 %collective-permute-start.5 = (bf16[768,640]{1,0:T(8,128)(2,1)S(1)}, bf16[768,640]{1,0:T(8,128)(2,1)S(1)}, u32[]{:S(2)}, u32[]{:S(2)}) collective-permute-start(bf16[768,640]{1,0:T(8,128)(2,1)S(1)} %bitcast.3), channel_id=1, source_target_pairs={{0,16},{16,0},{1,17},{17,1},{2,18},{18,2},{3,19},{19,3},{4,20},{20... | collective-permute-start | bytes 2949128 | tf_op jit(solution)/shard_map/ppermute | solution.py:264
  86.2 2.5 %collective-permute-start.11 = (bf16[384,640]{1,0:T(8,128)(2,1)S(1)}, bf16[384,640]{1,0:T(8,128)(2,1)S(1)}, u32[]{:S(2)}, u32[]{:S(2)}) collective-permute-start(bf16[384,640]{1,0:T(8,128)(2,1)S(1)} %get-tuple-element.42), channel_id=1, source_target_pairs={{0,1},{1,0},{2,3},{3,2},{4,5},{5,4},{6,7},{7,6},{8,9},{9,8},{10,11... | collective-permute-start | bytes 1474568 | tf_op jit(solution)/shard_map/ppermute | solution.py:264
  86.3 2.4 %collective-permute-start.12 = (bf16[384,512]{1,0:T(8,128)(2,1)S(1)}, bf16[384,512]{1,0:T(8,128)(2,1)S(1)}, u32[]{:S(2)}, u32[]{:S(2)}) collective-permute-start(bf16[384,512]{1,0:T(8,128)(2,1)S(1)} %get-tuple-element.44), channel_id=1, source_target_pairs={{0,1},{1,0},{2,3},{3,2},{4,5},{5,4},{6,7},{7,6},{8,9},{9,8},{10,11... | collective-permute-start | bytes 1179656 | tf_op jit(solution)/shard_map/ppermute | solution.py:264
  88.8 12.3 %collective-permute-start.14 = (bf16[192,1152]{1,0:T(8,128)(2,1)S(1)}, bf16[192,1152]{1,0:T(8,128)(2,1)S(1)}, u32[]{:S(2)}, u32[]{:S(2)}) collective-permute-start(bf16[192,1152]{1,0:T(8,128)(2,1)S(1)} %step.16.refs_3_), channel_id=1, source_target_pairs={{0,2},{1,3},{2,0},{3,1},{4,6},{5,7},{6,4},{7,5},{8,10},{9,11},{10,... | collective-permute-start | bytes 1327112 | tf_op jit(solution)/shard_map/ppermute | solution.py:264
  90.3 25.3 %collective-permute-start.6 = (bf16[768,640]{1,0:T(8,128)(2,1)S(1)}, bf16[768,640]{1,0:T(8,128)(2,1)S(1)}, u32[]{:S(2)}, u32[]{:S(2)}) collective-permute-start(bf16[768,640]{1,0:T(8,128)(2,1)S(1)} %bitcast.9), channel_id=1, source_target_pairs={{0,16},{16,0},{1,17},{17,1},{2,18},{18,2},{3,19},{19,3},{4,20},{20... | collective-permute-start | bytes 2949128 | tf_op jit(solution)/shard_map/ppermute | solution.py:264
  90.8 51.2 %collective-permute-start.8 = (bf16[640,1280]{1,0:T(8,128)(2,1)S(1)}, bf16[640,1280]{1,0:T(8,128)(2,1)S(1)}, u32[]{:S(2)}, u32[]{:S(2)}) collective-permute-start(bf16[640,1280]{1,0:T(8,128)(2,1)S(1)} %collective-permute-done.7.refs_2_.refs_3_), channel_id=1, source_target_pairs={{4,0},{8,12},{5,1},{9,13},{6,2},{10,14},{7,3},{11,15},{20,16},{24,... | collective-permute-start | bytes 4915208 | tf_op jit(solution)/shard_map/ppermute | solution.py:495
  98.1 13.6 %collective-permute-start.13 = (bf16[384,640]{1,0:T(8,128)(2,1)S(1)}, bf16[384,640]{1,0:T(8,128)(2,1)S(1)}, u32[]{:S(2)}, u32[]{:S(2)}) collective-permute-start(bf16[384,640]{1,0:T(8,128)(2,1)S(1)} %get-tuple-element.46.refs_9_), channel_id=1, source_target_pairs={{0,1},{1,0},{2,3},{3,2},{4,5},{5,4},{6,7},{7,6},{8,9},{9,8},{10,11... | collective-permute-start | bytes 1474568 | tf_op jit(solution)/shard_map/ppermute | solution.py:264
  109.6 2.1 %collective-permute-start.15 = (bf16[384,640]{1,0:T(8,128)(2,1)S(1)}, bf16[384,640]{1,0:T(8,128)(2,1)S(1)}, u32[]{:S(2)}, u32[]{:S(2)}) collective-permute-start(bf16[384,640]{1,0:T(8,128)(2,1)S(1)} %get-tuple-element.48), channel_id=1, source_target_pairs={{0,1},{1,0},{2,3},{3,2},{4,5},{5,4},{6,7},{7,6},{8,9},{9,8},{10,11... | collective-permute-start | bytes 1474568 | tf_op jit(solution)/shard_map/ppermute | solution.py:264
  109.7 2.0 %collective-permute-start.10 = (bf16[384,128]{1,0:T(8,128)(2,1)S(1)}, bf16[384,128]{1,0:T(8,128)(2,1)S(1)}, u32[]{:S(2)}, u32[]{:S(2)}) collective-permute-start(bf16[384,128]{1,0:T(8,128)(2,1)S(1)} %get-tuple-element.40), channel_id=1, source_target_pairs={{0,1},{1,0},{2,3},{3,2},{4,5},{5,4},{6,7},{7,6},{8,9},{9,8},{10,11... | collective-permute-start | bytes 294920 | tf_op jit(solution)/shard_map/ppermute | solution.py:264
  111.8 14.4 %collective-permute-start.18 = (bf16[192,1408]{1,0:T(8,128)(2,1)S(1)}, bf16[192,1408]{1,0:T(8,128)(2,1)S(1)}, u32[]{:S(2)}, u32[]{:S(2)}) collective-permute-start(bf16[192,1408]{1,0:T(8,128)(2,1)S(1)} %step.19.refs_5_), channel_id=1, source_target_pairs={{0,2},{1,3},{2,0},{3,1},{4,6},{5,7},{6,4},{7,5},{8,10},{9,11},{10,... | collective-permute-start | bytes 1622024 | tf_op jit(solution)/shard_map/ppermute | solution.py:264
  119.3 1.9 %collective-permute-start.17 = (bf16[384,640]{1,0:T(8,128)(2,1)S(1)}, bf16[384,640]{1,0:T(8,128)(2,1)S(1)}, u32[]{:S(2)}, u32[]{:S(2)}) collective-permute-start(bf16[384,640]{1,0:T(8,128)(2,1)S(1)} %get-tuple-element.52), channel_id=1, source_target_pairs={{0,1},{1,0},{2,3},{3,2},{4,5},{5,4},{6,7},{7,6},{8,9},{9,8},{10,11... | collective-permute-start | bytes 1474568 | tf_op jit(solution)/shard_map/ppermute | solution.py:264
  119.4 8.6 %collective-permute-start.16 = (bf16[384,640]{1,0:T(8,128)(2,1)S(1)}, bf16[384,640]{1,0:T(8,128)(2,1)S(1)}, u32[]{:S(2)}, u32[]{:S(2)}) collective-permute-start(bf16[384,640]{1,0:T(8,128)(2,1)S(1)} %get-tuple-element.50), channel_id=1, source_target_pairs={{0,1},{1,0},{2,3},{3,2},{4,5},{5,4},{6,7},{7,6},{8,9},{9,8},{10,11... | collective-permute-start | bytes 1474568 | tf_op jit(solution)/shard_map/ppermute | solution.py:264
  126.5 7.2 %collective-permute-start.19 = (bf16[192,640]{1,0:T(8,128)(2,1)S(1)}, bf16[192,640]{1,0:T(8,128)(2,1)S(1)}, u32[]{:S(2)}, u32[]{:S(2)}) collective-permute-start(bf16[192,640]{1,0:T(8,128)(2,1)S(1)} %get-tuple-element.53), channel_id=1, source_target_pairs={{0,2},{1,3},{2,0},{3,1},{4,6},{5,7},{6,4},{7,5},{8,10},{9,11},{10,... | collective-permute-start | bytes 737288 | tf_op jit(solution)/shard_map/ppermute | solution.py:264
  133.8 10.0 %collective-permute-start.21 = (bf16[192,640]{1,0:T(8,128)(2,1)S(1)}, bf16[192,640]{1,0:T(8,128)(2,1)S(1)}, u32[]{:S(2)}, u32[]{:S(2)}) collective-permute-start(bf16[192,640]{1,0:T(8,128)(2,1)S(1)} %get-tuple-element.54.refs_4_), channel_id=1, source_target_pairs={{0,2},{1,3},{2,0},{3,1},{4,6},{5,7},{6,4},{7,5},{8,10},{9,11},{10,... | collective-permute-start | bytes 737288 | tf_op jit(solution)/shard_map/ppermute | solution.py:264
  135.4 8.4 %collective-permute-start.22 = (bf16[192,640]{1,0:T(8,128)(2,1)S(1)}, bf16[192,640]{1,0:T(8,128)(2,1)S(1)}, u32[]{:S(2)}, u32[]{:S(2)}) collective-permute-start(bf16[192,640]{1,0:T(8,128)(2,1)S(1)} %get-tuple-element.57), channel_id=1, source_target_pairs={{0,16},{16,0},{1,17},{17,1},{2,18},{18,2},{3,19},{19,3},{4,20},{20... | collective-permute-start | bytes 737288 | tf_op jit(solution)/shard_map/ppermute | solution.py:264
  143.7 4.0 %collective-permute-start.20 = (bf16[384,640]{1,0:T(8,128)(2,1)S(1)}, bf16[384,640]{1,0:T(8,128)(2,1)S(1)}, u32[]{:S(2)}, u32[]{:S(2)}) collective-permute-start(bf16[384,640]{1,0:T(8,128)(2,1)S(1)} %get-tuple-element.56.refs_3_), channel_id=1, source_target_pairs={{0,1},{1,0},{2,3},{3,2},{4,5},{5,4},{6,7},{7,6},{8,9},{9,8},{10,11... | collective-permute-start | bytes 1474568 | tf_op jit(solution)/shard_map/ppermute | solution.py:264
  145.7 3.7 %collective-permute-start.24 = (bf16[384,640]{1,0:T(8,128)(2,1)S(1)}, bf16[384,640]{1,0:T(8,128)(2,1)S(1)}, u32[]{:S(2)}, u32[]{:S(2)}) collective-permute-start(bf16[384,640]{1,0:T(8,128)(2,1)S(1)} %get-tuple-element.58.refs_2_), channel_id=1, source_target_pairs={{0,1},{1,0},{2,3},{3,2},{4,5},{5,4},{6,7},{7,6},{8,9},{9,8},{10,11... | collective-permute-start | bytes 1474568 | tf_op jit(solution)/shard_map/ppermute | solution.py:264
  146.2 7.9 %collective-permute-start.25 = (bf16[192,640]{1,0:T(8,128)(2,1)S(1)}, bf16[192,640]{1,0:T(8,128)(2,1)S(1)}, u32[]{:S(2)}, u32[]{:S(2)}) collective-permute-start(bf16[192,640]{1,0:T(8,128)(2,1)S(1)} %step.24.refs_4_), channel_id=1, source_target_pairs={{0,16},{16,0},{1,17},{17,1},{2,18},{18,2},{3,19},{19,3},{4,20},{20... | collective-permute-start | bytes 737288 | tf_op jit(solution)/shard_map/ppermute | solution.py:264
  147.8 8.9 %collective-permute-start.23 = (bf16[192,640]{1,0:T(8,128)(2,1)S(1)}, bf16[192,640]{1,0:T(8,128)(2,1)S(1)}, u32[]{:S(2)}, u32[]{:S(2)}) collective-permute-start(bf16[192,640]{1,0:T(8,128)(2,1)S(1)} %step.26.refs_2_), channel_id=1, source_target_pairs={{0,2},{1,3},{2,0},{3,1},{4,6},{5,7},{6,4},{7,5},{8,10},{9,11},{10,... | collective-permute-start | bytes 737288 | tf_op jit(solution)/shard_map/ppermute | solution.py:264
  149.4 11.4 %collective-permute-start.27 = (bf16[192,640]{1,0:T(8,128)(2,1)S(1)}, bf16[192,640]{1,0:T(8,128)(2,1)S(1)}, u32[]{:S(2)}, u32[]{:S(2)}) collective-permute-start(bf16[192,640]{1,0:T(8,128)(2,1)S(1)} %step.27.refs_3_), channel_id=1, source_target_pairs={{0,2},{1,3},{2,0},{3,1},{4,6},{5,7},{6,4},{7,5},{8,10},{9,11},{10,... | collective-permute-start | bytes 737288 | tf_op jit(solution)/shard_map/ppermute | solution.py:264
  156.8 6.3 %collective-permute-start.26 = (bf16[192,640]{1,0:T(8,128)(2,1)S(1)}, bf16[192,640]{1,0:T(8,128)(2,1)S(1)}, u32[]{:S(2)}, u32[]{:S(2)}) collective-permute-start(bf16[192,640]{1,0:T(8,128)(2,1)S(1)} %step.28.refs_3_), channel_id=1, source_target_pairs={{0,16},{16,0},{1,17},{17,1},{2,18},{18,2},{3,19},{19,3},{4,20},{20... | collective-permute-start | bytes 737288 | tf_op jit(solution)/shard_map/ppermute | solution.py:264
  (2 other events, 10.8 us)

commit v2 on v1

--- a/solution.py
+++ b/solution.py
@@ -113,8 +113,10 @@
     )(slot_nodes, ancestors.T, depth, keys, values)
 
 
-def attend_body(kv, parts, count, table, query_hbm, keys_hbm, values_hbm, *refs):
-    got = refs[:count]
+def attend_body(kv, parts, counts, table, query_hbm, keys_hbm, values_hbm, *refs):
+    refs = list(refs)
+    got = [[refs.pop(0) for _ in range(count)] for count in counts]
+    middle = is_middle(lax.axis_index("node"))
     out, query, keys, values, above_keys, above_values, all_keys, all_values, sem = refs[-9:]
     nodes = query.shape[0] // NODE_TOK
     group = query.shape[1] // HEAD
@@ -130,19 +132,21 @@
     for copy in copies:
         copy.start()
     for step in range(CHAIN):
-        each = got[0].shape[0]
-        for order, array in enumerate(got):
+        each = got[0][0].shape[0]
+        for order, choice in enumerate(got):
             entry = table[2 + step] - order * each
             inside = jnp.clip(entry, 0, each - 1 - EXPORTS)
-            blocks = (
-                (array.at[inside, :, lanes], above_keys.at[step]),
-                (array.at[inside + EXPORTS, :, lanes], above_values.at[step]),
-            )
-            for part, (source, target) in enumerate(blocks):
-                copy = pltpu.make_async_copy(source, target, sem.at[3 + 2 * step + part])
-                pl.when((entry >= 0) & (entry < each))(copy.start)
-                if order == 0:
-                    copies.append(copy)
+            here = (entry >= 0) & (entry < each)
+            for array, pick in zip(choice, (middle, jnp.logical_not(middle))):
+                blocks = (
+                    (array.at[inside, :, lanes], above_keys.at[step]),
+                    (array.at[inside + EXPORTS, :, lanes], above_values.at[step]),
+                )
+                for part, (source, target) in enumerate(blocks):
+                    copy = pltpu.make_async_copy(source, target, sem.at[3 + 2 * step + part])
+                    pl.when(here & pick if len(choice) == 2 else here)(copy.start)
+                    if order == 0:
+                        copies.append(copy)
     ones = jnp.ones((NODE_TOK, HEAD), all_values.dtype)
     nothing = jnp.zeros((NODE_TOK, 2 * HEAD), all_values.dtype)
     query_index = lax.broadcasted_iota(jnp.int32, (NODE_TOK, NODE_TOK), 0)
@@ -238,11 +242,11 @@
     side = 2 if rows % (2 * NODE_TOK) == 0 else 1
     hbm = pl.BlockSpec(memory_space=pltpu.HBM)
     return pl.pallas_call(
-        functools.partial(attend_body, kv, parts, len(got)),
+        functools.partial(attend_body, kv, parts, [len(choice) for choice in got]),
         out_shape=jax.ShapeDtypeStruct((parts, rows // parts, width), queries.dtype),
         in_specs=[pl.BlockSpec(memory_space=pltpu.SMEM)]
         + [hbm] * 3
-        + [pl.BlockSpec(memory_space=pl.ANY)] * (len(got) + len(after)),
+        + [pl.BlockSpec(memory_space=pl.ANY)] * (sum(len(x) for x in got) + len(after)),
         scratch_shapes=[
             pltpu.VMEM((rows, width), queries.dtype),
             pltpu.VMEM((rows, HEAD), keys.dtype),
@@ -256,7 +260,7 @@
         compiler_params=pltpu.CompilerParams(vmem_limit_bytes=ATTEND_LIMIT),
         cost_estimate=LIGHT,
         name="attend",
-    )(table, *[in_hbm(x) for x in (queries, keys, values)], *got, *after)
+    )(table, *[in_hbm(x) for x in (queries, keys, values)], *[x for choice in got for x in choice], *after)
 
 
 def swap(array, axis, distance):
@@ -574,6 +578,15 @@
     return lax.psum_scatter(terms, "tensor", scatter_dimension=0, tiled=True)
 
 
+def spread(exported):
+    near = lax.ppermute(exported, "node", PAIRS)
+    across = lax.ppermute(exported, "node", MIDDLE)
+    near_across = lax.ppermute(near, "node", MIDDLE)
+    across_out = lax.ppermute(across, "node", OUTWARD)
+    far_out = lax.ppermute(near_across, "node", OUTWARD)
+    return [(near,), (near_across, across_out), (across, far_out)]
+
+
 def local(queries, keys, values, out_weight, slot_nodes, ancestors, depth):
     parts = lax.axis_size("tensor")
     devices = lax.axis_size("node")
@@ -583,9 +596,9 @@
     relative = devices == 4
     exported, table = prepare(slot_nodes, ancestors, depth, keys, values, relative)
     if relative:
-        got = [swap(exported, "node", distance) for distance in (1, 2, 3)]
+        got = spread(exported)
     else:
-        got = [lax.all_gather(exported, "node", axis=0, tiled=True)]
+        got = [(lax.all_gather(exported, "node", axis=0, tiled=True),)]
     if (
         devices == 4
         and parts == 4

time: 164 us -> 159 us (0.970)
  waiting for transfers between devices: 96 us -> 89.5 us
    ppermute x23 -> x20, waiting for transfers between devices: 84.6 us -> 36.3 us  [swap(): return lax.ppermute(array, axis, [(i, i ^ distance) for i in range(size)])]
    ppermute x0 -> x5, waiting for transfers between devices: none -> 47.7 us  [the longest x1 33.8 us: spread(): near = lax.ppermute(exported, 'node', PAIRS)]
    ppermute x0 -> x5, starting transfers between devices: none -> 8.28 us  [the longest x1 4.36 us: spread(): near = lax.ppermute(exported, 'node', PAIRS)]
    ppermute x23 -> x20, starting transfers between devices: 23.2 us -> 16.5 us  [swap(): return lax.ppermute(array, axis, [(i, i ^ distance) for i in range(size)])]
    ppermute x1, waiting for transfers between devices: 6.28 us -> 2.14 us  [relay(): across_out = lax.ppermute(across, 'node', OUTWARD)]
    ppermute x1, waiting for transfers between devices: 5.1 us -> 3.28 us  [project_split(): far_out = lax.ppermute(near_across, 'node', OUTWARD)]
  transfers between devices with their start and end apart: 28 -> 30, of which waited for: 16 -> 17; matrix products, arithmetic and copies ran while one was open for 0% -> 0% of each run, Pallas kernels for 21% -> 22%
where the time goes in v2:
time: 159 us
  waiting for transfers between devices  89.5 us (56%)
  Pallas kernels  37 us (23%)
  starting transfers between devices  31.9 us (20%)
    ppermute x20, waiting for transfers between devices, swap(): return lax.ppermute(array, axis, [(i, i ^ distance) for i in range(size)])  36.3 us
    ppermute x1, waiting for transfers between devices, spread(): near = lax.ppermute(exported, 'node', PAIRS)  33.8 us
    ppermute x20, starting transfers between devices, swap(): return lax.ppermute(array, axis, [(i, i ^ distance) for i in range(size)])  16.5 us
    pallas_call x2, Pallas kernels, attend(): pl.pallas_call(functools.partial(attend_body, kv, parts, [len(choice) for...  16.4 us
    pallas_call x15, Pallas kernels, step(): pl.pallas_call(functools.partial(step_body, plan), out_shape=[jax.ShapeDt...  15.3 us
    ppermute x1, waiting for transfers between devices, spread(): across_out = lax.ppermute(across, 'node', OUTWARD)  9 us
    ppermute x1, waiting for transfers between devices, spread(): far_out = lax.ppermute(near_across, 'node', OUTWARD)  4.98 us
    ppermute x1, starting transfers between devices, spread(): near = lax.ppermute(exported, 'node', PAIRS)  4.36 us
  transfers between devices with their start and end apart: 30, of which 17 were waited for; matrix products, arithmetic and copies ran while one was open for 0% of the time, Pallas kernels for 22%

profile of v2, /device:TPU:0, one launch (start us, length us, event | category | flops | bytes accessed | tf_op | source)
XLA Modules:
  0.0 158.9 jit_solution(4909084450826130717)
XLA Ops:
  1.5 3.1 %collective-permute-start.5 = (bf16[640,1280]{1,0:T(8,128)(2,1)S(1)}, bf16[640,1280]{1,0:T(8,128)(2,1)S(1)}, u32[]{:S(2)}, u32[]{:S(2)}) collective-permute-start(bf16[640,1280]{1,0:T(8,128)(2,1)S(1)} %cut.1), channel_id=1, source_target_pairs={{0,4},{4,0},{8,12},{12,8},{1,5},{5,1},{9,13},{13,9},{2,6},{6,2},{1... | collective-permute-start | bytes 4915208 | tf_op jit(solution)/shard_map/ppermute | solution.py:421
  5.4 1.8 %prepare.1 = (bf16[4,128,256]{2,1,0:T(8,128)(2,1)S(1)}, s32[8]{0:T(128)S(1)}) custom-call(s32[24]{0:T(128)S(1)} %copy-done.4, s32[7,24]{1,0:T(8,128)S(1)} %bitcast.13, s32[24]{0:T(128)S(1)} %copy-done.5, bf16[768,256]{1,0:T(8,128)(2,1)S(1)} %copy-done.1, bf16[768,256]{1,0:T(8,128)(2,1)S(1)} %copy-done.2), custom_call_target="tpu_custom_call" | custom-call | tf_op jit(solution)/shard_map/prepare/pallas_call | solution.py:93
  7.3 4.4 %collective-permute-start = (bf16[4,128,256]{2,1,0:T(8,128)(2,1)S(1)}, bf16[4,128,256]{2,1,0:T(8,128)(2,1)S(1)}, u32[]{:S(2)}, u32[]{:S(2)}) collective-permute-start(bf16[4,128,256]{2,1,0:T(8,128)(2,1)S(1)} %get-tuple-element.36), channel_id=1, source_target_pairs={{0,4},{4,0},{8,12},{12,8},{1,5},{5,1},{9,13},{13,9},{2,6},{6,2},{1... | collective-permute-start | bytes 786440 | tf_op jit(solution)/shard_map/ppermute | solution.py:582
  12.3 33.8 %collective-permute-done.refs_0_ = bf16[4,128,256]{2,1,0:T(8,128)(2,1)S(1)} collective-permute-done((bf16[4,128,256]{2,1,0:T(8,128)(2,1)S(1)}, bf16[4,128,256]{2,1,0:T(8,128)(2,1)S(1)}, u32[]{:S(2)}, u32[]{:S(2)}) %collective-permute-start) | collective-permute-done | bytes 262176 | tf_op jit(solution)/shard_map/ppermute | solution.py:582
  49.3 9.0 %collective-permute-done.3.refs_2_ = bf16[4,128,256]{2,1,0:T(8,128)(2,1)S(1)} collective-permute-done((bf16[4,128,256]{2,1,0:T(8,128)(2,1)S(1)}, bf16[4,128,256]{2,1,0:T(8,128)(2,1)S(1)}, u32[]{:S(2)}, u32[]{:S(2)}) %collective-permute-start.3) | collective-permute-done | bytes 262176 | tf_op jit(solution)/shard_map/ppermute | solution.py:585
  58.3 5.0 %collective-permute-done.4.refs_4_ = bf16[4,128,256]{2,1,0:T(8,128)(2,1)S(1)} collective-permute-done((bf16[4,128,256]{2,1,0:T(8,128)(2,1)S(1)}, bf16[4,128,256]{2,1,0:T(8,128)(2,1)S(1)}, u32[]{:S(2)}, u32[]{:S(2)}) %collective-permute-start.4) | collective-permute-done | bytes 262176 | tf_op jit(solution)/shard_map/ppermute | solution.py:586
  65.4 8.2 %attend.2.refs_5_ = bf16[4,192,640]{2,1,0:T(8,128)(2,1)S(1)} custom-call(s32[8]{0:T(128)S(1)} %get-tuple-element.35.table, bf16[768,1280]{1,0:T(8,128)(2,1)} %query_hbm.3, bf16[768,256]{1,0:T(8,128)(2,1)} %keys_hbm.3, bf16[768,256]{1,0:T(8,128)(2,1)} %values_hbm.3, bf16[4,128,256]{2,1,0:T(8,128)(2,1)S(1)} %collective-permute-done.refs_0_, ...), custom_call_target="tpu_custom_call" | custom-call | flops 1 | bytes 1 | tf_op jit(solution)/shard_map/attend/pallas_call | solution.py:244
  73.6 1.6 collective-permute-start.7
  75.2 8.2 %attend.3 = bf16[4,192,640]{2,1,0:T(8,128)(2,1)S(1)} custom-call(s32[8]{0:T(128)S(1)} %get-tuple-element.35.table, bf16[768,1280]{1,0:T(8,128)(2,1)} %query_hbm.3, bf16[768,256]{1,0:T(8,128)(2,1)} %keys_hbm.3, bf16[768,256]{1,0:T(8,128)(2,1)} %values_hbm.3, bf16[4,128,256]{2,1,0:T(8,128)(2,1)S(1)} %collective-permute-done.refs_0_, ...), custom_call_target="tpu_custom_call" | custom-call | flops 1 | bytes 1 | tf_op jit(solution)/shard_map/attend/pallas_call | solution.py:244
  83.4 3.2 %step.15 = (bf16[384,640]{1,0:T(8,128)(2,1)S(1)}, bf16[384,640]{1,0:T(8,128)(2,1)S(1)}, bf16[384,512]{1,0:T(8,128)(2,1)S(1)}, bf16[384,512]{1,0:T(8,128)(2,1)S(1...) custom-call(bf16[768,640]{1,0:T(8,128)(2,1)S(1)} %bitcast.4, bf16[768,640]{1,0:T(8,128)(2,1)S(1)} %bitcast.8, ...), custom_call_target="tpu_custom_call" | custom-call | flops 1 | bytes 1 | tf_op jit(solution)/shard_map/step/pallas_call | solution.py:404
  87.2 1.9 %collective-permute-done.14.refs_3_.refs_7_ = bf16[384,512]{1,0:T(8,128)(2,1)S(1)} collective-permute-done((bf16[384,512]{1,0:T(8,128)(2,1)S(1)}, bf16[384,512]{1,0:T(8,128)(2,1)S(1)}, u32[]{:S(2)}, u32[]{:S(2)}) %collective-permute-start.14) | collective-permute-done | bytes 393248 | tf_op jit(solution)/shard_map/ppermute | solution.py:268
  89.3 1.6 collective-permute-start.16
  92.6 4.9 %collective-permute-done.7.refs_4_.refs_0_ = bf16[768,640]{1,0:T(8,128)(2,1)S(1)} collective-permute-done((bf16[768,640]{1,0:T(8,128)(2,1)S(1)}, bf16[768,640]{1,0:T(8,128)(2,1)S(1)}, u32[]{:S(2)}, u32[]{:S(2)}) %collective-permute-start.7) | collective-permute-done | bytes 983072 | tf_op jit(solution)/shard_map/ppermute | solution.py:268
  97.5 1.7 %step.17 = (bf16[384,640]{1,0:T(8,128)(2,1)S(1)}, bf16[384,640]{1,0:T(8,128)(2,1)S(1)}) custom-call(bf16[768,640]{1,0:T(8,128)(2,1)S(1)} %bitcast.5, bf16[768,640]{1,0:T(8,128)(2,1)S(1)} %bitcast.10, bf16[640,1280]{1,0:T(8,128)(2,1)S(1)} %collective-permute-done.5.refs_5_.refs_2_, bf16[192,1152]{1,0:T(8,128)(2,1)S(1)} %step.16.refs_3_, ...), custom_call_target="tpu_custom_call" | custom-call | flops 1 | bytes 1 | tf_op jit(solution)/shard_map/step/pallas_call | solution.py:404
  99.3 2.2 %collective-permute-done.16.refs_8_ = bf16[192,1152]{1,0:T(8,128)(2,1)S(1)} collective-permute-done((bf16[192,1152]{1,0:T(8,128)(2,1)S(1)}, bf16[192,1152]{1,0:T(8,128)(2,1)S(1)}, u32[]{:S(2)}, u32[]{:S(2)}) %collective-permute-start.16) | collective-permute-done | bytes 442400 | tf_op jit(solution)/shard_map/ppermute | solution.py:268
  101.5 2.1 %collective-permute-done.11.refs_3_.refs_4_ = bf16[640,1280]{1,0:T(8,128)(2,1)S(1)} collective-permute-done((bf16[640,1280]{1,0:T(8,128)(2,1)S(1)}, bf16[640,1280]{1,0:T(8,128)(2,1)S(1)}, u32[]{:S(2)}, u32[]{:S(2)}) %collective-permute-start.11) | collective-permute-done | bytes 1638432 | tf_op jit(solution)/shard_map/ppermute | solution.py:425
  103.7 2.3 %step.18 = (bf16[384,640]{1,0:T(8,128)(2,1)S(1)}, bf16[384,640]{1,0:T(8,128)(2,1)S(1)}, bf16[192,640]{1,0:T(8,128)(2,1)S(1)}, bf16[192,512]{1,0:T(8,128)(2,1)S(1)}) custom-call(bf16[768,640]{1,0:T(8,128)(2,1)S(1)} %bitcast.6, bf16[768,640]{1,0:T(8,128)(2,1)S(1)} %bitcast.11, bf16[640,1280]{1,0:T(8,128)(2,1)S(1)} %collective-permute-done.9.refs_2_.refs_3_, ...), custom_call_target="tpu_custom_call" | custom-call | flops 1 | bytes 1 | tf_op jit(solution)/shard_map/step/pallas_call | solution.py:404
  108.1 1.6 collective-permute-start.20
  109.7 6.8 %collective-permute-done.8.refs_1_ = bf16[768,640]{1,0:T(8,128)(2,1)S(1)} collective-permute-done((bf16[768,640]{1,0:T(8,128)(2,1)S(1)}, bf16[768,640]{1,0:T(8,128)(2,1)S(1)}, u32[]{:S(2)}, u32[]{:S(2)}) %collective-permute-start.8) | collective-permute-done | bytes 983072 | tf_op jit(solution)/shard_map/ppermute | solution.py:268
  116.5 3.6 %step.20 = (bf16[384,640]{1,0:T(8,128)(2,1)S(1)}, bf16[384,640]{1,0:T(8,128)(2,1)S(1)}, bf16[384,640]{1,0:T(8,128)(2,1)S(1)}, bf16[384,640]{1,0:T(8,128)(2,1)S(1)}) custom-call(bf16[768,640]{1,0:T(8,128)(2,1)S(1)} %collective-permute-done.7.refs_4_.refs_0_, bf16[768,640]{1,0:T(8,128)(2,1)S(1)} %collective-permute-done.8.refs_1_, ...), custom_call_target="tpu_custom_call" | custom-call | flops 1 | bytes 1 | tf_op jit(solution)/shard_map/step/pallas_call | solution.py:404
  122.8 1.6 collective-permute-start.21
  124.4 6.1 %collective-permute-done.21.refs_4_ = bf16[192,640]{1,0:T(8,128)(2,1)S(1)} collective-permute-done((bf16[192,640]{1,0:T(8,128)(2,1)S(1)}, bf16[192,640]{1,0:T(8,128)(2,1)S(1)}, u32[]{:S(2)}, u32[]{:S(2)}) %collective-permute-start.21) | collective-permute-done | bytes 245792 | tf_op jit(solution)/shard_map/ppermute | solution.py:268
  130.6 1.6 collective-permute-start.23
  132.1 1.5 collective-permute-start.24
  133.6 3.3 %collective-permute-done.10.refs_3_ = bf16[640,1280]{1,0:T(8,128)(2,1)S(1)} collective-permute-done((bf16[640,1280]{1,0:T(8,128)(2,1)S(1)}, bf16[640,1280]{1,0:T(8,128)(2,1)S(1)}, u32[]{:S(2)}, u32[]{:S(2)}) %collective-permute-start.10) | collective-permute-done | bytes 1638432 | tf_op jit(solution)/shard_map/ppermute | solution.py:499
  136.9 1.7 %step.23 = (bf16[384,640]{1,0:T(8,128)(2,1)S(1)}, bf16[384,640]{1,0:T(8,128)(2,1)S(1)}) custom-call(bf16[768,640]{1,0:T(8,128)(2,1)S(1)} %collective-permute-done.7.refs_4_.refs_0_, bf16[768,640]{1,0:T(8,128)(2,1)S(1)} %collective-permute-done.8.refs_1_, bf16[640,1280]{1,0:T(8,128)(2,1)S(1)} %collective-permute-done.6.refs_6_.refs_2_, ...), custom_call_target="tpu_custom_call" | custom-call | flops 1 | bytes 1 | tf_op jit(solution)/shard_map/step/pallas_call | solution.py:404
  138.8 1.7 %step.25 = (bf16[384,640]{1,0:T(8,128)(2,1)S(1)}, bf16[384,640]{1,0:T(8,128)(2,1)S(1)}) custom-call(bf16[768,640]{1,0:T(8,128)(2,1)S(1)} %bitcast.7, bf16[768,640]{1,0:T(8,128)(2,1)S(1)} %bitcast.12, bf16[640,1280]{1,0:T(8,128)(2,1)S(1)} %collective-permute-done.6.refs_6_.refs_2_, bf16[640,1280]{1,0:T(8,128)(2,1)S(1)} %collective-permute-done.10.refs_3_, ...), custom_call_target="tpu_custom_call" | custom-call | flops 1 | bytes 1 | tf_op jit(solution)/shard_map/step/pallas_call | solution.py:404
  142.7 1.6 collective-permute-start.25
  144.9 4.1 %collective-permute-done.27.refs_4_.refs_6_ = bf16[192,640]{1,0:T(8,128)(2,1)S(1)} collective-permute-done((bf16[192,640]{1,0:T(8,128)(2,1)S(1)}, bf16[192,640]{1,0:T(8,128)(2,1)S(1)}, u32[]{:S(2)}, u32[]{:S(2)}) %collective-permute-start.27) | collective-permute-done | bytes 245792 | tf_op jit(solution)/shard_map/ppermute | solution.py:268
  149.0 2.6 %collective-permute-done.25.refs_2_ = bf16[192,640]{1,0:T(8,128)(2,1)S(1)} collective-permute-done((bf16[192,640]{1,0:T(8,128)(2,1)S(1)}, bf16[192,640]{1,0:T(8,128)(2,1)S(1)}, u32[]{:S(2)}, u32[]{:S(2)}) %collective-permute-start.25) | collective-permute-done | bytes 245792 | tf_op jit(solution)/shard_map/ppermute | solution.py:268
  153.4 2.2 %collective-permute-done.29.refs_2_ = bf16[192,640]{1,0:T(8,128)(2,1)S(1)} collective-permute-done((bf16[192,640]{1,0:T(8,128)(2,1)S(1)}, bf16[192,640]{1,0:T(8,128)(2,1)S(1)}, u32[]{:S(2)}, u32[]{:S(2)}) %collective-permute-start.29) | collective-permute-done | bytes 245792 | tf_op jit(solution)/shard_map/ppermute | solution.py:268
  155.8 2.2 %collective-permute-done.28.refs_0_ = bf16[192,640]{1,0:T(8,128)(2,1)S(1)} collective-permute-done((bf16[192,640]{1,0:T(8,128)(2,1)S(1)}, bf16[192,640]{1,0:T(8,128)(2,1)S(1)}, u32[]{:S(2)}, u32[]{:S(2)}) %collective-permute-start.28) | collective-permute-done | bytes 245792 | tf_op jit(solution)/shard_map/ppermute | solution.py:268
  (61 shorter events, 21.4 us)
Async XLA Ops:
  0.0 5.4 %copy-start.2 = (bf16[768,256]{1,0:T(8,128)(2,1)S(1)}, bf16[768,256]{1,0:T(8,128)(2,1)}, u32[]{:S(2)}) copy-start(bf16[768,256]{1,0:T(8,128)(2,1)} %values_hbm.3) | copy-start | bytes 1179652
  1.5 61.8 %collective-permute-start.5 = (bf16[640,1280]{1,0:T(8,128)(2,1)S(1)}, bf16[640,1280]{1,0:T(8,128)(2,1)S(1)}, u32[]{:S(2)}, u32[]{:S(2)}) collective-permute-start(bf16[640,1280]{1,0:T(8,128)(2,1)S(1)} %cut.1), channel_id=1, source_target_pairs={{0,4},{4,0},{8,12},{12,8},{1,5},{5,1},{9,13},{13,9},{2,6},{6,2},{1... | collective-permute-start | bytes 4915208 | tf_op jit(solution)/shard_map/ppermute | solution.py:421
  4.6 59.5 %collective-permute-start.6 = (bf16[640,1280]{1,0:T(8,128)(2,1)S(1)}, bf16[640,1280]{1,0:T(8,128)(2,1)S(1)}, u32[]{:S(2)}, u32[]{:S(2)}) collective-permute-start(bf16[640,1280]{1,0:T(8,128)(2,1)S(1)} %cut.1), channel_id=1, source_target_pairs={{4,8},{8,4},{5,9},{9,5},{6,10},{10,6},{7,11},{11,7},{20,24},{24,20... | collective-permute-start | bytes 4915208 | tf_op jit(solution)/shard_map/ppermute | solution.py:422
  7.3 38.8 %collective-permute-start = (bf16[4,128,256]{2,1,0:T(8,128)(2,1)S(1)}, bf16[4,128,256]{2,1,0:T(8,128)(2,1)S(1)}, u32[]{:S(2)}, u32[]{:S(2)}) collective-permute-start(bf16[4,128,256]{2,1,0:T(8,128)(2,1)S(1)} %get-tuple-element.36), channel_id=1, source_target_pairs={{0,4},{4,0},{8,12},{12,8},{1,5},{5,1},{9,13},{13,9},{2,6},{6,2},{1... | collective-permute-start | bytes 786440 | tf_op jit(solution)/shard_map/ppermute | solution.py:582
  11.6 35.1 %collective-permute-start.2 = (bf16[4,128,256]{2,1,0:T(8,128)(2,1)S(1)}, bf16[4,128,256]{2,1,0:T(8,128)(2,1)S(1)}, u32[]{:S(2)}, u32[]{:S(2)}) collective-permute-start(bf16[4,128,256]{2,1,0:T(8,128)(2,1)S(1)} %get-tuple-element.36), channel_id=1, source_target_pairs={{4,8},{8,4},{5,9},{9,5},{6,10},{10,6},{7,11},{11,7},{20,24},{24,20... | collective-permute-start | bytes 786440 | tf_op jit(solution)/shard_map/ppermute | solution.py:583
  46.0 2.0 %collective-permute-start.1 = (bf16[4,128,256]{2,1,0:T(8,128)(2,1)S(1)}, bf16[4,128,256]{2,1,0:T(8,128)(2,1)S(1)}, u32[]{:S(2)}, u32[]{:S(2)}) collective-permute-start(bf16[4,128,256]{2,1,0:T(8,128)(2,1)S(1)} %collective-permute-done.refs_0_), channel_id=1, source_target_pairs={{4,8},{8,4},{5,9},{9,5},{6,10},{10,6},{7,11},{11,7},{20,24},{24,20... | collective-permute-start | bytes 786440 | tf_op jit(solution)/shard_map/ppermute | solution.py:584
  46.7 11.6 %collective-permute-start.3 = (bf16[4,128,256]{2,1,0:T(8,128)(2,1)S(1)}, bf16[4,128,256]{2,1,0:T(8,128)(2,1)S(1)}, u32[]{:S(2)}, u32[]{:S(2)}) collective-permute-start(bf16[4,128,256]{2,1,0:T(8,128)(2,1)S(1)} %collective-permute-done.2.refs_3_), channel_id=1, source_target_pairs={{4,0},{8,12},{5,1},{9,13},{6,2},{10,14},{7,3},{11,15},{20,16},{24,... | collective-permute-start | bytes 786440 | tf_op jit(solution)/shard_map/ppermute | solution.py:585
  48.0 15.3 %collective-permute-start.4 = (bf16[4,128,256]{2,1,0:T(8,128)(2,1)S(1)}, bf16[4,128,256]{2,1,0:T(8,128)(2,1)S(1)}, u32[]{:S(2)}, u32[]{:S(2)}) collective-permute-start(bf16[4,128,256]{2,1,0:T(8,128)(2,1)S(1)} %collective-permute-done.1.refs_1_), channel_id=1, source_target_pairs={{4,0},{8,12},{5,1},{9,13},{6,2},{10,14},{7,3},{11,15},{20,16},{24,... | collective-permute-start | bytes 786440 | tf_op jit(solution)/shard_map/ppermute | solution.py:586
  63.3 28.0 %collective-permute-start.9 = (bf16[640,1280]{1,0:T(8,128)(2,1)S(1)}, bf16[640,1280]{1,0:T(8,128)(2,1)S(1)}, u32[]{:S(2)}, u32[]{:S(2)}) collective-permute-start(bf16[640,1280]{1,0:T(8,128)(2,1)S(1)} %collective-permute-done.5.refs_5_.refs_2_), channel_id=1, source_target_pairs={{4,8},{8,4},{5,9},{9,5},{6,10},{10,6},{7,11},{11,7},{20,24},{24,20... | collective-permute-start | bytes 4915208 | tf_op jit(solution)/shard_map/ppermute | solution.py:426
  64.1 39.6 %collective-permute-start.11 = (bf16[640,1280]{1,0:T(8,128)(2,1)S(1)}, bf16[640,1280]{1,0:T(8,128)(2,1)S(1)}, u32[]{:S(2)}, u32[]{:S(2)}) collective-permute-start(bf16[640,1280]{1,0:T(8,128)(2,1)S(1)} %collective-permute-done.6.refs_6_.refs_2_), channel_id=1, source_target_pairs={{4,0},{8,12},{5,1},{9,13},{6,2},{10,14},{7,3},{11,15},{20,16},{24,... | collective-permute-start | bytes 4915208 | tf_op jit(solution)/shard_map/ppermute | solution.py:425
  73.6 9.8 %copy-start = (bf16[1280,1280]{1,0:T(8,128)(2,1)S(1)}, bf16[1280,1280]{1,0:T(8,128)(2,1)}, u32[]{:S(2)}) copy-start(bf16[1280,1280]{1,0:T(8,128)(2,1)} %refs_2_.3) | copy-start | bytes 9830404
  73.6 23.9 %collective-permute-start.7 = (bf16[768,640]{1,0:T(8,128)(2,1)S(1)}, bf16[768,640]{1,0:T(8,128)(2,1)S(1)}, u32[]{:S(2)}, u32[]{:S(2)}) collective-permute-start(bf16[768,640]{1,0:T(8,128)(2,1)S(1)} %bitcast.3), channel_id=1, source_target_pairs={{0,16},{16,0},{1,17},{17,1},{2,18},{18,2},{3,19},{19,3},{4,20},{20... | collective-permute-start | bytes 2949128 | tf_op jit(solution)/shard_map/ppermute | solution.py:268
  86.7 2.5 %collective-permute-start.13 = (bf16[384,640]{1,0:T(8,128)(2,1)S(1)}, bf16[384,640]{1,0:T(8,128)(2,1)S(1)}, u32[]{:S(2)}, u32[]{:S(2)}) collective-permute-start(bf16[384,640]{1,0:T(8,128)(2,1)S(1)} %get-tuple-element.42), channel_id=1, source_target_pairs={{0,1},{1,0},{2,3},{3,2},{4,5},{5,4},{6,7},{7,6},{8,9},{9,8},{10,11... | collective-permute-start | bytes 1474568 | tf_op jit(solution)/shard_map/ppermute | solution.py:268
  86.7 2.4 %collective-permute-start.14 = (bf16[384,512]{1,0:T(8,128)(2,1)S(1)}, bf16[384,512]{1,0:T(8,128)(2,1)S(1)}, u32[]{:S(2)}, u32[]{:S(2)}) collective-permute-start(bf16[384,512]{1,0:T(8,128)(2,1)S(1)} %get-tuple-element.44), channel_id=1, source_target_pairs={{0,1},{1,0},{2,3},{3,2},{4,5},{5,4},{6,7},{7,6},{8,9},{9,8},{10,11... | collective-permute-start | bytes 1179656 | tf_op jit(solution)/shard_map/ppermute | solution.py:268
  89.3 12.3 %collective-permute-start.16 = (bf16[192,1152]{1,0:T(8,128)(2,1)S(1)}, bf16[192,1152]{1,0:T(8,128)(2,1)S(1)}, u32[]{:S(2)}, u32[]{:S(2)}) collective-permute-start(bf16[192,1152]{1,0:T(8,128)(2,1)S(1)} %step.16.refs_3_), channel_id=1, source_target_pairs={{0,2},{1,3},{2,0},{3,1},{4,6},{5,7},{6,4},{7,5},{8,10},{9,11},{10,... | collective-permute-start | bytes 1327112 | tf_op jit(solution)/shard_map/ppermute | solution.py:268
  90.8 25.7 %collective-permute-start.8 = (bf16[768,640]{1,0:T(8,128)(2,1)S(1)}, bf16[768,640]{1,0:T(8,128)(2,1)S(1)}, u32[]{:S(2)}, u32[]{:S(2)}) collective-permute-start(bf16[768,640]{1,0:T(8,128)(2,1)S(1)} %bitcast.9), channel_id=1, source_target_pairs={{0,16},{16,0},{1,17},{17,1},{2,18},{18,2},{3,19},{19,3},{4,20},{20... | collective-permute-start | bytes 2949128 | tf_op jit(solution)/shard_map/ppermute | solution.py:268
  91.3 45.6 %collective-permute-start.10 = (bf16[640,1280]{1,0:T(8,128)(2,1)S(1)}, bf16[640,1280]{1,0:T(8,128)(2,1)S(1)}, u32[]{:S(2)}, u32[]{:S(2)}) collective-permute-start(bf16[640,1280]{1,0:T(8,128)(2,1)S(1)} %collective-permute-done.9.refs_2_.refs_3_), channel_id=1, source_target_pairs={{4,0},{8,12},{5,1},{9,13},{6,2},{10,14},{7,3},{11,15},{20,16},{24,... | collective-permute-start | bytes 4915208 | tf_op jit(solution)/shard_map/ppermute | solution.py:499
  99.3 8.7 %collective-permute-start.15 = (bf16[384,640]{1,0:T(8,128)(2,1)S(1)}, bf16[384,640]{1,0:T(8,128)(2,1)S(1)}, u32[]{:S(2)}, u32[]{:S(2)}) collective-permute-start(bf16[384,640]{1,0:T(8,128)(2,1)S(1)} %get-tuple-element.46.refs_9_), channel_id=1, source_target_pairs={{0,1},{1,0},{2,3},{3,2},{4,5},{5,4},{6,7},{7,6},{8,9},{9,8},{10,11... | collective-permute-start | bytes 1474568 | tf_op jit(solution)/shard_map/ppermute | solution.py:268
  105.9 2.1 %collective-permute-start.17 = (bf16[384,640]{1,0:T(8,128)(2,1)S(1)}, bf16[384,640]{1,0:T(8,128)(2,1)S(1)}, u32[]{:S(2)}, u32[]{:S(2)}) collective-permute-start(bf16[384,640]{1,0:T(8,128)(2,1)S(1)} %get-tuple-element.48), channel_id=1, source_target_pairs={{0,1},{1,0},{2,3},{3,2},{4,5},{5,4},{6,7},{7,6},{8,9},{9,8},{10,11... | collective-permute-start | bytes 1474568 | tf_op jit(solution)/shard_map/ppermute | solution.py:268
  106.0 2.0 %collective-permute-start.12 = (bf16[384,128]{1,0:T(8,128)(2,1)S(1)}, bf16[384,128]{1,0:T(8,128)(2,1)S(1)}, u32[]{:S(2)}, u32[]{:S(2)}) collective-permute-start(bf16[384,128]{1,0:T(8,128)(2,1)S(1)} %get-tuple-element.40), channel_id=1, source_target_pairs={{0,1},{1,0},{2,3},{3,2},{4,5},{5,4},{6,7},{7,6},{8,9},{9,8},{10,11... | collective-permute-start | bytes 294920 | tf_op jit(solution)/shard_map/ppermute | solution.py:268
  108.1 14.4 %collective-permute-start.20 = (bf16[192,1408]{1,0:T(8,128)(2,1)S(1)}, bf16[192,1408]{1,0:T(8,128)(2,1)S(1)}, u32[]{:S(2)}, u32[]{:S(2)}) collective-permute-start(bf16[192,1408]{1,0:T(8,128)(2,1)S(1)} %step.19.refs_5_), channel_id=1, source_target_pairs={{0,2},{1,3},{2,0},{3,1},{4,6},{5,7},{6,4},{7,5},{8,10},{9,11},{10,... | collective-permute-start | bytes 1622024 | tf_op jit(solution)/shard_map/ppermute | solution.py:268
  120.1 1.9 %collective-permute-start.19 = (bf16[384,640]{1,0:T(8,128)(2,1)S(1)}, bf16[384,640]{1,0:T(8,128)(2,1)S(1)}, u32[]{:S(2)}, u32[]{:S(2)}) collective-permute-start(bf16[384,640]{1,0:T(8,128)(2,1)S(1)} %get-tuple-element.52), channel_id=1, source_target_pairs={{0,1},{1,0},{2,3},{3,2},{4,5},{5,4},{6,7},{7,6},{8,9},{9,8},{10,11... | collective-permute-start | bytes 1474568 | tf_op jit(solution)/shard_map/ppermute | solution.py:268
  120.2 4.1 %collective-permute-start.18 = (bf16[384,640]{1,0:T(8,128)(2,1)S(1)}, bf16[384,640]{1,0:T(8,128)(2,1)S(1)}, u32[]{:S(2)}, u32[]{:S(2)}) collective-permute-start(bf16[384,640]{1,0:T(8,128)(2,1)S(1)} %get-tuple-element.50), channel_id=1, source_target_pairs={{0,1},{1,0},{2,3},{3,2},{4,5},{5,4},{6,7},{7,6},{8,9},{9,8},{10,11... | collective-permute-start | bytes 1474568 | tf_op jit(solution)/shard_map/ppermute | solution.py:268
  122.8 7.6 %collective-permute-start.21 = (bf16[192,640]{1,0:T(8,128)(2,1)S(1)}, bf16[192,640]{1,0:T(8,128)(2,1)S(1)}, u32[]{:S(2)}, u32[]{:S(2)}) collective-permute-start(bf16[192,640]{1,0:T(8,128)(2,1)S(1)} %get-tuple-element.53), channel_id=1, source_target_pairs={{0,2},{1,3},{2,0},{3,1},{4,6},{5,7},{6,4},{7,5},{8,10},{9,11},{10,... | collective-permute-start | bytes 737288 | tf_op jit(solution)/shard_map/ppermute | solution.py:268
  130.6 8.2 %collective-permute-start.23 = (bf16[192,640]{1,0:T(8,128)(2,1)S(1)}, bf16[192,640]{1,0:T(8,128)(2,1)S(1)}, u32[]{:S(2)}, u32[]{:S(2)}) collective-permute-start(bf16[192,640]{1,0:T(8,128)(2,1)S(1)} %get-tuple-element.54.refs_4_), channel_id=1, source_target_pairs={{0,2},{1,3},{2,0},{3,1},{4,6},{5,7},{6,4},{7,5},{8,10},{9,11},{10,... | collective-permute-start | bytes 737288 | tf_op jit(solution)/shard_map/ppermute | solution.py:268
  132.1 6.6 %collective-permute-start.24 = (bf16[192,640]{1,0:T(8,128)(2,1)S(1)}, bf16[192,640]{1,0:T(8,128)(2,1)S(1)}, u32[]{:S(2)}, u32[]{:S(2)}) collective-permute-start(bf16[192,640]{1,0:T(8,128)(2,1)S(1)} %get-tuple-element.57), channel_id=1, source_target_pairs={{0,16},{16,0},{1,17},{17,1},{2,18},{18,2},{3,19},{19,3},{4,20},{20... | collective-permute-start | bytes 737288 | tf_op jit(solution)/shard_map/ppermute | solution.py:268
  138.6 4.0 %collective-permute-start.22 = (bf16[384,640]{1,0:T(8,128)(2,1)S(1)}, bf16[384,640]{1,0:T(8,128)(2,1)S(1)}, u32[]{:S(2)}, u32[]{:S(2)}) collective-permute-start(bf16[384,640]{1,0:T(8,128)(2,1)S(1)} %get-tuple-element.56.refs_3_), channel_id=1, source_target_pairs={{0,1},{1,0},{2,3},{3,2},{4,5},{5,4},{6,7},{7,6},{8,9},{9,8},{10,11... | collective-permute-start | bytes 1474568 | tf_op jit(solution)/shard_map/ppermute | solution.py:268
  140.6 3.7 %collective-permute-start.26 = (bf16[384,640]{1,0:T(8,128)(2,1)S(1)}, bf16[384,640]{1,0:T(8,128)(2,1)S(1)}, u32[]{:S(2)}, u32[]{:S(2)}) collective-permute-start(bf16[384,640]{1,0:T(8,128)(2,1)S(1)} %get-tuple-element.58.refs_2_), channel_id=1, source_target_pairs={{0,1},{1,0},{2,3},{3,2},{4,5},{5,4},{6,7},{7,6},{8,9},{9,8},{10,11... | collective-permute-start | bytes 1474568 | tf_op jit(solution)/shard_map/ppermute | solution.py:268
  141.1 7.9 %collective-permute-start.27 = (bf16[192,640]{1,0:T(8,128)(2,1)S(1)}, bf16[192,640]{1,0:T(8,128)(2,1)S(1)}, u32[]{:S(2)}, u32[]{:S(2)}) collective-permute-start(bf16[192,640]{1,0:T(8,128)(2,1)S(1)} %step.24.refs_4_), channel_id=1, source_target_pairs={{0,16},{16,0},{1,17},{17,1},{2,18},{18,2},{3,19},{19,3},{4,20},{20... | collective-permute-start | bytes 737288 | tf_op jit(solution)/shard_map/ppermute | solution.py:268
  142.7 8.9 %collective-permute-start.25 = (bf16[192,640]{1,0:T(8,128)(2,1)S(1)}, bf16[192,640]{1,0:T(8,128)(2,1)S(1)}, u32[]{:S(2)}, u32[]{:S(2)}) collective-permute-start(bf16[192,640]{1,0:T(8,128)(2,1)S(1)} %step.26.refs_2_), channel_id=1, source_target_pairs={{0,2},{1,3},{2,0},{3,1},{4,6},{5,7},{6,4},{7,5},{8,10},{9,11},{10,... | collective-permute-start | bytes 737288 | tf_op jit(solution)/shard_map/ppermute | solution.py:268
  144.3 11.4 %collective-permute-start.29 = (bf16[192,640]{1,0:T(8,128)(2,1)S(1)}, bf16[192,640]{1,0:T(8,128)(2,1)S(1)}, u32[]{:S(2)}, u32[]{:S(2)}) collective-permute-start(bf16[192,640]{1,0:T(8,128)(2,1)S(1)} %step.27.refs_3_), channel_id=1, source_target_pairs={{0,2},{1,3},{2,0},{3,1},{4,6},{5,7},{6,4},{7,5},{8,10},{9,11},{10,... | collective-permute-start | bytes 737288 | tf_op jit(solution)/shard_map/ppermute | solution.py:268
  151.7 6.3 %collective-permute-start.28 = (bf16[192,640]{1,0:T(8,128)(2,1)S(1)}, bf16[192,640]{1,0:T(8,128)(2,1)S(1)}, u32[]{:S(2)}, u32[]{:S(2)}) collective-permute-start(bf16[192,640]{1,0:T(8,128)(2,1)S(1)} %step.28.refs_3_), channel_id=1, source_target_pairs={{0,16},{16,0},{1,17},{17,1},{2,18},{18,2},{3,19},{19,3},{4,20},{20... | collective-permute-start | bytes 737288 | tf_op jit(solution)/shard_map/ppermute | solution.py:268
  (4 other events, 21.6 us)

commit v3 on v2

--- a/solution.py
+++ b/solution.py
@@ -415,6 +415,7 @@
 PAIRS = [(0, 1), (1, 0), (2, 3), (3, 2)]
 MIDDLE = [(1, 2), (2, 1)]
 OUTWARD = [(1, 0), (2, 3)]
+ENDS = [(0, 3), (3, 0)]
 
 
 def relay(piece, got):
@@ -583,8 +584,8 @@
     across = lax.ppermute(exported, "node", MIDDLE)
     near_across = lax.ppermute(near, "node", MIDDLE)
     across_out = lax.ppermute(across, "node", OUTWARD)
-    far_out = lax.ppermute(near_across, "node", OUTWARD)
-    return [(near,), (near_across, across_out), (across, far_out)]
+    far = lax.ppermute(exported, "node", ENDS)
+    return [(near,), (near_across, across_out), (across, far)]
 
 
 def local(queries, keys, values, out_weight, slot_nodes, ancestors, depth):

time: 159 us -> 159 us (level)
  waiting for transfers between devices: 89.5 us -> 87.5 us
    ppermute x1, waiting for transfers between devices: 33.8 us -> 31.3 us  [spread(): near = lax.ppermute(exported, 'node', PAIRS)]
where the time goes in v3:
time: 159 us; the launch traced here: 158 us
  waiting for transfers between devices  87.5 us (55%)
  Pallas kernels  37.1 us (23%)
  starting transfers between devices  33.3 us (21%)
    ppermute x20, waiting for transfers between devices, swap(): return lax.ppermute(array, axis, [(i, i ^ distance) for i in range(size)])  36.3 us
    ppermute x1, waiting for transfers between devices, spread(): near = lax.ppermute(exported, 'node', PAIRS)  31.3 us
    pallas_call x2, Pallas kernels, attend(): pl.pallas_call(functools.partial(attend_body, kv, parts, [len(choice) for...  16.5 us
    ppermute x20, starting transfers between devices, swap(): return lax.ppermute(array, axis, [(i, i ^ distance) for i in range(size)])  16.3 us
    pallas_call x15, Pallas kernels, step(): pl.pallas_call(functools.partial(step_body, plan), out_shape=[jax.ShapeDt...  15.3 us
    ppermute x1, waiting for transfers between devices, spread(): across_out = lax.ppermute(across, 'node', OUTWARD)  9.22 us
    ppermute x1, waiting for transfers between devices, spread(): far = lax.ppermute(exported, 'node', ENDS)  5.52 us
    ppermute x1, starting transfers between devices, spread(): near = lax.ppermute(exported, 'node', PAIRS)  4.36 us
  transfers between devices with their start and end apart: 30, of which 17 were waited for; matrix products, arithmetic and copies ran while one was open for 0% of the time, Pallas kernels for 22%

profile of v3, /device:TPU:0, one launch (start us, length us, event | category | flops | bytes accessed | tf_op | source)
XLA Modules:
  0.0 158.4 jit_solution(7275496721487750598)
XLA Ops:
  1.5 3.1 %collective-permute-start.5 = (bf16[640,1280]{1,0:T(8,128)(2,1)S(1)}, bf16[640,1280]{1,0:T(8,128)(2,1)S(1)}, u32[]{:S(2)}, u32[]{:S(2)}) collective-permute-start(bf16[640,1280]{1,0:T(8,128)(2,1)S(1)} %cut.1), channel_id=1, source_target_pairs={{0,4},{4,0},{8,12},{12,8},{1,5},{5,1},{9,13},{13,9},{2,6},{6,2},{1... | collective-permute-start | bytes 4915208 | tf_op jit(solution)/shard_map/ppermute | solution.py:422
  5.4 1.8 %prepare.1 = (bf16[4,128,256]{2,1,0:T(8,128)(2,1)S(1)}, s32[8]{0:T(128)S(1)}) custom-call(s32[24]{0:T(128)S(1)} %copy-done.4, s32[7,24]{1,0:T(8,128)S(1)} %bitcast.13, s32[24]{0:T(128)S(1)} %copy-done.5, bf16[768,256]{1,0:T(8,128)(2,1)S(1)} %copy-done.1, bf16[768,256]{1,0:T(8,128)(2,1)S(1)} %copy-done.2), custom_call_target="tpu_custom_call" | custom-call | tf_op jit(solution)/shard_map/prepare/pallas_call | solution.py:93
  7.3 4.4 %collective-permute-start = (bf16[4,128,256]{2,1,0:T(8,128)(2,1)S(1)}, bf16[4,128,256]{2,1,0:T(8,128)(2,1)S(1)}, u32[]{:S(2)}, u32[]{:S(2)}) collective-permute-start(bf16[4,128,256]{2,1,0:T(8,128)(2,1)S(1)} %get-tuple-element.36), channel_id=1, source_target_pairs={{0,4},{4,0},{8,12},{12,8},{1,5},{5,1},{9,13},{13,9},{2,6},{6,2},{1... | collective-permute-start | bytes 786440 | tf_op jit(solution)/shard_map/ppermute | solution.py:583
  12.3 2.8 %collective-permute-start.4 = (bf16[4,128,256]{2,1,0:T(8,128)(2,1)S(1)}, bf16[4,128,256]{2,1,0:T(8,128)(2,1)S(1)}, u32[]{:S(2)}, u32[]{:S(2)}) collective-permute-start(bf16[4,128,256]{2,1,0:T(8,128)(2,1)S(1)} %get-tuple-element.36), channel_id=1, source_target_pairs={{0,12},{12,0},{1,13},{13,1},{2,14},{14,2},{3,15},{15,3},{16,28},{2... | collective-permute-start | bytes 786440 | tf_op jit(solution)/shard_map/ppermute | solution.py:587
  15.1 31.3 %collective-permute-done.refs_0_ = bf16[4,128,256]{2,1,0:T(8,128)(2,1)S(1)} collective-permute-done((bf16[4,128,256]{2,1,0:T(8,128)(2,1)S(1)}, bf16[4,128,256]{2,1,0:T(8,128)(2,1)S(1)}, u32[]{:S(2)}, u32[]{:S(2)}) %collective-permute-start) | collective-permute-done | bytes 262176 | tf_op jit(solution)/shard_map/ppermute | solution.py:583
  48.4 5.5 %collective-permute-done.4.refs_4_ = bf16[4,128,256]{2,1,0:T(8,128)(2,1)S(1)} collective-permute-done((bf16[4,128,256]{2,1,0:T(8,128)(2,1)S(1)}, bf16[4,128,256]{2,1,0:T(8,128)(2,1)S(1)}, u32[]{:S(2)}, u32[]{:S(2)}) %collective-permute-start.4) | collective-permute-done | bytes 262176 | tf_op jit(solution)/shard_map/ppermute | solution.py:587
  54.0 9.2 %collective-permute-done.3.refs_2_ = bf16[4,128,256]{2,1,0:T(8,128)(2,1)S(1)} collective-permute-done((bf16[4,128,256]{2,1,0:T(8,128)(2,1)S(1)}, bf16[4,128,256]{2,1,0:T(8,128)(2,1)S(1)}, u32[]{:S(2)}, u32[]{:S(2)}) %collective-permute-start.3) | collective-permute-done | bytes 262176 | tf_op jit(solution)/shard_map/ppermute | solution.py:586
  65.3 8.3 %attend.2.refs_5_ = bf16[4,192,640]{2,1,0:T(8,128)(2,1)S(1)} custom-call(s32[8]{0:T(128)S(1)} %get-tuple-element.35.table, bf16[768,1280]{1,0:T(8,128)(2,1)} %query_hbm.3, bf16[768,256]{1,0:T(8,128)(2,1)} %keys_hbm.3, bf16[768,256]{1,0:T(8,128)(2,1)} %values_hbm.3, bf16[4,128,256]{2,1,0:T(8,128)(2,1)S(1)} %collective-permute-done.refs_0_, ...), custom_call_target="tpu_custom_call" | custom-call | flops 1 | bytes 1 | tf_op jit(solution)/shard_map/attend/pallas_call | solution.py:244
  73.5 1.5 collective-permute-start.7
  75.1 8.3 %attend.3 = bf16[4,192,640]{2,1,0:T(8,128)(2,1)S(1)} custom-call(s32[8]{0:T(128)S(1)} %get-tuple-element.35.table, bf16[768,1280]{1,0:T(8,128)(2,1)} %query_hbm.3, bf16[768,256]{1,0:T(8,128)(2,1)} %keys_hbm.3, bf16[768,256]{1,0:T(8,128)(2,1)} %values_hbm.3, bf16[4,128,256]{2,1,0:T(8,128)(2,1)S(1)} %collective-permute-done.refs_0_, ...), custom_call_target="tpu_custom_call" | custom-call | flops 1 | bytes 1 | tf_op jit(solution)/shard_map/attend/pallas_call | solution.py:244
  83.3 3.2 %step.15 = (bf16[384,640]{1,0:T(8,128)(2,1)S(1)}, bf16[384,640]{1,0:T(8,128)(2,1)S(1)}, bf16[384,512]{1,0:T(8,128)(2,1)S(1)}, bf16[384,512]{1,0:T(8,128)(2,1)S(1...) custom-call(bf16[768,640]{1,0:T(8,128)(2,1)S(1)} %bitcast.4, bf16[768,640]{1,0:T(8,128)(2,1)S(1)} %bitcast.8, ...), custom_call_target="tpu_custom_call" | custom-call | flops 1 | bytes 1 | tf_op jit(solution)/shard_map/step/pallas_call | solution.py:404
  87.2 1.9 %collective-permute-done.14.refs_3_.refs_7_ = bf16[384,512]{1,0:T(8,128)(2,1)S(1)} collective-permute-done((bf16[384,512]{1,0:T(8,128)(2,1)S(1)}, bf16[384,512]{1,0:T(8,128)(2,1)S(1)}, u32[]{:S(2)}, u32[]{:S(2)}) %collective-permute-start.14) | collective-permute-done | bytes 393248 | tf_op jit(solution)/shard_map/ppermute | solution.py:268
  89.2 1.6 collective-permute-start.16
  92.5 2.6 %collective-permute-done.7.refs_4_.refs_0_ = bf16[768,640]{1,0:T(8,128)(2,1)S(1)} collective-permute-done((bf16[768,640]{1,0:T(8,128)(2,1)S(1)}, bf16[768,640]{1,0:T(8,128)(2,1)S(1)}, u32[]{:S(2)}, u32[]{:S(2)}) %collective-permute-start.7) | collective-permute-done | bytes 983072 | tf_op jit(solution)/shard_map/ppermute | solution.py:268
  95.2 1.7 %step.17 = (bf16[384,640]{1,0:T(8,128)(2,1)S(1)}, bf16[384,640]{1,0:T(8,128)(2,1)S(1)}) custom-call(bf16[768,640]{1,0:T(8,128)(2,1)S(1)} %bitcast.5, bf16[768,640]{1,0:T(8,128)(2,1)S(1)} %bitcast.10, bf16[640,1280]{1,0:T(8,128)(2,1)S(1)} %collective-permute-done.5.refs_5_.refs_2_, bf16[192,1152]{1,0:T(8,128)(2,1)S(1)} %step.16.refs_3_, ...), custom_call_target="tpu_custom_call" | custom-call | flops 1 | bytes 1 | tf_op jit(solution)/shard_map/step/pallas_call | solution.py:404
  97.0 4.5 %collective-permute-done.16.refs_8_ = bf16[192,1152]{1,0:T(8,128)(2,1)S(1)} collective-permute-done((bf16[192,1152]{1,0:T(8,128)(2,1)S(1)}, bf16[192,1152]{1,0:T(8,128)(2,1)S(1)}, u32[]{:S(2)}, u32[]{:S(2)}) %collective-permute-start.16) | collective-permute-done | bytes 442400 | tf_op jit(solution)/shard_map/ppermute | solution.py:268
  102.5 2.3 %step.18 = (bf16[384,640]{1,0:T(8,128)(2,1)S(1)}, bf16[384,640]{1,0:T(8,128)(2,1)S(1)}, bf16[192,640]{1,0:T(8,128)(2,1)S(1)}, bf16[192,512]{1,0:T(8,128)(2,1)S(1)}) custom-call(bf16[768,640]{1,0:T(8,128)(2,1)S(1)} %bitcast.6, bf16[768,640]{1,0:T(8,128)(2,1)S(1)} %bitcast.11, bf16[640,1280]{1,0:T(8,128)(2,1)S(1)} %collective-permute-done.9.refs_2_.refs_3_, ...), custom_call_target="tpu_custom_call" | custom-call | flops 1 | bytes 1 | tf_op jit(solution)/shard_map/step/pallas_call | solution.py:404
  107.0 1.6 collective-permute-start.20
  108.5 6.7 %collective-permute-done.8.refs_1_ = bf16[768,640]{1,0:T(8,128)(2,1)S(1)} collective-permute-done((bf16[768,640]{1,0:T(8,128)(2,1)S(1)}, bf16[768,640]{1,0:T(8,128)(2,1)S(1)}, u32[]{:S(2)}, u32[]{:S(2)}) %collective-permute-start.8) | collective-permute-done | bytes 983072 | tf_op jit(solution)/shard_map/ppermute | solution.py:268
  115.3 3.6 %step.20 = (bf16[384,640]{1,0:T(8,128)(2,1)S(1)}, bf16[384,640]{1,0:T(8,128)(2,1)S(1)}, bf16[384,640]{1,0:T(8,128)(2,1)S(1)}, bf16[384,640]{1,0:T(8,128)(2,1)S(1)}) custom-call(bf16[768,640]{1,0:T(8,128)(2,1)S(1)} %collective-permute-done.7.refs_4_.refs_0_, bf16[768,640]{1,0:T(8,128)(2,1)S(1)} %collective-permute-done.8.refs_1_, ...), custom_call_target="tpu_custom_call" | custom-call | flops 1 | bytes 1 | tf_op jit(solution)/shard_map/step/pallas_call | solution.py:404
  121.6 1.6 collective-permute-start.21
  123.2 6.0 %collective-permute-done.21.refs_4_ = bf16[192,640]{1,0:T(8,128)(2,1)S(1)} collective-permute-done((bf16[192,640]{1,0:T(8,128)(2,1)S(1)}, bf16[192,640]{1,0:T(8,128)(2,1)S(1)}, u32[]{:S(2)}, u32[]{:S(2)}) %collective-permute-start.21) | collective-permute-done | bytes 245792 | tf_op jit(solution)/shard_map/ppermute | solution.py:268
  129.3 1.6 collective-permute-start.23
  132.3 4.1 %collective-permute-done.10.refs_3_ = bf16[640,1280]{1,0:T(8,128)(2,1)S(1)} collective-permute-done((bf16[640,1280]{1,0:T(8,128)(2,1)S(1)}, bf16[640,1280]{1,0:T(8,128)(2,1)S(1)}, u32[]{:S(2)}, u32[]{:S(2)}) %collective-permute-start.10) | collective-permute-done | bytes 1638432 | tf_op jit(solution)/shard_map/ppermute | solution.py:500
  136.4 1.7 %step.23 = (bf16[384,640]{1,0:T(8,128)(2,1)S(1)}, bf16[384,640]{1,0:T(8,128)(2,1)S(1)}) custom-call(bf16[768,640]{1,0:T(8,128)(2,1)S(1)} %collective-permute-done.7.refs_4_.refs_0_, bf16[768,640]{1,0:T(8,128)(2,1)S(1)} %collective-permute-done.8.refs_1_, bf16[640,1280]{1,0:T(8,128)(2,1)S(1)} %collective-permute-done.6.refs_6_.refs_2_, ...), custom_call_target="tpu_custom_call" | custom-call | flops 1 | bytes 1 | tf_op jit(solution)/shard_map/step/pallas_call | solution.py:404
  138.3 1.7 %step.25 = (bf16[384,640]{1,0:T(8,128)(2,1)S(1)}, bf16[384,640]{1,0:T(8,128)(2,1)S(1)}) custom-call(bf16[768,640]{1,0:T(8,128)(2,1)S(1)} %bitcast.7, bf16[768,640]{1,0:T(8,128)(2,1)S(1)} %bitcast.12, bf16[640,1280]{1,0:T(8,128)(2,1)S(1)} %collective-permute-done.6.refs_6_.refs_2_, bf16[640,1280]{1,0:T(8,128)(2,1)S(1)} %collective-permute-done.10.refs_3_, ...), custom_call_target="tpu_custom_call" | custom-call | flops 1 | bytes 1 | tf_op jit(solution)/shard_map/step/pallas_call | solution.py:404
  140.6 1.5 collective-permute-start.27
  142.2 1.5 collective-permute-start.25
  144.4 4.1 %collective-permute-done.27.refs_4_.refs_6_ = bf16[192,640]{1,0:T(8,128)(2,1)S(1)} collective-permute-done((bf16[192,640]{1,0:T(8,128)(2,1)S(1)}, bf16[192,640]{1,0:T(8,128)(2,1)S(1)}, u32[]{:S(2)}, u32[]{:S(2)}) %collective-permute-start.27) | collective-permute-done | bytes 245792 | tf_op jit(solution)/shard_map/ppermute | solution.py:268
  148.5 2.6 %collective-permute-done.25.refs_2_ = bf16[192,640]{1,0:T(8,128)(2,1)S(1)} collective-permute-done((bf16[192,640]{1,0:T(8,128)(2,1)S(1)}, bf16[192,640]{1,0:T(8,128)(2,1)S(1)}, u32[]{:S(2)}, u32[]{:S(2)}) %collective-permute-start.25) | collective-permute-done | bytes 245792 | tf_op jit(solution)/shard_map/ppermute | solution.py:268
  152.9 2.2 %collective-permute-done.29.refs_2_ = bf16[192,640]{1,0:T(8,128)(2,1)S(1)} collective-permute-done((bf16[192,640]{1,0:T(8,128)(2,1)S(1)}, bf16[192,640]{1,0:T(8,128)(2,1)S(1)}, u32[]{:S(2)}, u32[]{:S(2)}) %collective-permute-start.29) | collective-permute-done | bytes 245792 | tf_op jit(solution)/shard_map/ppermute | solution.py:268
  155.3 2.2 %collective-permute-done.28.refs_0_ = bf16[192,640]{1,0:T(8,128)(2,1)S(1)} collective-permute-done((bf16[192,640]{1,0:T(8,128)(2,1)S(1)}, bf16[192,640]{1,0:T(8,128)(2,1)S(1)}, u32[]{:S(2)}, u32[]{:S(2)}) %collective-permute-start.28) | collective-permute-done | bytes 245792 | tf_op jit(solution)/shard_map/ppermute | solution.py:268
  (61 shorter events, 21.2 us)
Async XLA Ops:
  0.0 5.4 %copy-start.2 = (bf16[768,256]{1,0:T(8,128)(2,1)S(1)}, bf16[768,256]{1,0:T(8,128)(2,1)}, u32[]{:S(2)}) copy-start(bf16[768,256]{1,0:T(8,128)(2,1)} %values_hbm.3) | copy-start | bytes 1179652
  1.5 61.7 %collective-permute-start.5 = (bf16[640,1280]{1,0:T(8,128)(2,1)S(1)}, bf16[640,1280]{1,0:T(8,128)(2,1)S(1)}, u32[]{:S(2)}, u32[]{:S(2)}) collective-permute-start(bf16[640,1280]{1,0:T(8,128)(2,1)S(1)} %cut.1), channel_id=1, source_target_pairs={{0,4},{4,0},{8,12},{12,8},{1,5},{5,1},{9,13},{13,9},{2,6},{6,2},{1... | collective-permute-start | bytes 4915208 | tf_op jit(solution)/shard_map/ppermute | solution.py:422
  4.6 59.3 %collective-permute-start.6 = (bf16[640,1280]{1,0:T(8,128)(2,1)S(1)}, bf16[640,1280]{1,0:T(8,128)(2,1)S(1)}, u32[]{:S(2)}, u32[]{:S(2)}) collective-permute-start(bf16[640,1280]{1,0:T(8,128)(2,1)S(1)} %cut.1), channel_id=1, source_target_pairs={{4,8},{8,4},{5,9},{9,5},{6,10},{10,6},{7,11},{11,7},{20,24},{24,20... | collective-permute-start | bytes 4915208 | tf_op jit(solution)/shard_map/ppermute | solution.py:423
  7.3 39.2 %collective-permute-start = (bf16[4,128,256]{2,1,0:T(8,128)(2,1)S(1)}, bf16[4,128,256]{2,1,0:T(8,128)(2,1)S(1)}, u32[]{:S(2)}, u32[]{:S(2)}) collective-permute-start(bf16[4,128,256]{2,1,0:T(8,128)(2,1)S(1)} %get-tuple-element.36), channel_id=1, source_target_pairs={{0,4},{4,0},{8,12},{12,8},{1,5},{5,1},{9,13},{13,9},{2,6},{6,2},{1... | collective-permute-start | bytes 786440 | tf_op jit(solution)/shard_map/ppermute | solution.py:583
  11.6 35.5 %collective-permute-start.2 = (bf16[4,128,256]{2,1,0:T(8,128)(2,1)S(1)}, bf16[4,128,256]{2,1,0:T(8,128)(2,1)S(1)}, u32[]{:S(2)}, u32[]{:S(2)}) collective-permute-start(bf16[4,128,256]{2,1,0:T(8,128)(2,1)S(1)} %get-tuple-element.36), channel_id=1, source_target_pairs={{4,8},{8,4},{5,9},{9,5},{6,10},{10,6},{7,11},{11,7},{20,24},{24,20... | collective-permute-start | bytes 786440 | tf_op jit(solution)/shard_map/ppermute | solution.py:584
  12.3 41.7 %collective-permute-start.4 = (bf16[4,128,256]{2,1,0:T(8,128)(2,1)S(1)}, bf16[4,128,256]{2,1,0:T(8,128)(2,1)S(1)}, u32[]{:S(2)}, u32[]{:S(2)}) collective-permute-start(bf16[4,128,256]{2,1,0:T(8,128)(2,1)S(1)} %get-tuple-element.36), channel_id=1, source_target_pairs={{0,12},{12,0},{1,13},{13,1},{2,14},{14,2},{3,15},{15,3},{16,28},{2... | collective-permute-start | bytes 786440 | tf_op jit(solution)/shard_map/ppermute | solution.py:587
  46.4 7.5 %collective-permute-start.1 = (bf16[4,128,256]{2,1,0:T(8,128)(2,1)S(1)}, bf16[4,128,256]{2,1,0:T(8,128)(2,1)S(1)}, u32[]{:S(2)}, u32[]{:S(2)}) collective-permute-start(bf16[4,128,256]{2,1,0:T(8,128)(2,1)S(1)} %collective-permute-done.refs_0_), channel_id=1, source_target_pairs={{4,8},{8,4},{5,9},{9,5},{6,10},{10,6},{7,11},{11,7},{20,24},{24,20... | collective-permute-start | bytes 786440 | tf_op jit(solution)/shard_map/ppermute | solution.py:585
  47.1 16.1 %collective-permute-start.3 = (bf16[4,128,256]{2,1,0:T(8,128)(2,1)S(1)}, bf16[4,128,256]{2,1,0:T(8,128)(2,1)S(1)}, u32[]{:S(2)}, u32[]{:S(2)}) collective-permute-start(bf16[4,128,256]{2,1,0:T(8,128)(2,1)S(1)} %collective-permute-done.2.refs_3_), channel_id=1, source_target_pairs={{4,0},{8,12},{5,1},{9,13},{6,2},{10,14},{7,3},{11,15},{20,16},{24,... | collective-permute-start | bytes 786440 | tf_op jit(solution)/shard_map/ppermute | solution.py:586
  63.2 28.1 %collective-permute-start.9 = (bf16[640,1280]{1,0:T(8,128)(2,1)S(1)}, bf16[640,1280]{1,0:T(8,128)(2,1)S(1)}, u32[]{:S(2)}, u32[]{:S(2)}) collective-permute-start(bf16[640,1280]{1,0:T(8,128)(2,1)S(1)} %collective-permute-done.5.refs_5_.refs_2_), channel_id=1, source_target_pairs={{4,8},{8,4},{5,9},{9,5},{6,10},{10,6},{7,11},{11,7},{20,24},{24,20... | collective-permute-start | bytes 4915208 | tf_op jit(solution)/shard_map/ppermute | solution.py:427
  64.0 38.5 %collective-permute-start.11 = (bf16[640,1280]{1,0:T(8,128)(2,1)S(1)}, bf16[640,1280]{1,0:T(8,128)(2,1)S(1)}, u32[]{:S(2)}, u32[]{:S(2)}) collective-permute-start(bf16[640,1280]{1,0:T(8,128)(2,1)S(1)} %collective-permute-done.6.refs_6_.refs_2_), channel_id=1, source_target_pairs={{4,0},{8,12},{5,1},{9,13},{6,2},{10,14},{7,3},{11,15},{20,16},{24,... | collective-permute-start | bytes 4915208 | tf_op jit(solution)/shard_map/ppermute | solution.py:426
  73.5 9.8 %copy-start = (bf16[1280,1280]{1,0:T(8,128)(2,1)S(1)}, bf16[1280,1280]{1,0:T(8,128)(2,1)}, u32[]{:S(2)}) copy-start(bf16[1280,1280]{1,0:T(8,128)(2,1)} %refs_2_.3) | copy-start | bytes 9830404
  73.5 21.6 %collective-permute-start.7 = (bf16[768,640]{1,0:T(8,128)(2,1)S(1)}, bf16[768,640]{1,0:T(8,128)(2,1)S(1)}, u32[]{:S(2)}, u32[]{:S(2)}) collective-permute-start(bf16[768,640]{1,0:T(8,128)(2,1)S(1)} %bitcast.3), channel_id=1, source_target_pairs={{0,16},{16,0},{1,17},{17,1},{2,18},{18,2},{3,19},{19,3},{4,20},{20... | collective-permute-start | bytes 2949128 | tf_op jit(solution)/shard_map/ppermute | solution.py:268
  86.6 2.5 %collective-permute-start.13 = (bf16[384,640]{1,0:T(8,128)(2,1)S(1)}, bf16[384,640]{1,0:T(8,128)(2,1)S(1)}, u32[]{:S(2)}, u32[]{:S(2)}) collective-permute-start(bf16[384,640]{1,0:T(8,128)(2,1)S(1)} %get-tuple-element.42), channel_id=1, source_target_pairs={{0,1},{1,0},{2,3},{3,2},{4,5},{5,4},{6,7},{7,6},{8,9},{9,8},{10,11... | collective-permute-start | bytes 1474568 | tf_op jit(solution)/shard_map/ppermute | solution.py:268
  86.7 2.4 %collective-permute-start.14 = (bf16[384,512]{1,0:T(8,128)(2,1)S(1)}, bf16[384,512]{1,0:T(8,128)(2,1)S(1)}, u32[]{:S(2)}, u32[]{:S(2)}) collective-permute-start(bf16[384,512]{1,0:T(8,128)(2,1)S(1)} %get-tuple-element.44), channel_id=1, source_target_pairs={{0,1},{1,0},{2,3},{3,2},{4,5},{5,4},{6,7},{7,6},{8,9},{9,8},{10,11... | collective-permute-start | bytes 1179656 | tf_op jit(solution)/shard_map/ppermute | solution.py:268
  89.2 12.3 %collective-permute-start.16 = (bf16[192,1152]{1,0:T(8,128)(2,1)S(1)}, bf16[192,1152]{1,0:T(8,128)(2,1)S(1)}, u32[]{:S(2)}, u32[]{:S(2)}) collective-permute-start(bf16[192,1152]{1,0:T(8,128)(2,1)S(1)} %step.16.refs_3_), channel_id=1, source_target_pairs={{0,2},{1,3},{2,0},{3,1},{4,6},{5,7},{6,4},{7,5},{8,10},{9,11},{10,... | collective-permute-start | bytes 1327112 | tf_op jit(solution)/shard_map/ppermute | solution.py:268
  90.7 24.5 %collective-permute-start.8 = (bf16[768,640]{1,0:T(8,128)(2,1)S(1)}, bf16[768,640]{1,0:T(8,128)(2,1)S(1)}, u32[]{:S(2)}, u32[]{:S(2)}) collective-permute-start(bf16[768,640]{1,0:T(8,128)(2,1)S(1)} %bitcast.9), channel_id=1, source_target_pairs={{0,16},{16,0},{1,17},{17,1},{2,18},{18,2},{3,19},{19,3},{4,20},{20... | collective-permute-start | bytes 2949128 | tf_op jit(solution)/shard_map/ppermute | solution.py:268
  91.2 45.2 %collective-permute-start.10 = (bf16[640,1280]{1,0:T(8,128)(2,1)S(1)}, bf16[640,1280]{1,0:T(8,128)(2,1)S(1)}, u32[]{:S(2)}, u32[]{:S(2)}) collective-permute-start(bf16[640,1280]{1,0:T(8,128)(2,1)S(1)} %collective-permute-done.9.refs_2_.refs_3_), channel_id=1, source_target_pairs={{4,0},{8,12},{5,1},{9,13},{6,2},{10,14},{7,3},{11,15},{20,16},{24,... | collective-permute-start | bytes 4915208 | tf_op jit(solution)/shard_map/ppermute | solution.py:500
  96.9 10.0 %collective-permute-start.15 = (bf16[384,640]{1,0:T(8,128)(2,1)S(1)}, bf16[384,640]{1,0:T(8,128)(2,1)S(1)}, u32[]{:S(2)}, u32[]{:S(2)}) collective-permute-start(bf16[384,640]{1,0:T(8,128)(2,1)S(1)} %get-tuple-element.46.refs_9_), channel_id=1, source_target_pairs={{0,1},{1,0},{2,3},{3,2},{4,5},{5,4},{6,7},{7,6},{8,9},{9,8},{10,11... | collective-permute-start | bytes 1474568 | tf_op jit(solution)/shard_map/ppermute | solution.py:268
  104.8 2.1 %collective-permute-start.17 = (bf16[384,640]{1,0:T(8,128)(2,1)S(1)}, bf16[384,640]{1,0:T(8,128)(2,1)S(1)}, u32[]{:S(2)}, u32[]{:S(2)}) collective-permute-start(bf16[384,640]{1,0:T(8,128)(2,1)S(1)} %get-tuple-element.48), channel_id=1, source_target_pairs={{0,1},{1,0},{2,3},{3,2},{4,5},{5,4},{6,7},{7,6},{8,9},{9,8},{10,11... | collective-permute-start | bytes 1474568 | tf_op jit(solution)/shard_map/ppermute | solution.py:268
  104.8 2.0 %collective-permute-start.12 = (bf16[384,128]{1,0:T(8,128)(2,1)S(1)}, bf16[384,128]{1,0:T(8,128)(2,1)S(1)}, u32[]{:S(2)}, u32[]{:S(2)}) collective-permute-start(bf16[384,128]{1,0:T(8,128)(2,1)S(1)} %get-tuple-element.40), channel_id=1, source_target_pairs={{0,1},{1,0},{2,3},{3,2},{4,5},{5,4},{6,7},{7,6},{8,9},{9,8},{10,11... | collective-permute-start | bytes 294920 | tf_op jit(solution)/shard_map/ppermute | solution.py:268
  107.0 14.4 %collective-permute-start.20 = (bf16[192,1408]{1,0:T(8,128)(2,1)S(1)}, bf16[192,1408]{1,0:T(8,128)(2,1)S(1)}, u32[]{:S(2)}, u32[]{:S(2)}) collective-permute-start(bf16[192,1408]{1,0:T(8,128)(2,1)S(1)} %step.19.refs_5_), channel_id=1, source_target_pairs={{0,2},{1,3},{2,0},{3,1},{4,6},{5,7},{6,4},{7,5},{8,10},{9,11},{10,... | collective-permute-start | bytes 1622024 | tf_op jit(solution)/shard_map/ppermute | solution.py:268
  118.9 1.9 %collective-permute-start.19 = (bf16[384,640]{1,0:T(8,128)(2,1)S(1)}, bf16[384,640]{1,0:T(8,128)(2,1)S(1)}, u32[]{:S(2)}, u32[]{:S(2)}) collective-permute-start(bf16[384,640]{1,0:T(8,128)(2,1)S(1)} %get-tuple-element.52), channel_id=1, source_target_pairs={{0,1},{1,0},{2,3},{3,2},{4,5},{5,4},{6,7},{7,6},{8,9},{9,8},{10,11... | collective-permute-start | bytes 1474568 | tf_op jit(solution)/shard_map/ppermute | solution.py:268
  119.0 4.2 %collective-permute-start.18 = (bf16[384,640]{1,0:T(8,128)(2,1)S(1)}, bf16[384,640]{1,0:T(8,128)(2,1)S(1)}, u32[]{:S(2)}, u32[]{:S(2)}) collective-permute-start(bf16[384,640]{1,0:T(8,128)(2,1)S(1)} %get-tuple-element.50), channel_id=1, source_target_pairs={{0,1},{1,0},{2,3},{3,2},{4,5},{5,4},{6,7},{7,6},{8,9},{9,8},{10,11... | collective-permute-start | bytes 1474568 | tf_op jit(solution)/shard_map/ppermute | solution.py:268
  121.6 7.6 %collective-permute-start.21 = (bf16[192,640]{1,0:T(8,128)(2,1)S(1)}, bf16[192,640]{1,0:T(8,128)(2,1)S(1)}, u32[]{:S(2)}, u32[]{:S(2)}) collective-permute-start(bf16[192,640]{1,0:T(8,128)(2,1)S(1)} %get-tuple-element.53), channel_id=1, source_target_pairs={{0,2},{1,3},{2,0},{3,1},{4,6},{5,7},{6,4},{7,5},{8,10},{9,11},{10,... | collective-permute-start | bytes 737288 | tf_op jit(solution)/shard_map/ppermute | solution.py:268
  129.3 8.9 %collective-permute-start.23 = (bf16[192,640]{1,0:T(8,128)(2,1)S(1)}, bf16[192,640]{1,0:T(8,128)(2,1)S(1)}, u32[]{:S(2)}, u32[]{:S(2)}) collective-permute-start(bf16[192,640]{1,0:T(8,128)(2,1)S(1)} %get-tuple-element.54.refs_4_), channel_id=1, source_target_pairs={{0,2},{1,3},{2,0},{3,1},{4,6},{5,7},{6,4},{7,5},{8,10},{9,11},{10,... | collective-permute-start | bytes 737288 | tf_op jit(solution)/shard_map/ppermute | solution.py:268
  130.9 7.3 %collective-permute-start.24 = (bf16[192,640]{1,0:T(8,128)(2,1)S(1)}, bf16[192,640]{1,0:T(8,128)(2,1)S(1)}, u32[]{:S(2)}, u32[]{:S(2)}) collective-permute-start(bf16[192,640]{1,0:T(8,128)(2,1)S(1)} %get-tuple-element.57), channel_id=1, source_target_pairs={{0,16},{16,0},{1,17},{17,1},{2,18},{18,2},{3,19},{19,3},{4,20},{20... | collective-permute-start | bytes 737288 | tf_op jit(solution)/shard_map/ppermute | solution.py:268
  138.1 4.0 %collective-permute-start.22 = (bf16[384,640]{1,0:T(8,128)(2,1)S(1)}, bf16[384,640]{1,0:T(8,128)(2,1)S(1)}, u32[]{:S(2)}, u32[]{:S(2)}) collective-permute-start(bf16[384,640]{1,0:T(8,128)(2,1)S(1)} %get-tuple-element.56.refs_3_), channel_id=1, source_target_pairs={{0,1},{1,0},{2,3},{3,2},{4,5},{5,4},{6,7},{7,6},{8,9},{9,8},{10,11... | collective-permute-start | bytes 1474568 | tf_op jit(solution)/shard_map/ppermute | solution.py:268
  140.1 3.7 %collective-permute-start.26 = (bf16[384,640]{1,0:T(8,128)(2,1)S(1)}, bf16[384,640]{1,0:T(8,128)(2,1)S(1)}, u32[]{:S(2)}, u32[]{:S(2)}) collective-permute-start(bf16[384,640]{1,0:T(8,128)(2,1)S(1)} %get-tuple-element.58.refs_2_), channel_id=1, source_target_pairs={{0,1},{1,0},{2,3},{3,2},{4,5},{5,4},{6,7},{7,6},{8,9},{9,8},{10,11... | collective-permute-start | bytes 1474568 | tf_op jit(solution)/shard_map/ppermute | solution.py:268
  140.6 7.9 %collective-permute-start.27 = (bf16[192,640]{1,0:T(8,128)(2,1)S(1)}, bf16[192,640]{1,0:T(8,128)(2,1)S(1)}, u32[]{:S(2)}, u32[]{:S(2)}) collective-permute-start(bf16[192,640]{1,0:T(8,128)(2,1)S(1)} %step.24.refs_4_), channel_id=1, source_target_pairs={{0,16},{16,0},{1,17},{17,1},{2,18},{18,2},{3,19},{19,3},{4,20},{20... | collective-permute-start | bytes 737288 | tf_op jit(solution)/shard_map/ppermute | solution.py:268
  142.2 8.9 %collective-permute-start.25 = (bf16[192,640]{1,0:T(8,128)(2,1)S(1)}, bf16[192,640]{1,0:T(8,128)(2,1)S(1)}, u32[]{:S(2)}, u32[]{:S(2)}) collective-permute-start(bf16[192,640]{1,0:T(8,128)(2,1)S(1)} %step.26.refs_2_), channel_id=1, source_target_pairs={{0,2},{1,3},{2,0},{3,1},{4,6},{5,7},{6,4},{7,5},{8,10},{9,11},{10,... | collective-permute-start | bytes 737288 | tf_op jit(solution)/shard_map/ppermute | solution.py:268
  143.8 11.4 %collective-permute-start.29 = (bf16[192,640]{1,0:T(8,128)(2,1)S(1)}, bf16[192,640]{1,0:T(8,128)(2,1)S(1)}, u32[]{:S(2)}, u32[]{:S(2)}) collective-permute-start(bf16[192,640]{1,0:T(8,128)(2,1)S(1)} %step.27.refs_3_), channel_id=1, source_target_pairs={{0,2},{1,3},{2,0},{3,1},{4,6},{5,7},{6,4},{7,5},{8,10},{9,11},{10,... | collective-permute-start | bytes 737288 | tf_op jit(solution)/shard_map/ppermute | solution.py:268
  151.2 6.3 %collective-permute-start.28 = (bf16[192,640]{1,0:T(8,128)(2,1)S(1)}, bf16[192,640]{1,0:T(8,128)(2,1)S(1)}, u32[]{:S(2)}, u32[]{:S(2)}) collective-permute-start(bf16[192,640]{1,0:T(8,128)(2,1)S(1)} %step.28.refs_3_), channel_id=1, source_target_pairs={{0,16},{16,0},{1,17},{17,1},{2,18},{18,2},{3,19},{19,3},{4,20},{20... | collective-permute-start | bytes 737288 | tf_op jit(solution)/shard_map/ppermute | solution.py:268
  (4 other events, 21.6 us)

commit v4 on v3

--- a/solution.py
+++ b/solution.py
@@ -543,7 +543,7 @@
     six = [(kept_6, core(sent_6))]
     (away,) = step(cores=[five], after=[sent_6])
     five.append(chip(away))
-    (away,) = step(cores=[six], after=[away])
+    (away,) = step(cores=[six], after=[away, back_4])
     six.append(chip(away))
     (done_5,) = step(chips=[five], after=[away, back_4])
     back_5 = back(done_5)

time: 159 us -> 158 us (level)
  waiting for transfers between devices: 87.5 us -> 85.1 us
  starting transfers between devices: 33.3 us -> 35.5 us
    ppermute x20, waiting for transfers between devices: 36.3 us -> 33.9 us  [swap(): return lax.ppermute(array, axis, [(i, i ^ distance) for i in range(size)])]
    ppermute x20, starting transfers between devices: 16.3 us -> 18.5 us  [swap(): return lax.ppermute(array, axis, [(i, i ^ distance) for i in range(size)])]
  transfers between devices with their start and end apart: 30 -> 30, of which waited for: 17 -> 16; matrix products, arithmetic and copies ran while one was open for 0% -> 0% of each run, Pallas kernels for 22% -> 22%
where the time goes in v4:
time: 158 us
  waiting for transfers between devices  85.1 us (54%)
  Pallas kernels  37 us (23%)
  starting transfers between devices  35.5 us (22%)
    ppermute x20, waiting for transfers between devices, swap(): return lax.ppermute(array, axis, [(i, i ^ distance) for i in range(size)])  33.9 us
    ppermute x1, waiting for transfers between devices, spread(): near = lax.ppermute(exported, 'node', PAIRS)  31.3 us
    ppermute x20, starting transfers between devices, swap(): return lax.ppermute(array, axis, [(i, i ^ distance) for i in range(size)])  18.5 us
    pallas_call x2, Pallas kernels, attend(): pl.pallas_call(functools.partial(attend_body, kv, parts, [len(choice) for...  16.4 us
    pallas_call x15, Pallas kernels, step(): pl.pallas_call(functools.partial(step_body, plan), out_shape=[jax.ShapeDt...  15.3 us
    ppermute x1, waiting for transfers between devices, spread(): across_out = lax.ppermute(across, 'node', OUTWARD)  9.22 us
    ppermute x1, waiting for transfers between devices, spread(): far = lax.ppermute(exported, 'node', ENDS)  5.52 us
    ppermute x1, starting transfers between devices, spread(): near = lax.ppermute(exported, 'node', PAIRS)  4.36 us
  transfers between devices with their start and end apart: 30, of which 16 were waited for; matrix products, arithmetic and copies ran while one was open for 0% of the time, Pallas kernels for 22%

profile of v4, /device:TPU:0, one launch (start us, length us, event | category | flops | bytes accessed | tf_op | source)
XLA Modules:
  0.0 158.1 jit_solution(14238709105975227298)
XLA Ops:
  1.5 3.1 %collective-permute-start.5 = (bf16[640,1280]{1,0:T(8,128)(2,1)S(1)}, bf16[640,1280]{1,0:T(8,128)(2,1)S(1)}, u32[]{:S(2)}, u32[]{:S(2)}) collective-permute-start(bf16[640,1280]{1,0:T(8,128)(2,1)S(1)} %cut.1), channel_id=1, source_target_pairs={{0,4},{4,0},{8,12},{12,8},{1,5},{5,1},{9,13},{13,9},{2,6},{6,2},{1... | collective-permute-start | bytes 4915208 | tf_op jit(solution)/shard_map/ppermute | solution.py:422
  5.4 1.8 %prepare.1 = (bf16[4,128,256]{2,1,0:T(8,128)(2,1)S(1)}, s32[8]{0:T(128)S(1)}) custom-call(s32[24]{0:T(128)S(1)} %copy-done.4, s32[7,24]{1,0:T(8,128)S(1)} %bitcast.13, s32[24]{0:T(128)S(1)} %copy-done.5, bf16[768,256]{1,0:T(8,128)(2,1)S(1)} %copy-done.1, bf16[768,256]{1,0:T(8,128)(2,1)S(1)} %copy-done.2), custom_call_target="tpu_custom_call" | custom-call | tf_op jit(solution)/shard_map/prepare/pallas_call | solution.py:93
  7.3 4.4 %collective-permute-start = (bf16[4,128,256]{2,1,0:T(8,128)(2,1)S(1)}, bf16[4,128,256]{2,1,0:T(8,128)(2,1)S(1)}, u32[]{:S(2)}, u32[]{:S(2)}) collective-permute-start(bf16[4,128,256]{2,1,0:T(8,128)(2,1)S(1)} %get-tuple-element.36), channel_id=1, source_target_pairs={{0,4},{4,0},{8,12},{12,8},{1,5},{5,1},{9,13},{13,9},{2,6},{6,2},{1... | collective-permute-start | bytes 786440 | tf_op jit(solution)/shard_map/ppermute | solution.py:583
  12.3 2.8 %collective-permute-start.4 = (bf16[4,128,256]{2,1,0:T(8,128)(2,1)S(1)}, bf16[4,128,256]{2,1,0:T(8,128)(2,1)S(1)}, u32[]{:S(2)}, u32[]{:S(2)}) collective-permute-start(bf16[4,128,256]{2,1,0:T(8,128)(2,1)S(1)} %get-tuple-element.36), channel_id=1, source_target_pairs={{0,12},{12,0},{1,13},{13,1},{2,14},{14,2},{3,15},{15,3},{16,28},{2... | collective-permute-start | bytes 786440 | tf_op jit(solution)/shard_map/ppermute | solution.py:587
  15.1 31.3 %collective-permute-done.refs_0_ = bf16[4,128,256]{2,1,0:T(8,128)(2,1)S(1)} collective-permute-done((bf16[4,128,256]{2,1,0:T(8,128)(2,1)S(1)}, bf16[4,128,256]{2,1,0:T(8,128)(2,1)S(1)}, u32[]{:S(2)}, u32[]{:S(2)}) %collective-permute-start) | collective-permute-done | bytes 262176 | tf_op jit(solution)/shard_map/ppermute | solution.py:583
  48.4 5.5 %collective-permute-done.4.refs_4_ = bf16[4,128,256]{2,1,0:T(8,128)(2,1)S(1)} collective-permute-done((bf16[4,128,256]{2,1,0:T(8,128)(2,1)S(1)}, bf16[4,128,256]{2,1,0:T(8,128)(2,1)S(1)}, u32[]{:S(2)}, u32[]{:S(2)}) %collective-permute-start.4) | collective-permute-done | bytes 262176 | tf_op jit(solution)/shard_map/ppermute | solution.py:587
  54.0 9.2 %collective-permute-done.3.refs_2_ = bf16[4,128,256]{2,1,0:T(8,128)(2,1)S(1)} collective-permute-done((bf16[4,128,256]{2,1,0:T(8,128)(2,1)S(1)}, bf16[4,128,256]{2,1,0:T(8,128)(2,1)S(1)}, u32[]{:S(2)}, u32[]{:S(2)}) %collective-permute-start.3) | collective-permute-done | bytes 262176 | tf_op jit(solution)/shard_map/ppermute | solution.py:586
  65.3 8.2 %attend.2.refs_5_ = bf16[4,192,640]{2,1,0:T(8,128)(2,1)S(1)} custom-call(s32[8]{0:T(128)S(1)} %get-tuple-element.35.table, bf16[768,1280]{1,0:T(8,128)(2,1)} %query_hbm.3, bf16[768,256]{1,0:T(8,128)(2,1)} %keys_hbm.3, bf16[768,256]{1,0:T(8,128)(2,1)} %values_hbm.3, bf16[4,128,256]{2,1,0:T(8,128)(2,1)S(1)} %collective-permute-done.refs_0_, ...), custom_call_target="tpu_custom_call" | custom-call | flops 1 | bytes 1 | tf_op jit(solution)/shard_map/attend/pallas_call | solution.py:244
  73.5 1.6 %collective-permute-start.7 = (bf16[768,640]{1,0:T(8,128)(2,1)S(1)}, bf16[768,640]{1,0:T(8,128)(2,1)S(1)}, u32[]{:S(2)}, u32[]{:S(2)}) collective-permute-start(bf16[768,640]{1,0:T(8,128)(2,1)S(1)} %bitcast.3), channel_id=1, source_target_pairs={{0,16},{16,0},{1,17},{17,1},{2,18},{18,2},{3,19},{19,3},{4,20},{20... | collective-permute-start | bytes 2949128 | tf_op jit(solution)/shard_map/ppermute | solution.py:268
  75.1 8.2 %attend.3 = bf16[4,192,640]{2,1,0:T(8,128)(2,1)S(1)} custom-call(s32[8]{0:T(128)S(1)} %get-tuple-element.35.table, bf16[768,1280]{1,0:T(8,128)(2,1)} %query_hbm.3, bf16[768,256]{1,0:T(8,128)(2,1)} %keys_hbm.3, bf16[768,256]{1,0:T(8,128)(2,1)} %values_hbm.3, bf16[4,128,256]{2,1,0:T(8,128)(2,1)S(1)} %collective-permute-done.refs_0_, ...), custom_call_target="tpu_custom_call" | custom-call | flops 1 | bytes 1 | tf_op jit(solution)/shard_map/attend/pallas_call | solution.py:244
  83.3 3.2 %step.15 = (bf16[384,640]{1,0:T(8,128)(2,1)S(1)}, bf16[384,640]{1,0:T(8,128)(2,1)S(1)}, bf16[384,512]{1,0:T(8,128)(2,1)S(1)}, bf16[384,512]{1,0:T(8,128)(2,1)S(1...) custom-call(bf16[768,640]{1,0:T(8,128)(2,1)S(1)} %bitcast.4, bf16[768,640]{1,0:T(8,128)(2,1)S(1)} %bitcast.8, ...), custom_call_target="tpu_custom_call" | custom-call | flops 1 | bytes 1 | tf_op jit(solution)/shard_map/step/pallas_call | solution.py:404
  87.1 1.9 %collective-permute-done.14.refs_3_.refs_7_ = bf16[384,512]{1,0:T(8,128)(2,1)S(1)} collective-permute-done((bf16[384,512]{1,0:T(8,128)(2,1)S(1)}, bf16[384,512]{1,0:T(8,128)(2,1)S(1)}, u32[]{:S(2)}, u32[]{:S(2)}) %collective-permute-start.14) | collective-permute-done | bytes 393248 | tf_op jit(solution)/shard_map/ppermute | solution.py:268
  89.2 1.6 collective-permute-start.16
  92.5 2.7 %collective-permute-done.7.refs_4_.refs_0_ = bf16[768,640]{1,0:T(8,128)(2,1)S(1)} collective-permute-done((bf16[768,640]{1,0:T(8,128)(2,1)S(1)}, bf16[768,640]{1,0:T(8,128)(2,1)S(1)}, u32[]{:S(2)}, u32[]{:S(2)}) %collective-permute-start.7) | collective-permute-done | bytes 983072 | tf_op jit(solution)/shard_map/ppermute | solution.py:268
  95.2 1.7 %step.17 = (bf16[384,640]{1,0:T(8,128)(2,1)S(1)}, bf16[384,640]{1,0:T(8,128)(2,1)S(1)}) custom-call(bf16[768,640]{1,0:T(8,128)(2,1)S(1)} %bitcast.5, bf16[768,640]{1,0:T(8,128)(2,1)S(1)} %bitcast.10, bf16[640,1280]{1,0:T(8,128)(2,1)S(1)} %collective-permute-done.5.refs_5_.refs_2_, bf16[192,1152]{1,0:T(8,128)(2,1)S(1)} %step.16.refs_3_, ...), custom_call_target="tpu_custom_call" | custom-call | flops 1 | bytes 1 | tf_op jit(solution)/shard_map/step/pallas_call | solution.py:404
  97.0 4.4 %collective-permute-done.16.refs_8_ = bf16[192,1152]{1,0:T(8,128)(2,1)S(1)} collective-permute-done((bf16[192,1152]{1,0:T(8,128)(2,1)S(1)}, bf16[192,1152]{1,0:T(8,128)(2,1)S(1)}, u32[]{:S(2)}, u32[]{:S(2)}) %collective-permute-start.16) | collective-permute-done | bytes 442400 | tf_op jit(solution)/shard_map/ppermute | solution.py:268
  102.5 2.3 %step.18 = (bf16[384,640]{1,0:T(8,128)(2,1)S(1)}, bf16[384,640]{1,0:T(8,128)(2,1)S(1)}, bf16[192,640]{1,0:T(8,128)(2,1)S(1)}, bf16[192,512]{1,0:T(8,128)(2,1)S(1)}) custom-call(bf16[768,640]{1,0:T(8,128)(2,1)S(1)} %bitcast.6, bf16[768,640]{1,0:T(8,128)(2,1)S(1)} %bitcast.11, bf16[640,1280]{1,0:T(8,128)(2,1)S(1)} %collective-permute-done.9.refs_2_.refs_3_, ...), custom_call_target="tpu_custom_call" | custom-call | flops 1 | bytes 1 | tf_op jit(solution)/shard_map/step/pallas_call | solution.py:404
  107.0 1.6 collective-permute-start.20
  108.5 6.7 %collective-permute-done.8.refs_1_ = bf16[768,640]{1,0:T(8,128)(2,1)S(1)} collective-permute-done((bf16[768,640]{1,0:T(8,128)(2,1)S(1)}, bf16[768,640]{1,0:T(8,128)(2,1)S(1)}, u32[]{:S(2)}, u32[]{:S(2)}) %collective-permute-start.8) | collective-permute-done | bytes 983072 | tf_op jit(solution)/shard_map/ppermute | solution.py:268
  115.2 3.6 %step.20 = (bf16[384,640]{1,0:T(8,128)(2,1)S(1)}, bf16[384,640]{1,0:T(8,128)(2,1)S(1)}, bf16[384,640]{1,0:T(8,128)(2,1)S(1)}, bf16[384,640]{1,0:T(8,128)(2,1)S(1)}) custom-call(bf16[768,640]{1,0:T(8,128)(2,1)S(1)} %collective-permute-done.7.refs_4_.refs_0_, bf16[768,640]{1,0:T(8,128)(2,1)S(1)} %collective-permute-done.8.refs_1_, ...), custom_call_target="tpu_custom_call" | custom-call | flops 1 | bytes 1 | tf_op jit(solution)/shard_map/step/pallas_call | solution.py:404
  121.6 1.6 collective-permute-start.21
  123.2 5.9 %collective-permute-done.21.refs_4_ = bf16[192,640]{1,0:T(8,128)(2,1)S(1)} collective-permute-done((bf16[192,640]{1,0:T(8,128)(2,1)S(1)}, bf16[192,640]{1,0:T(8,128)(2,1)S(1)}, u32[]{:S(2)}, u32[]{:S(2)}) %collective-permute-start.21) | collective-permute-done | bytes 245792 | tf_op jit(solution)/shard_map/ppermute | solution.py:268
  129.3 1.6 collective-permute-start.23
  130.8 1.6 collective-permute-start.24
  132.4 4.0 %collective-permute-done.10.refs_3_ = bf16[640,1280]{1,0:T(8,128)(2,1)S(1)} collective-permute-done((bf16[640,1280]{1,0:T(8,128)(2,1)S(1)}, bf16[640,1280]{1,0:T(8,128)(2,1)S(1)}, u32[]{:S(2)}, u32[]{:S(2)}) %collective-permute-start.10) | collective-permute-done | bytes 1638432 | tf_op jit(solution)/shard_map/ppermute | solution.py:500
  136.4 1.7 %step.23 = (bf16[384,640]{1,0:T(8,128)(2,1)S(1)}, bf16[384,640]{1,0:T(8,128)(2,1)S(1)}) custom-call(bf16[768,640]{1,0:T(8,128)(2,1)S(1)} %collective-permute-done.7.refs_4_.refs_0_, bf16[768,640]{1,0:T(8,128)(2,1)S(1)} %collective-permute-done.8.refs_1_, bf16[640,1280]{1,0:T(8,128)(2,1)S(1)} %collective-permute-done.6.refs_6_.refs_2_, ...), custom_call_target="tpu_custom_call" | custom-call | flops 1 | bytes 1 | tf_op jit(solution)/shard_map/step/pallas_call | solution.py:404
  138.3 1.7 %step.25 = (bf16[384,640]{1,0:T(8,128)(2,1)S(1)}, bf16[384,640]{1,0:T(8,128)(2,1)S(1)}) custom-call(bf16[768,640]{1,0:T(8,128)(2,1)S(1)} %bitcast.7, bf16[768,640]{1,0:T(8,128)(2,1)S(1)} %bitcast.12, bf16[640,1280]{1,0:T(8,128)(2,1)S(1)} %collective-permute-done.6.refs_6_.refs_2_, bf16[640,1280]{1,0:T(8,128)(2,1)S(1)} %collective-permute-done.10.refs_3_, ...), custom_call_target="tpu_custom_call" | custom-call | flops 1 | bytes 1 | tf_op jit(solution)/shard_map/step/pallas_call | solution.py:404
  142.2 1.5 collective-permute-start.25
  143.7 4.8 %collective-permute-done.27.refs_3_.refs_4_.refs_6_ = bf16[192,640]{1,0:T(8,128)(2,1)S(1)} collective-permute-done((bf16[192,640]{1,0:T(8,128)(2,1)S(1)}, bf16[192,640]{1,0:T(8,128)(2,1)S(1)}, u32[]{:S(2)}, u32[]{:S(2)}) %collective-permute-start.27) | collective-permute-done | bytes 245792 | tf_op jit(solution)/shard_map/ppermute | solution.py:268
  148.6 1.6 collective-permute-start.29
  150.3 1.6 %collective-permute-start.28 = (bf16[192,640]{1,0:T(8,128)(2,1)S(1)}, bf16[192,640]{1,0:T(8,128)(2,1)S(1)}, u32[]{:S(2)}, u32[]{:S(2)}) collective-permute-start(bf16[192,640]{1,0:T(8,128)(2,1)S(1)} %step.28.refs_3_), channel_id=1, source_target_pairs={{0,16},{16,0},{1,17},{17,1},{2,18},{18,2},{3,19},{19,3},{4,20},{20... | collective-permute-start | bytes 737288 | tf_op jit(solution)/shard_map/ppermute | solution.py:268
  153.0 2.8 %collective-permute-done.29.refs_2_ = bf16[192,640]{1,0:T(8,128)(2,1)S(1)} collective-permute-done((bf16[192,640]{1,0:T(8,128)(2,1)S(1)}, bf16[192,640]{1,0:T(8,128)(2,1)S(1)}, u32[]{:S(2)}, u32[]{:S(2)}) %collective-permute-start.29) | collective-permute-done | bytes 245792 | tf_op jit(solution)/shard_map/ppermute | solution.py:268
  (61 shorter events, 21.4 us)
Async XLA Ops:
  0.0 5.4 %copy-start.2 = (bf16[768,256]{1,0:T(8,128)(2,1)S(1)}, bf16[768,256]{1,0:T(8,128)(2,1)}, u32[]{:S(2)}) copy-start(bf16[768,256]{1,0:T(8,128)(2,1)} %values_hbm.3) | copy-start | bytes 1179652
  1.5 61.7 %collective-permute-start.5 = (bf16[640,1280]{1,0:T(8,128)(2,1)S(1)}, bf16[640,1280]{1,0:T(8,128)(2,1)S(1)}, u32[]{:S(2)}, u32[]{:S(2)}) collective-permute-start(bf16[640,1280]{1,0:T(8,128)(2,1)S(1)} %cut.1), channel_id=1, source_target_pairs={{0,4},{4,0},{8,12},{12,8},{1,5},{5,1},{9,13},{13,9},{2,6},{6,2},{1... | collective-permute-start | bytes 4915208 | tf_op jit(solution)/shard_map/ppermute | solution.py:422
  4.6 59.3 %collective-permute-start.6 = (bf16[640,1280]{1,0:T(8,128)(2,1)S(1)}, bf16[640,1280]{1,0:T(8,128)(2,1)S(1)}, u32[]{:S(2)}, u32[]{:S(2)}) collective-permute-start(bf16[640,1280]{1,0:T(8,128)(2,1)S(1)} %cut.1), channel_id=1, source_target_pairs={{4,8},{8,4},{5,9},{9,5},{6,10},{10,6},{7,11},{11,7},{20,24},{24,20... | collective-permute-start | bytes 4915208 | tf_op jit(solution)/shard_map/ppermute | solution.py:423
  7.3 39.2 %collective-permute-start = (bf16[4,128,256]{2,1,0:T(8,128)(2,1)S(1)}, bf16[4,128,256]{2,1,0:T(8,128)(2,1)S(1)}, u32[]{:S(2)}, u32[]{:S(2)}) collective-permute-start(bf16[4,128,256]{2,1,0:T(8,128)(2,1)S(1)} %get-tuple-element.36), channel_id=1, source_target_pairs={{0,4},{4,0},{8,12},{12,8},{1,5},{5,1},{9,13},{13,9},{2,6},{6,2},{1... | collective-permute-start | bytes 786440 | tf_op jit(solution)/shard_map/ppermute | solution.py:583
  11.6 35.5 %collective-permute-start.2 = (bf16[4,128,256]{2,1,0:T(8,128)(2,1)S(1)}, bf16[4,128,256]{2,1,0:T(8,128)(2,1)S(1)}, u32[]{:S(2)}, u32[]{:S(2)}) collective-permute-start(bf16[4,128,256]{2,1,0:T(8,128)(2,1)S(1)} %get-tuple-element.36), channel_id=1, source_target_pairs={{4,8},{8,4},{5,9},{9,5},{6,10},{10,6},{7,11},{11,7},{20,24},{24,20... | collective-permute-start | bytes 786440 | tf_op jit(solution)/shard_map/ppermute | solution.py:584
  12.3 41.7 %collective-permute-start.4 = (bf16[4,128,256]{2,1,0:T(8,128)(2,1)S(1)}, bf16[4,128,256]{2,1,0:T(8,128)(2,1)S(1)}, u32[]{:S(2)}, u32[]{:S(2)}) collective-permute-start(bf16[4,128,256]{2,1,0:T(8,128)(2,1)S(1)} %get-tuple-element.36), channel_id=1, source_target_pairs={{0,12},{12,0},{1,13},{13,1},{2,14},{14,2},{3,15},{15,3},{16,28},{2... | collective-permute-start | bytes 786440 | tf_op jit(solution)/shard_map/ppermute | solution.py:587
  46.4 7.5 %collective-permute-start.1 = (bf16[4,128,256]{2,1,0:T(8,128)(2,1)S(1)}, bf16[4,128,256]{2,1,0:T(8,128)(2,1)S(1)}, u32[]{:S(2)}, u32[]{:S(2)}) collective-permute-start(bf16[4,128,256]{2,1,0:T(8,128)(2,1)S(1)} %collective-permute-done.refs_0_), channel_id=1, source_target_pairs={{4,8},{8,4},{5,9},{9,5},{6,10},{10,6},{7,11},{11,7},{20,24},{24,20... | collective-permute-start | bytes 786440 | tf_op jit(solution)/shard_map/ppermute | solution.py:585
  47.1 16.1 %collective-permute-start.3 = (bf16[4,128,256]{2,1,0:T(8,128)(2,1)S(1)}, bf16[4,128,256]{2,1,0:T(8,128)(2,1)S(1)}, u32[]{:S(2)}, u32[]{:S(2)}) collective-permute-start(bf16[4,128,256]{2,1,0:T(8,128)(2,1)S(1)} %collective-permute-done.2.refs_3_), channel_id=1, source_target_pairs={{4,0},{8,12},{5,1},{9,13},{6,2},{10,14},{7,3},{11,15},{20,16},{24,... | collective-permute-start | bytes 786440 | tf_op jit(solution)/shard_map/ppermute | solution.py:586
  63.2 28.1 %collective-permute-start.9 = (bf16[640,1280]{1,0:T(8,128)(2,1)S(1)}, bf16[640,1280]{1,0:T(8,128)(2,1)S(1)}, u32[]{:S(2)}, u32[]{:S(2)}) collective-permute-start(bf16[640,1280]{1,0:T(8,128)(2,1)S(1)} %collective-permute-done.5.refs_5_.refs_2_), channel_id=1, source_target_pairs={{4,8},{8,4},{5,9},{9,5},{6,10},{10,6},{7,11},{11,7},{20,24},{24,20... | collective-permute-start | bytes 4915208 | tf_op jit(solution)/shard_map/ppermute | solution.py:427
  64.0 38.5 %collective-permute-start.11 = (bf16[640,1280]{1,0:T(8,128)(2,1)S(1)}, bf16[640,1280]{1,0:T(8,128)(2,1)S(1)}, u32[]{:S(2)}, u32[]{:S(2)}) collective-permute-start(bf16[640,1280]{1,0:T(8,128)(2,1)S(1)} %collective-permute-done.6.refs_6_.refs_2_), channel_id=1, source_target_pairs={{4,0},{8,12},{5,1},{9,13},{6,2},{10,14},{7,3},{11,15},{20,16},{24,... | collective-permute-start | bytes 4915208 | tf_op jit(solution)/shard_map/ppermute | solution.py:426
  73.5 9.9 %copy-start = (bf16[1280,1280]{1,0:T(8,128)(2,1)S(1)}, bf16[1280,1280]{1,0:T(8,128)(2,1)}, u32[]{:S(2)}) copy-start(bf16[1280,1280]{1,0:T(8,128)(2,1)} %refs_2_.3) | copy-start | bytes 9830404
  73.5 21.7 %collective-permute-start.7 = (bf16[768,640]{1,0:T(8,128)(2,1)S(1)}, bf16[768,640]{1,0:T(8,128)(2,1)S(1)}, u32[]{:S(2)}, u32[]{:S(2)}) collective-permute-start(bf16[768,640]{1,0:T(8,128)(2,1)S(1)} %bitcast.3), channel_id=1, source_target_pairs={{0,16},{16,0},{1,17},{17,1},{2,18},{18,2},{3,19},{19,3},{4,20},{20... | collective-permute-start | bytes 2949128 | tf_op jit(solution)/shard_map/ppermute | solution.py:268
  86.6 2.5 %collective-permute-start.13 = (bf16[384,640]{1,0:T(8,128)(2,1)S(1)}, bf16[384,640]{1,0:T(8,128)(2,1)S(1)}, u32[]{:S(2)}, u32[]{:S(2)}) collective-permute-start(bf16[384,640]{1,0:T(8,128)(2,1)S(1)} %get-tuple-element.42), channel_id=1, source_target_pairs={{0,1},{1,0},{2,3},{3,2},{4,5},{5,4},{6,7},{7,6},{8,9},{9,8},{10,11... | collective-permute-start | bytes 1474568 | tf_op jit(solution)/shard_map/ppermute | solution.py:268
  86.7 2.4 %collective-permute-start.14 = (bf16[384,512]{1,0:T(8,128)(2,1)S(1)}, bf16[384,512]{1,0:T(8,128)(2,1)S(1)}, u32[]{:S(2)}, u32[]{:S(2)}) collective-permute-start(bf16[384,512]{1,0:T(8,128)(2,1)S(1)} %get-tuple-element.44), channel_id=1, source_target_pairs={{0,1},{1,0},{2,3},{3,2},{4,5},{5,4},{6,7},{7,6},{8,9},{9,8},{10,11... | collective-permute-start | bytes 1179656 | tf_op jit(solution)/shard_map/ppermute | solution.py:268
  89.2 12.3 %collective-permute-start.16 = (bf16[192,1152]{1,0:T(8,128)(2,1)S(1)}, bf16[192,1152]{1,0:T(8,128)(2,1)S(1)}, u32[]{:S(2)}, u32[]{:S(2)}) collective-permute-start(bf16[192,1152]{1,0:T(8,128)(2,1)S(1)} %step.16.refs_3_), channel_id=1, source_target_pairs={{0,2},{1,3},{2,0},{3,1},{4,6},{5,7},{6,4},{7,5},{8,10},{9,11},{10,... | collective-permute-start | bytes 1327112 | tf_op jit(solution)/shard_map/ppermute | solution.py:268
  90.7 24.5 %collective-permute-start.8 = (bf16[768,640]{1,0:T(8,128)(2,1)S(1)}, bf16[768,640]{1,0:T(8,128)(2,1)S(1)}, u32[]{:S(2)}, u32[]{:S(2)}) collective-permute-start(bf16[768,640]{1,0:T(8,128)(2,1)S(1)} %bitcast.9), channel_id=1, source_target_pairs={{0,16},{16,0},{1,17},{17,1},{2,18},{18,2},{3,19},{19,3},{4,20},{20... | collective-permute-start | bytes 2949128 | tf_op jit(solution)/shard_map/ppermute | solution.py:268
  91.2 45.2 %collective-permute-start.10 = (bf16[640,1280]{1,0:T(8,128)(2,1)S(1)}, bf16[640,1280]{1,0:T(8,128)(2,1)S(1)}, u32[]{:S(2)}, u32[]{:S(2)}) collective-permute-start(bf16[640,1280]{1,0:T(8,128)(2,1)S(1)} %collective-permute-done.9.refs_2_.refs_3_), channel_id=1, source_target_pairs={{4,0},{8,12},{5,1},{9,13},{6,2},{10,14},{7,3},{11,15},{20,16},{24,... | collective-permute-start | bytes 4915208 | tf_op jit(solution)/shard_map/ppermute | solution.py:500
  96.9 9.9 %collective-permute-start.15 = (bf16[384,640]{1,0:T(8,128)(2,1)S(1)}, bf16[384,640]{1,0:T(8,128)(2,1)S(1)}, u32[]{:S(2)}, u32[]{:S(2)}) collective-permute-start(bf16[384,640]{1,0:T(8,128)(2,1)S(1)} %get-tuple-element.46.refs_9_), channel_id=1, source_target_pairs={{0,1},{1,0},{2,3},{3,2},{4,5},{5,4},{6,7},{7,6},{8,9},{9,8},{10,11... | collective-permute-start | bytes 1474568 | tf_op jit(solution)/shard_map/ppermute | solution.py:268
  104.8 2.1 %collective-permute-start.17 = (bf16[384,640]{1,0:T(8,128)(2,1)S(1)}, bf16[384,640]{1,0:T(8,128)(2,1)S(1)}, u32[]{:S(2)}, u32[]{:S(2)}) collective-permute-start(bf16[384,640]{1,0:T(8,128)(2,1)S(1)} %get-tuple-element.48), channel_id=1, source_target_pairs={{0,1},{1,0},{2,3},{3,2},{4,5},{5,4},{6,7},{7,6},{8,9},{9,8},{10,11... | collective-permute-start | bytes 1474568 | tf_op jit(solution)/shard_map/ppermute | solution.py:268
  104.8 2.0 %collective-permute-start.12 = (bf16[384,128]{1,0:T(8,128)(2,1)S(1)}, bf16[384,128]{1,0:T(8,128)(2,1)S(1)}, u32[]{:S(2)}, u32[]{:S(2)}) collective-permute-start(bf16[384,128]{1,0:T(8,128)(2,1)S(1)} %get-tuple-element.40), channel_id=1, source_target_pairs={{0,1},{1,0},{2,3},{3,2},{4,5},{5,4},{6,7},{7,6},{8,9},{9,8},{10,11... | collective-permute-start | bytes 294920 | tf_op jit(solution)/shard_map/ppermute | solution.py:268
  107.0 14.4 %collective-permute-start.20 = (bf16[192,1408]{1,0:T(8,128)(2,1)S(1)}, bf16[192,1408]{1,0:T(8,128)(2,1)S(1)}, u32[]{:S(2)}, u32[]{:S(2)}) collective-permute-start(bf16[192,1408]{1,0:T(8,128)(2,1)S(1)} %step.19.refs_5_), channel_id=1, source_target_pairs={{0,2},{1,3},{2,0},{3,1},{4,6},{5,7},{6,4},{7,5},{8,10},{9,11},{10,... | collective-permute-start | bytes 1622024 | tf_op jit(solution)/shard_map/ppermute | solution.py:268
  118.9 1.9 %collective-permute-start.19 = (bf16[384,640]{1,0:T(8,128)(2,1)S(1)}, bf16[384,640]{1,0:T(8,128)(2,1)S(1)}, u32[]{:S(2)}, u32[]{:S(2)}) collective-permute-start(bf16[384,640]{1,0:T(8,128)(2,1)S(1)} %get-tuple-element.52), channel_id=1, source_target_pairs={{0,1},{1,0},{2,3},{3,2},{4,5},{5,4},{6,7},{7,6},{8,9},{9,8},{10,11... | collective-permute-start | bytes 1474568 | tf_op jit(solution)/shard_map/ppermute | solution.py:268
  118.9 4.2 %collective-permute-start.18 = (bf16[384,640]{1,0:T(8,128)(2,1)S(1)}, bf16[384,640]{1,0:T(8,128)(2,1)S(1)}, u32[]{:S(2)}, u32[]{:S(2)}) collective-permute-start(bf16[384,640]{1,0:T(8,128)(2,1)S(1)} %get-tuple-element.50), channel_id=1, source_target_pairs={{0,1},{1,0},{2,3},{3,2},{4,5},{5,4},{6,7},{7,6},{8,9},{9,8},{10,11... | collective-permute-start | bytes 1474568 | tf_op jit(solution)/shard_map/ppermute | solution.py:268
  121.6 7.5 %collective-permute-start.21 = (bf16[192,640]{1,0:T(8,128)(2,1)S(1)}, bf16[192,640]{1,0:T(8,128)(2,1)S(1)}, u32[]{:S(2)}, u32[]{:S(2)}) collective-permute-start(bf16[192,640]{1,0:T(8,128)(2,1)S(1)} %get-tuple-element.53), channel_id=1, source_target_pairs={{0,2},{1,3},{2,0},{3,1},{4,6},{5,7},{6,4},{7,5},{8,10},{9,11},{10,... | collective-permute-start | bytes 737288 | tf_op jit(solution)/shard_map/ppermute | solution.py:268
  129.3 8.9 %collective-permute-start.23 = (bf16[192,640]{1,0:T(8,128)(2,1)S(1)}, bf16[192,640]{1,0:T(8,128)(2,1)S(1)}, u32[]{:S(2)}, u32[]{:S(2)}) collective-permute-start(bf16[192,640]{1,0:T(8,128)(2,1)S(1)} %get-tuple-element.54.refs_4_), channel_id=1, source_target_pairs={{0,2},{1,3},{2,0},{3,1},{4,6},{5,7},{6,4},{7,5},{8,10},{9,11},{10,... | collective-permute-start | bytes 737288 | tf_op jit(solution)/shard_map/ppermute | solution.py:268
  130.8 7.4 %collective-permute-start.24 = (bf16[192,640]{1,0:T(8,128)(2,1)S(1)}, bf16[192,640]{1,0:T(8,128)(2,1)S(1)}, u32[]{:S(2)}, u32[]{:S(2)}) collective-permute-start(bf16[192,640]{1,0:T(8,128)(2,1)S(1)} %get-tuple-element.57), channel_id=1, source_target_pairs={{0,16},{16,0},{1,17},{17,1},{2,18},{18,2},{3,19},{19,3},{4,20},{20... | collective-permute-start | bytes 737288 | tf_op jit(solution)/shard_map/ppermute | solution.py:268
  138.1 4.0 %collective-permute-start.22 = (bf16[384,640]{1,0:T(8,128)(2,1)S(1)}, bf16[384,640]{1,0:T(8,128)(2,1)S(1)}, u32[]{:S(2)}, u32[]{:S(2)}) collective-permute-start(bf16[384,640]{1,0:T(8,128)(2,1)S(1)} %get-tuple-element.56.refs_3_), channel_id=1, source_target_pairs={{0,1},{1,0},{2,3},{3,2},{4,5},{5,4},{6,7},{7,6},{8,9},{9,8},{10,11... | collective-permute-start | bytes 1474568 | tf_op jit(solution)/shard_map/ppermute | solution.py:268
  140.1 8.5 %collective-permute-start.26 = (bf16[384,640]{1,0:T(8,128)(2,1)S(1)}, bf16[384,640]{1,0:T(8,128)(2,1)S(1)}, u32[]{:S(2)}, u32[]{:S(2)}) collective-permute-start(bf16[384,640]{1,0:T(8,128)(2,1)S(1)} %get-tuple-element.58.refs_2_), channel_id=1, source_target_pairs={{0,1},{1,0},{2,3},{3,2},{4,5},{5,4},{6,7},{7,6},{8,9},{9,8},{10,11... | collective-permute-start | bytes 1474568 | tf_op jit(solution)/shard_map/ppermute | solution.py:268
  140.6 7.9 %collective-permute-start.27 = (bf16[192,640]{1,0:T(8,128)(2,1)S(1)}, bf16[192,640]{1,0:T(8,128)(2,1)S(1)}, u32[]{:S(2)}, u32[]{:S(2)}) collective-permute-start(bf16[192,640]{1,0:T(8,128)(2,1)S(1)} %step.24.refs_4_), channel_id=1, source_target_pairs={{0,16},{16,0},{1,17},{17,1},{2,18},{18,2},{3,19},{19,3},{4,20},{20... | collective-permute-start | bytes 737288 | tf_op jit(solution)/shard_map/ppermute | solution.py:268
  142.2 8.0 %collective-permute-start.25 = (bf16[192,640]{1,0:T(8,128)(2,1)S(1)}, bf16[192,640]{1,0:T(8,128)(2,1)S(1)}, u32[]{:S(2)}, u32[]{:S(2)}) collective-permute-start(bf16[192,640]{1,0:T(8,128)(2,1)S(1)} %step.26.refs_2_), channel_id=1, source_target_pairs={{0,2},{1,3},{2,0},{3,1},{4,6},{5,7},{6,4},{7,5},{8,10},{9,11},{10,... | collective-permute-start | bytes 737288 | tf_op jit(solution)/shard_map/ppermute | solution.py:268
  148.6 7.2 %collective-permute-start.29 = (bf16[192,640]{1,0:T(8,128)(2,1)S(1)}, bf16[192,640]{1,0:T(8,128)(2,1)S(1)}, u32[]{:S(2)}, u32[]{:S(2)}) collective-permute-start(bf16[192,640]{1,0:T(8,128)(2,1)S(1)} %step.27.refs_3_), channel_id=1, source_target_pairs={{0,2},{1,3},{2,0},{3,1},{4,6},{5,7},{6,4},{7,5},{8,10},{9,11},{10,... | collective-permute-start | bytes 737288 | tf_op jit(solution)/shard_map/ppermute | solution.py:268
  150.3 6.9 %collective-permute-start.28 = (bf16[192,640]{1,0:T(8,128)(2,1)S(1)}, bf16[192,640]{1,0:T(8,128)(2,1)S(1)}, u32[]{:S(2)}, u32[]{:S(2)}) collective-permute-start(bf16[192,640]{1,0:T(8,128)(2,1)S(1)} %step.28.refs_3_), channel_id=1, source_target_pairs={{0,16},{16,0},{1,17},{17,1},{2,18},{18,2},{3,19},{19,3},{4,20},{20... | collective-permute-start | bytes 737288 | tf_op jit(solution)/shard_map/ppermute | solution.py:268
  (4 other events, 21.6 us)
